TPU v7x, 256 devices: a whole 4x4x8 slice. The times are simulated.
256 devices in a mesh: sx: 16 (over y, x), sy: 16 (over z, core).
Axes of the slice: x: 4, y: 4, z: 8, core: 2. Of those that a mesh axis runs over, the one named last changes fastest.
Arguments:
- points: bfloat16 [16, 16, 96, 1024], P('sx', 'sy'), may hold values from -6 to 6
- owners: int32 [16, 16, 1024, 1], P('sx', 'sy'), may hold values from 0 to 15; in each aligned block of 1024 rows (0 to 1023, 1024 to 2047, ..., all dimensions but the last counted through in order) at most 128 rows name the same one
- kernel_maps: int32 [16, 16, 27, 2048], P('sx', 'sy'), may hold values from 0 to 2560
- face_rows: int32 [16, 16, 2, 256], P('sx', 'sy'), may hold values from 0 to 2047
- weight: bfloat16 [27, 96, 96], replicated, may hold values from -0.15625 to 0.15625
- cotangent: bfloat16 [16, 16, 96, 2048], P('sx', 'sy'), may hold values from -6 to 6
Outputs:
- output: bfloat16 [16, 16, 96, 2048], P('sx', 'sy')
- point_grad: bfloat16 [16, 16, 96, 1024], P('sx', 'sy')
- weight_grad: float32 [27, 96, 96], replicated
Inputs may be any that keep to these rules, and one draw needn't show every extreme that they name: `owners`: among the voxels of one device no owner is named more than 128 times, a bound that some block reaches.
All inputs are finite; a program needn't handle non-finite values.
Results may differ from a plain program's by a relative error of at most 0.005.
Values may be sent and summed in bfloat16 or wider, within the bound.
No kernel may reach another device: no remote copies, remote signals or barrier semaphores. Data moves between devices by JAX's collectives and lax.ppermute only.
A program may use at most 64 MiB of HBM per device.

v0:
```python
import math

import jax
import jax.numpy as jnp
from jax import lax
from jax.sharding import PartitionSpec as P


def with_halo(block, sides, width):
    for axis, dim in sides:
        count = lax.axis_size(axis)
        forward = [(i, i + 1) for i in range(count - 1)]
        backward = [(target, source) for source, target in forward]
        low = lax.ppermute(
            lax.slice_in_dim(block, block.shape[dim] - width, None, axis=dim), axis, forward
        )
        high = lax.ppermute(lax.slice_in_dim(block, 0, width, axis=dim), axis, backward)
        block = jnp.concatenate([low, block, high], axis=dim)
    return block


def silu_pair(preact):
    logistic = jax.nn.sigmoid(preact)
    return (preact * logistic, logistic * (1.0 + preact * (1.0 - logistic)))


def slot_positions(owner_of, groups, capacity):
    count = owner_of.shape[-1]
    onehot = (owner_of[..., None] == jnp.arange(groups, dtype=jnp.int32)).astype(jnp.bfloat16)
    order = jnp.arange(count, dtype=jnp.int32)
    earlier = (order[None, :] < order[:, None]).astype(jnp.bfloat16)
    before = jnp.einsum("rs,...sg->...rg", earlier, onehot, preferred_element_type=jnp.float32)
    rank_in = jnp.sum(before * onehot.astype(jnp.float32), axis=-1).astype(jnp.int32)
    return (owner_of * capacity + rank_in).astype(jnp.int32)


def column_block(width):
    return math.gcd(width, 512)


def gather_columns(data, wanted):
    count = wanted.shape[0]
    block = column_block(count)
    row_ids = jnp.arange(data.shape[1], dtype=jnp.int32)[:, None]

    def gather_block_product(wanted_block):
        selector = (row_ids == wanted_block[None, :]).astype(data.dtype)
        return jnp.dot(
            data, selector, preferred_element_type=jnp.float32, precision=lax.Precision.HIGHEST
        )

    pieces = lax.map(gather_block_product, wanted.reshape(count // block, block))
    return jnp.transpose(pieces, (1, 0, 2)).reshape(data.shape[0], count)


def place_columns(data, target, width):
    block = column_block(width)
    column_ids = jnp.arange(block, dtype=jnp.int32)[None, :]

    def place_block_product(first_col):
        selector = (target[:, None] == first_col + column_ids).astype(data.dtype)
        return jnp.dot(
            data, selector, preferred_element_type=jnp.float32, precision=lax.Precision.HIGHEST
        )

    starts = jnp.arange(width // block, dtype=jnp.int32) * block
    pieces = lax.map(place_block_product, starts)
    return jnp.transpose(pieces, (1, 0, 2)).reshape(data.shape[0], width)


def device_pass(lookup, kernel_map, weight, incoming):
    channels = lookup.shape[0]
    wide = lookup.shape[1]
    offsets = kernel_map.shape[0]
    owned_len = kernel_map.shape[1]
    per_group = 3
    group_count = offsets // per_group
    table_rows = jnp.transpose(lookup)
    grouped_maps = kernel_map.reshape(group_count, per_group * owned_len)
    grouped_weight = weight.reshape(group_count, per_group, channels, channels)

    def forward(running, pieces):
        columns, kernel = pieces
        picked = jnp.take(table_rows, columns, axis=0).reshape(per_group, owned_len, channels)
        term = jnp.einsum("goc,gvc->ov", kernel, picked, preferred_element_type=jnp.float32)
        return (running + term, None)

    preact = lax.scan(
        forward, jnp.zeros((channels, owned_len), jnp.float32), (grouped_maps, grouped_weight)
    )[0]
    activated, derivative = silu_pair(preact)
    output = activated.astype(jnp.bfloat16)
    grad_pre = (incoming.astype(jnp.float32) * derivative).astype(jnp.bfloat16)

    def backward(grad_rows, pieces):
        columns, kernel = pieces
        picked = jnp.take(table_rows, columns, axis=0).reshape(per_group, owned_len, channels)
        kernel_grad = jnp.einsum(
            "ov,gvc->goc", grad_pre, picked, preferred_element_type=jnp.float32
        )
        spread = jnp.einsum("goc,ov->gvc", kernel, grad_pre, preferred_element_type=jnp.float32)
        grad_rows = grad_rows.at[columns].add(spread.reshape(per_group * owned_len, channels))
        return (grad_rows, kernel_grad)

    grad_rows, kernel_grads = lax.scan(
        backward, jnp.zeros((wide, channels), jnp.float32), (grouped_maps, grouped_weight)
    )
    table_grad = jnp.transpose(grad_rows)
    return (output, table_grad, kernel_grads.reshape(offsets, channels, channels))


def body(points, owners, kernel_maps, face_rows, weight, cotangent):
    local_points = points[0, 0]
    owner_of = owners[0, 0, :, 0]
    kernel_map = kernel_maps[0, 0]
    face_list = face_rows[0, 0]
    incoming = cotangent[0, 0]
    groups = lax.axis_size("sx")
    owned_len = kernel_map.shape[1]
    capacity = owned_len // groups
    channels = local_points.shape[0]
    arrived = local_points.shape[1]
    face_len = face_list.shape[1]
    every_point, every_owner = (
        lax.all_gather(local_points, "sx", axis=1, tiled=True),
        lax.all_gather(owner_of[:, None], "sx", axis=0, tiled=True),
    )
    source_owner = every_owner[:, 0].reshape(groups, arrived)
    source_pos = slot_positions(source_owner, groups, capacity)
    my_index = lax.axis_index("sx")
    sources = jnp.arange(groups, dtype=jnp.int32)[:, None]
    landing = (
        jnp.where(
            source_owner == my_index,
            sources * capacity + source_pos - source_owner * capacity,
            owned_len,
        )
        .reshape(-1)
        .astype(jnp.int32)
    )
    owned = place_columns(every_point, landing, owned_len).astype(jnp.bfloat16)
    boundary = (
        gather_columns(owned, face_list.reshape(-1))
        .astype(jnp.bfloat16)
        .reshape(channels, 2, face_len)
    )
    widened = with_halo(boundary, (("sy", 1),), 1)
    lookup = jnp.concatenate(
        [owned, widened[:, 0], widened[:, 3], jnp.zeros((channels, 1), jnp.bfloat16)], axis=1
    )
    output, table_grad, kernel_grads = device_pass(lookup, kernel_map, weight, incoming)
    scale_factor = 1.0 / math.sqrt(groups * lax.axis_size("sy") * owned_len)
    weight_grad = lax.psum(kernel_grads, ("sx", "sy")) * scale_factor
    back_faces = jnp.stack(
        [
            table_grad[:, owned_len : owned_len + face_len],
            table_grad[:, owned_len + face_len : owned_len + 2 * face_len],
        ],
        axis=1,
    )
    returned_faces = with_halo(back_faces, (("sy", 1),), 1)
    face_grads = jnp.concatenate([returned_faces[:, 0], returned_faces[:, 3]], axis=1)
    owned_grad = table_grad[:, :owned_len] + place_columns(
        face_grads, face_list.reshape(-1), owned_len
    )
    owned_grad = owned_grad.astype(jnp.bfloat16)
    contrib = gather_columns(owned_grad, landing)
    point_grad = lax.psum_scatter(
        contrib.astype(jnp.bfloat16), "sx", scatter_dimension=1, tiled=True
    )
    return (output[None, None], point_grad[None, None], weight_grad)


def solution(mesh):
    return jax.shard_map(
        body,
        mesh=mesh,
        in_specs=(
            P("sx", "sy", None, None),
            P("sx", "sy", None, None),
            P("sx", "sy", None, None),
            P("sx", "sy", None, None),
            P(),
            P("sx", "sy", None, None),
        ),
        out_specs=(P("sx", "sy", None, None), P("sx", "sy", None, None), P()),
        check_vma=False,
    )
```

profile of v0, /device:TPU:1, one launch (start us, length us, event | category | flops | bytes accessed | tf_op | source)
XLA Modules:
  0.0 1334.0 jit_solution(17002541823048862754)
XLA Ops:
  7.9 19.4 %all-gather = s32[1,1,16384,1]{2,3,1,0:T(1,128)S(1)} all-gather(s32[1,1,1024,1]{2,3,1,0:T(1,128)} %param.19), channel_id=2, replica_groups=mesh['sx'=16,'sy'=16] {'sx'}, dimensions={2}, use_global_device_ids=true | all-gather | bytes 69632 | tf_op jit(solution)/shard_map/all_gather | solution.py:126
  31.2 35.7 %all-gather.4.cloned.1.call-done = bf16[1,1,96,16384]{3,2,1,0:T(8,128)(2,1)} async-done(((bf16[1,1,96,1024]{3,2,1,0:T(8,128)(2,1)}), bf16[1,1,96,16384]{3,2,1,0:T(8,128)(2,1)}) %all-gather.4.cloned.1.call-update) | async-done | bytes 3145744 | tf_op jit(solution)/shard_map/all_gather | solution.py:125
  66.9 34.2 %while.66 = (s32[]{:T(128)}, bf16[4,96,512]{2,1,0:T(8,128)(2,1)S(1)}, s32[16,1024]{1,0:T(8,128)S(1)}, s32[4]{0:T(128)S(1)}, bf16[96,16384]{1,0:T(8,128)(2,1)}) while((s32[]{:T(128)}, bf16[4,96,512]{2,1,0:T(8,128)(2,1)S(1)}, s32[16,1024]{1,0:T(8,128)S(1)}, s32[4]{0:T(128)S(1)}, bf16[96,16384]{1,0:T(8,128)(2,1)}) %tuple.142), condition=%wide.region_2.3_spmd.clone.clone, body=%wide.region_1.2_spmd.clone.sunk.clone | while | flops 1619001856 | bytes 3543121 | solution.py:67
  68.2 7.3 fusion.101
  76.7 7.3 fusion.101
  85.3 7.3 fusion.101
  93.9 7.3 fusion.101
  112.3 254.5 %while.69 = (s32[]{:T(128)}, f32[96,2048]{1,0:T(8,128)S(1)}, bf16[9,3,96,96]{3,2,1,0:T(8,128)(2,1)}, s32[9,6144]{1,0:T(8,128)S(1)}, bf16[2561,96]{1,0:T(8,128)(2,1)S(1)}) while((s32[]{:T(128)}, f32[96,2048]{1,0:T(8,128)S(1)}, bf16[9,3,96,96]{3,2,1,0:T(8,128)(2,1)}, s32[9,6144]{1,0:T(8,128)S(1)}, ...), condition=%wide.region_4.6_spmd.clone.clone, body=%wide.region_3.5_spmd.clone.sunk.clone | while | flops 114290688 | bytes 7705163 | solution.py:88
  112.3 22.2 %gather_fusion.1 = bf16[6144,96]{1,0:T(8,128)(2,1)} fusion(bf16[2561,96]{1,0:T(8,128)(2,1)S(1)} %get-tuple-element.575, s32[6144]{0:T(1024)S(1)} %fusion.109), kind=kCustom, calls=%fused_computation.clone.clone.1.clone | custom fusion | bytes 2383872 | tf_op jit(solution)/shard_map/while/body/eval_jaxpr/jit(_take)/gather | solution.py:84
  134.5 4.4 broadcast_select_fusion.7
  140.6 22.2 %gather_fusion.1 = bf16[6144,96]{1,0:T(8,128)(2,1)} fusion(bf16[2561,96]{1,0:T(8,128)(2,1)S(1)} %get-tuple-element.575, s32[6144]{0:T(1024)S(1)} %fusion.109), kind=kCustom, calls=%fused_computation.clone.clone.1.clone | custom fusion | bytes 2383872 | tf_op jit(solution)/shard_map/while/body/eval_jaxpr/jit(_take)/gather | solution.py:84
  162.8 4.4 broadcast_select_fusion.7
  168.9 22.2 %gather_fusion.1 = bf16[6144,96]{1,0:T(8,128)(2,1)} fusion(bf16[2561,96]{1,0:T(8,128)(2,1)S(1)} %get-tuple-element.575, s32[6144]{0:T(1024)S(1)} %fusion.109), kind=kCustom, calls=%fused_computation.clone.clone.1.clone | custom fusion | bytes 2383872 | tf_op jit(solution)/shard_map/while/body/eval_jaxpr/jit(_take)/gather | solution.py:84
  191.1 4.4 broadcast_select_fusion.7
  197.2 22.2 %gather_fusion.1 = bf16[6144,96]{1,0:T(8,128)(2,1)} fusion(bf16[2561,96]{1,0:T(8,128)(2,1)S(1)} %get-tuple-element.575, s32[6144]{0:T(1024)S(1)} %fusion.109), kind=kCustom, calls=%fused_computation.clone.clone.1.clone | custom fusion | bytes 2383872 | tf_op jit(solution)/shard_map/while/body/eval_jaxpr/jit(_take)/gather | solution.py:84
  219.4 4.4 broadcast_select_fusion.7
  225.5 22.2 %gather_fusion.1 = bf16[6144,96]{1,0:T(8,128)(2,1)} fusion(bf16[2561,96]{1,0:T(8,128)(2,1)S(1)} %get-tuple-element.575, s32[6144]{0:T(1024)S(1)} %fusion.109), kind=kCustom, calls=%fused_computation.clone.clone.1.clone | custom fusion | bytes 2383872 | tf_op jit(solution)/shard_map/while/body/eval_jaxpr/jit(_take)/gather | solution.py:84
  247.7 4.4 broadcast_select_fusion.7
  253.8 22.2 %gather_fusion.1 = bf16[6144,96]{1,0:T(8,128)(2,1)} fusion(bf16[2561,96]{1,0:T(8,128)(2,1)S(1)} %get-tuple-element.575, s32[6144]{0:T(1024)S(1)} %fusion.109), kind=kCustom, calls=%fused_computation.clone.clone.1.clone | custom fusion | bytes 2383872 | tf_op jit(solution)/shard_map/while/body/eval_jaxpr/jit(_take)/gather | solution.py:84
  276.0 4.4 broadcast_select_fusion.7
  282.0 22.2 %gather_fusion.1 = bf16[6144,96]{1,0:T(8,128)(2,1)} fusion(bf16[2561,96]{1,0:T(8,128)(2,1)S(1)} %get-tuple-element.575, s32[6144]{0:T(1024)S(1)} %fusion.109), kind=kCustom, calls=%fused_computation.clone.clone.1.clone | custom fusion | bytes 2383872 | tf_op jit(solution)/shard_map/while/body/eval_jaxpr/jit(_take)/gather | solution.py:84
  304.2 4.4 broadcast_select_fusion.7
  310.3 22.2 %gather_fusion.1 = bf16[6144,96]{1,0:T(8,128)(2,1)} fusion(bf16[2561,96]{1,0:T(8,128)(2,1)S(1)} %get-tuple-element.575, s32[6144]{0:T(1024)S(1)} %fusion.109), kind=kCustom, calls=%fused_computation.clone.clone.1.clone | custom fusion | bytes 2383872 | tf_op jit(solution)/shard_map/while/body/eval_jaxpr/jit(_take)/gather | solution.py:84
  332.5 4.4 broadcast_select_fusion.7
  338.6 22.2 %gather_fusion.1 = bf16[6144,96]{1,0:T(8,128)(2,1)} fusion(bf16[2561,96]{1,0:T(8,128)(2,1)S(1)} %get-tuple-element.575, s32[6144]{0:T(1024)S(1)} %fusion.109), kind=kCustom, calls=%fused_computation.clone.clone.1.clone | custom fusion | bytes 2383872 | tf_op jit(solution)/shard_map/while/body/eval_jaxpr/jit(_take)/gather | solution.py:84
  369.2 611.8 %while.65 = (s32[]{:T(128)}, f32[2561,96]{1,0:T(8,128)S(1)}, f32[9,3,96,96]{3,2,1,0:T(8,128)}, s32[9,6144]{1,0:T(8,128)S(1)}, bf16[9,3,96,96]{3,2,1,0:T(8,128)(2...) while((s32[]{:T(128)}, f32[2561,96]{1,0:T(8,128)S(1)}, ...), condition=%wide.region_7.9_spmd.clone, body=%wide.region_5.8_spmd.sunk.clone | while | flops 227751936 | bytes 26825976 | solution.py:105
  370.5 21.0 %gather_fusion = bf16[6144,96]{1,0:T(8,128)(2,1)S(1)} fusion(bf16[2561,96]{1,0:T(8,128)(2,1)S(1)} %get-tuple-element.596, s32[6144]{0:T(1024)} %fusion.98), kind=kCustom, calls=%fused_computation.1.clone.clone.1.clone | custom fusion | bytes 2383872 | tf_op jit(solution)/shard_map/while/body/eval_jaxpr/jit(_take)/gather | solution.py:97
  403.2 33.9 %scatter_fusion = f32[2561,96]{1,0:T(8,128)S(1)} fusion(f32[2561,96]{1,0:T(8,128)S(1)} %get-tuple-element.584, s32[6144]{0:T(1024)S(1)} %bitcast.226, f32[6144,96]{1,0:T(8,128)} %bitcast.211), kind=kCustom, calls=%fused_computation.2.clone.1.clone | custom fusion | flops 589824 | bytes 7102464 | tf_op jit(solution)/shard_map/while/body/eval_jaxpr/scatter-add | solution.py:102
  438.5 21.0 %gather_fusion = bf16[6144,96]{1,0:T(8,128)(2,1)S(1)} fusion(bf16[2561,96]{1,0:T(8,128)(2,1)S(1)} %get-tuple-element.596, s32[6144]{0:T(1024)} %fusion.98), kind=kCustom, calls=%fused_computation.1.clone.clone.1.clone | custom fusion | bytes 2383872 | tf_op jit(solution)/shard_map/while/body/eval_jaxpr/jit(_take)/gather | solution.py:97
  471.2 33.9 %scatter_fusion = f32[2561,96]{1,0:T(8,128)S(1)} fusion(f32[2561,96]{1,0:T(8,128)S(1)} %get-tuple-element.584, s32[6144]{0:T(1024)S(1)} %bitcast.226, f32[6144,96]{1,0:T(8,128)} %bitcast.211), kind=kCustom, calls=%fused_computation.2.clone.1.clone | custom fusion | flops 589824 | bytes 7102464 | tf_op jit(solution)/shard_map/while/body/eval_jaxpr/scatter-add | solution.py:102
  506.5 21.0 %gather_fusion = bf16[6144,96]{1,0:T(8,128)(2,1)S(1)} fusion(bf16[2561,96]{1,0:T(8,128)(2,1)S(1)} %get-tuple-element.596, s32[6144]{0:T(1024)} %fusion.98), kind=kCustom, calls=%fused_computation.1.clone.clone.1.clone | custom fusion | bytes 2383872 | tf_op jit(solution)/shard_map/while/body/eval_jaxpr/jit(_take)/gather | solution.py:97
  539.1 33.9 %scatter_fusion = f32[2561,96]{1,0:T(8,128)S(1)} fusion(f32[2561,96]{1,0:T(8,128)S(1)} %get-tuple-element.584, s32[6144]{0:T(1024)S(1)} %bitcast.226, f32[6144,96]{1,0:T(8,128)} %bitcast.211), kind=kCustom, calls=%fused_computation.2.clone.1.clone | custom fusion | flops 589824 | bytes 7102464 | tf_op jit(solution)/shard_map/while/body/eval_jaxpr/scatter-add | solution.py:102
  574.5 21.0 %gather_fusion = bf16[6144,96]{1,0:T(8,128)(2,1)S(1)} fusion(bf16[2561,96]{1,0:T(8,128)(2,1)S(1)} %get-tuple-element.596, s32[6144]{0:T(1024)} %fusion.98), kind=kCustom, calls=%fused_computation.1.clone.clone.1.clone | custom fusion | bytes 2383872 | tf_op jit(solution)/shard_map/while/body/eval_jaxpr/jit(_take)/gather | solution.py:97
  607.1 33.9 %scatter_fusion = f32[2561,96]{1,0:T(8,128)S(1)} fusion(f32[2561,96]{1,0:T(8,128)S(1)} %get-tuple-element.584, s32[6144]{0:T(1024)S(1)} %bitcast.226, f32[6144,96]{1,0:T(8,128)} %bitcast.211), kind=kCustom, calls=%fused_computation.2.clone.1.clone | custom fusion | flops 589824 | bytes 7102464 | tf_op jit(solution)/shard_map/while/body/eval_jaxpr/scatter-add | solution.py:102
  642.4 21.0 %gather_fusion = bf16[6144,96]{1,0:T(8,128)(2,1)S(1)} fusion(bf16[2561,96]{1,0:T(8,128)(2,1)S(1)} %get-tuple-element.596, s32[6144]{0:T(1024)} %fusion.98), kind=kCustom, calls=%fused_computation.1.clone.clone.1.clone | custom fusion | bytes 2383872 | tf_op jit(solution)/shard_map/while/body/eval_jaxpr/jit(_take)/gather | solution.py:97
  675.1 33.9 %scatter_fusion = f32[2561,96]{1,0:T(8,128)S(1)} fusion(f32[2561,96]{1,0:T(8,128)S(1)} %get-tuple-element.584, s32[6144]{0:T(1024)S(1)} %bitcast.226, f32[6144,96]{1,0:T(8,128)} %bitcast.211), kind=kCustom, calls=%fused_computation.2.clone.1.clone | custom fusion | flops 589824 | bytes 7102464 | tf_op jit(solution)/shard_map/while/body/eval_jaxpr/scatter-add | solution.py:102
  710.4 21.0 %gather_fusion = bf16[6144,96]{1,0:T(8,128)(2,1)S(1)} fusion(bf16[2561,96]{1,0:T(8,128)(2,1)S(1)} %get-tuple-element.596, s32[6144]{0:T(1024)} %fusion.98), kind=kCustom, calls=%fused_computation.1.clone.clone.1.clone | custom fusion | bytes 2383872 | tf_op jit(solution)/shard_map/while/body/eval_jaxpr/jit(_take)/gather | solution.py:97
  743.1 33.9 %scatter_fusion = f32[2561,96]{1,0:T(8,128)S(1)} fusion(f32[2561,96]{1,0:T(8,128)S(1)} %get-tuple-element.584, s32[6144]{0:T(1024)S(1)} %bitcast.226, f32[6144,96]{1,0:T(8,128)} %bitcast.211), kind=kCustom, calls=%fused_computation.2.clone.1.clone | custom fusion | flops 589824 | bytes 7102464 | tf_op jit(solution)/shard_map/while/body/eval_jaxpr/scatter-add | solution.py:102
  778.4 21.0 %gather_fusion = bf16[6144,96]{1,0:T(8,128)(2,1)S(1)} fusion(bf16[2561,96]{1,0:T(8,128)(2,1)S(1)} %get-tuple-element.596, s32[6144]{0:T(1024)} %fusion.98), kind=kCustom, calls=%fused_computation.1.clone.clone.1.clone | custom fusion | bytes 2383872 | tf_op jit(solution)/shard_map/while/body/eval_jaxpr/jit(_take)/gather | solution.py:97
  811.0 33.9 %scatter_fusion = f32[2561,96]{1,0:T(8,128)S(1)} fusion(f32[2561,96]{1,0:T(8,128)S(1)} %get-tuple-element.584, s32[6144]{0:T(1024)S(1)} %bitcast.226, f32[6144,96]{1,0:T(8,128)} %bitcast.211), kind=kCustom, calls=%fused_computation.2.clone.1.clone | custom fusion | flops 589824 | bytes 7102464 | tf_op jit(solution)/shard_map/while/body/eval_jaxpr/scatter-add | solution.py:102
  846.4 21.0 %gather_fusion = bf16[6144,96]{1,0:T(8,128)(2,1)S(1)} fusion(bf16[2561,96]{1,0:T(8,128)(2,1)S(1)} %get-tuple-element.596, s32[6144]{0:T(1024)} %fusion.98), kind=kCustom, calls=%fused_computation.1.clone.clone.1.clone | custom fusion | bytes 2383872 | tf_op jit(solution)/shard_map/while/body/eval_jaxpr/jit(_take)/gather | solution.py:97
  879.0 33.9 %scatter_fusion = f32[2561,96]{1,0:T(8,128)S(1)} fusion(f32[2561,96]{1,0:T(8,128)S(1)} %get-tuple-element.584, s32[6144]{0:T(1024)S(1)} %bitcast.226, f32[6144,96]{1,0:T(8,128)} %bitcast.211), kind=kCustom, calls=%fused_computation.2.clone.1.clone | custom fusion | flops 589824 | bytes 7102464 | tf_op jit(solution)/shard_map/while/body/eval_jaxpr/scatter-add | solution.py:102
  914.3 21.0 %gather_fusion = bf16[6144,96]{1,0:T(8,128)(2,1)S(1)} fusion(bf16[2561,96]{1,0:T(8,128)(2,1)S(1)} %get-tuple-element.596, s32[6144]{0:T(1024)} %fusion.98), kind=kCustom, calls=%fused_computation.1.clone.clone.1.clone | custom fusion | bytes 2383872 | tf_op jit(solution)/shard_map/while/body/eval_jaxpr/jit(_take)/gather | solution.py:97
  947.0 33.9 %scatter_fusion = f32[2561,96]{1,0:T(8,128)S(1)} fusion(f32[2561,96]{1,0:T(8,128)S(1)} %get-tuple-element.584, s32[6144]{0:T(1024)S(1)} %bitcast.226, f32[6144,96]{1,0:T(8,128)} %bitcast.211), kind=kCustom, calls=%fused_computation.2.clone.1.clone | custom fusion | flops 589824 | bytes 7102464 | tf_op jit(solution)/shard_map/while/body/eval_jaxpr/scatter-add | solution.py:102
  990.8 6.9 while.67
  997.9 46.9 %while.68 = (s32[]{:T(128)}, bf16[32,96,512]{2,1,0:T(8,128)(2,1)}, s32[32,512]{1,0:T(8,128)S(1)}, bf16[96,2048]{1,0:T(8,128)(2,1)S(1)}) while((s32[]{:T(128)}, bf16[32,96,512]{2,1,0:T(8,128)(2,1)}, s32[32,512]{1,0:T(8,128)S(1)}, bf16[96,2048]{1,0:T(8,128)(2,1)S(1)}) %tuple.128), condition=%wide.region_11.13_spmd.clone.clone, body=%wide.region_10.12_spmd.clone.sunk.clone | while | flops 202375168 | bytes 596537 | solution.py:52
  1048.8 196.4 %all-reduce.2.cloned.1.call-done = f32[27,96,96]{2,1,0:T(8,128)} async-done(((f32[27,96,96]{2,1,0:T(8,128)}), f32[27,96,96]{2,1,0:T(8,128)}) %all-reduce.2.cloned.1.call-update) | async-done | bytes 995344 | tf_op jit(solution)/shard_map/psum | solution.py:153
  1247.7 79.8 %reduce-scatter.2.cloned.1.call-done = bf16[96,1024]{1,0:T(8,128)(2,1)} async-done(((bf16[96,16384]{1,0:T(8,128)(2,1)}), bf16[96,1024]{1,0:T(8,128)(2,1)}) %reduce-scatter.2.cloned.1.call-update) | async-done | bytes 196624 | tf_op jit(solution)/shard_map/reduce_scatter | solution.py:168
  (382 shorter events, 228.8 us)
Async XLA Ops:
  7.2 59.8 %all-gather.4.cloned.1.call-start = ((), (), s32[]{:S(2)}) async-start(), calls=%async_computation.3 | async-start | bytes 3342336 | tf_op jit(solution)/shard_map/all_gather | solution.py:125
  7.9 1237.3 %all-reduce.2.cloned.1.call-start = ((), (), s32[]{:S(2)}) async-start(), calls=%async_computation.2 | async-start | bytes 2654208 | tf_op jit(solution)/shard_map/psum | solution.py:153
  101.2 7.5 copy-start.8
  102.3 9.1 collective-permute-start
  106.3 5.4 collective-permute-start.1
  392.3 3.2 copy-start
  395.5 1.4 copy-start.1
  399.8 3.4 copy-start.3
  403.2 33.9 %copy-start.5 = (s32[9,6144]{1,0:T(8,128)S(1)}, s32[9,6144]{1,0:T(8,128)}, u32[]{:S(2)}) copy-start(s32[9,6144]{1,0:T(8,128)} %copy-done.4) | copy-start | bytes 663556 | tf_op jit(solution)/shard_map/while
  460.3 3.2 copy-start
  463.5 1.4 copy-start.1
  467.8 3.4 copy-start.3
  471.2 33.9 %copy-start.5 = (s32[9,6144]{1,0:T(8,128)S(1)}, s32[9,6144]{1,0:T(8,128)}, u32[]{:S(2)}) copy-start(s32[9,6144]{1,0:T(8,128)} %copy-done.4) | copy-start | bytes 663556 | tf_op jit(solution)/shard_map/while
  528.2 3.2 copy-start
  531.5 1.4 copy-start.1
  535.7 3.4 copy-start.3
  539.1 33.9 %copy-start.5 = (s32[9,6144]{1,0:T(8,128)S(1)}, s32[9,6144]{1,0:T(8,128)}, u32[]{:S(2)}) copy-start(s32[9,6144]{1,0:T(8,128)} %copy-done.4) | copy-start | bytes 663556 | tf_op jit(solution)/shard_map/while
  596.2 3.2 copy-start
  599.5 1.4 copy-start.1
  603.7 3.4 copy-start.3
  607.1 33.9 %copy-start.5 = (s32[9,6144]{1,0:T(8,128)S(1)}, s32[9,6144]{1,0:T(8,128)}, u32[]{:S(2)}) copy-start(s32[9,6144]{1,0:T(8,128)} %copy-done.4) | copy-start | bytes 663556 | tf_op jit(solution)/shard_map/while
  664.2 3.2 copy-start
  667.4 1.4 copy-start.1
  671.7 3.4 copy-start.3
  675.1 33.9 %copy-start.5 = (s32[9,6144]{1,0:T(8,128)S(1)}, s32[9,6144]{1,0:T(8,128)}, u32[]{:S(2)}) copy-start(s32[9,6144]{1,0:T(8,128)} %copy-done.4) | copy-start | bytes 663556 | tf_op jit(solution)/shard_map/while
  732.2 3.2 copy-start
  735.4 1.4 copy-start.1
  739.7 3.4 copy-start.3
  743.1 33.9 %copy-start.5 = (s32[9,6144]{1,0:T(8,128)S(1)}, s32[9,6144]{1,0:T(8,128)}, u32[]{:S(2)}) copy-start(s32[9,6144]{1,0:T(8,128)} %copy-done.4) | copy-start | bytes 663556 | tf_op jit(solution)/shard_map/while
  800.1 3.2 copy-start
  803.4 1.4 copy-start.1
  807.6 3.4 copy-start.3
  811.0 33.9 %copy-start.5 = (s32[9,6144]{1,0:T(8,128)S(1)}, s32[9,6144]{1,0:T(8,128)}, u32[]{:S(2)}) copy-start(s32[9,6144]{1,0:T(8,128)} %copy-done.4) | copy-start | bytes 663556 | tf_op jit(solution)/shard_map/while
  868.1 3.2 copy-start
  871.4 1.4 copy-start.1
  875.6 3.4 copy-start.3
  879.0 33.9 %copy-start.5 = (s32[9,6144]{1,0:T(8,128)S(1)}, s32[9,6144]{1,0:T(8,128)}, u32[]{:S(2)}) copy-start(s32[9,6144]{1,0:T(8,128)} %copy-done.4) | copy-start | bytes 663556 | tf_op jit(solution)/shard_map/while
  936.1 3.2 copy-start
  939.3 1.4 copy-start.1
  943.6 3.4 copy-start.3
  947.0 33.9 %copy-start.5 = (s32[9,6144]{1,0:T(8,128)S(1)}, s32[9,6144]{1,0:T(8,128)}, u32[]{:S(2)}) copy-start(s32[9,6144]{1,0:T(8,128)} %copy-done.4) | copy-start | bytes 663556 | tf_op jit(solution)/shard_map/while
  980.9 5.8 copy-start.6
  980.9 5.8 copy-start.7
  981.0 5.8 copy-start.10
  981.4 9.4 copy-start.9
  981.4 5.6 collective-permute-start.2
  984.8 5.9 collective-permute-start.3
  986.9 340.5 %reduce-scatter.2.cloned.1.call-start = ((), (), s32[]{:S(2)}) async-start(), calls=%async_computation.1 | async-start | bytes 3342336 | tf_op jit(solution)/shard_map/reduce_scatter | solution.py:168
  (18 other events, 18.0 us)
Sparse Core Ops, SparseCore 0:
  10.4 56.4 all-gather.3
  987.0 258.0 all-reduce.1
  1249.8 77.5 reduce-scatter.1
where the time goes:
time: 1340 us; the launch traced here: 1330 us
  local copies, waits for them, and re-layouts  440 us (33%)
  other arithmetic  405 us (30%)
  waiting for transfers between devices  317 us (24%)
  matrix products  125 us (9%)
  blocking collectives  19.4 us (1%)
  between operations  14.1 us (1%)
    scatter-add x9, other arithmetic, backward(): grad_rows.at[columns].add(spread.reshape(per_group * owned_len, channels))  305 us
    gather x9, local copies, waits for them, and re-layouts, forward(): jnp.take(table_rows, columns, axis=0)  200 us
    psum x1, waiting for transfers between devices, body(): weight_grad = lax.psum(kernel_grads, ('sx', 'sy')) * scale_factor  196 us
    gather x9, local copies, waits for them, and re-layouts, backward(): jnp.take(table_rows, columns, axis=0)  189 us
    reduce_scatter x1, waiting for transfers between devices, body(): lax.psum_scatter(contrib.astype(jnp.bfloat16), 'sx', scatter_dimension=1,...  79.8 us
    dot_general x33, matrix products, gather_block_product(): jnp.dot(data, selector, preferred_element_type=jnp.float32, precision=lax...  47.4 us
    select_n x9, other arithmetic, forward(): jnp.take(table_rows, columns, axis=0)  39.3 us
    all_gather x1, waiting for transfers between devices, body(): lax.all_gather(local_points, 'sx', axis=1, tiled=True)  35.7 us
  transfers between devices with their start and end apart: 7, of which 5 were waited for; matrix products, arithmetic and copies ran while one was open for 5% of the time, Pallas kernels for 0%

commit v1 on v0

v1 whole, which is shorter than its diff:
```python
import math

import jax
import jax.numpy as jnp
from jax import lax
from jax.experimental import pallas as pl
from jax.experimental.pallas import tpu as pltpu
from jax.sharding import PartitionSpec as P

C = 96
K = 27
R = 1024
F = 256
CAP = 128
V = 2048
GROUPS = 16
LO = 256
BANKS = V // LO
ALL_BANKS = BANKS + 2
VB = 256
PER_DOT = 3

BF = jnp.bfloat16
F32 = jnp.float32
NT = (((1,), (1,)), ((), ()))


def onehot_rows(low, rows):
    row = lax.broadcasted_iota(jnp.int32, (rows, low.shape[-1]), 0)
    return jnp.where(row == low, 1.0, 0.0).astype(BF)


def select_banks(product, bank, banks):
    n = bank.shape[-1]
    bank8 = jnp.broadcast_to(bank, (8, n))
    kept = jnp.zeros((C // 8, 8, n), F32)
    for a in range(banks):
        part = product[a * C : (a + 1) * C].reshape(C // 8, 8, n)
        kept = jnp.where((bank8 == a)[None], part, kept)
    return kept.reshape(C, n)


def masked_banks(values, bank, banks, out_ref, column):
    n = bank.shape[-1]
    for a in range(banks):
        mask = jnp.where(jnp.broadcast_to(bank, (16, n)) == a, 1.0, 0.0).astype(BF)
        spread = values.reshape(C // 16, 16, n) * mask[None]
        out_ref[a * C : (a + 1) * C, column : column + n] = spread.reshape(C, n)


def place_kernel(points_ref, owner_ref, out_ref, slot_ref, masked_ref):
    owner = owner_ref[...]
    row = lax.broadcasted_iota(jnp.int32, (CAP, CAP), 0)
    col = lax.broadcasted_iota(jnp.int32, (CAP, CAP), 1)
    earlier = jnp.where(row < col, 1.0, 0.0).astype(BF)
    group = lax.broadcasted_iota(jnp.int32, (GROUPS, CAP), 0)
    total = jnp.zeros((GROUPS, 1), F32)
    for b in range(R // CAP):
        mine = jnp.where(group == owner[:, b * CAP : (b + 1) * CAP], 1.0, 0.0)
        before = jnp.dot(mine.astype(BF), earlier, preferred_element_type=F32) + total
        slot = jnp.sum(mine * before, axis=0, keepdims=True)
        slot_ref[:, b * CAP : (b + 1) * CAP] = slot.astype(jnp.int32)
        total = total + jnp.sum(mine, axis=1, keepdims=True)
    masked_banks(points_ref[...], owner, GROUPS, masked_ref, 0)
    onehot = onehot_rows(slot_ref[...], CAP)
    for g in range(GROUPS):
        out_ref[g] = lax.dot_general(
            masked_ref[g * C : (g + 1) * C, :], onehot, NT, preferred_element_type=F32
        ).astype(BF)


def place_points(points, owner):
    return pl.pallas_call(
        place_kernel,
        out_shape=(
            jax.ShapeDtypeStruct((GROUPS, C, CAP), BF),
            jax.ShapeDtypeStruct((1, R), jnp.int32),
        ),
        scratch_shapes=[pltpu.VMEM((GROUPS * C, R), BF)],
        compiler_params=pltpu.CompilerParams(vmem_limit_bytes=48 << 20),
        name="place",
    )(points, owner)


def faces_kernel(owned_ref, rows_ref, lower_ref, upper_ref):
    table = owned_ref[...].reshape(GROUPS * C, CAP)
    for j, out_ref in enumerate((lower_ref, upper_ref)):
        rows = rows_ref[j : j + 1, :]
        product = jnp.dot(table, onehot_rows(rows & (CAP - 1), CAP), preferred_element_type=F32)
        out_ref[...] = select_banks(product, rows >> 7, GROUPS).astype(BF)


def take_faces(owned, face_rows):
    return pl.pallas_call(
        faces_kernel,
        out_shape=(jax.ShapeDtypeStruct((C, F), BF),) * 2,
        compiler_params=pltpu.CompilerParams(vmem_limit_bytes=48 << 20),
        name="faces",
    )(owned, face_rows)


def forward_kernel(
    owned_ref, low_ref, high_ref, map_ref, weight_ref, cot_ref, out_ref, pre_ref, wg_ref, table_ref, picked_ref, acc_ref
):
    step = pl.program_id(0)

    @pl.when(step == 0)
    def _():
        for g in range(GROUPS):
            table_ref[(g // 2) * C : (g // 2 + 1) * C, (g % 2) * CAP : (g % 2 + 1) * CAP] = owned_ref[g]
        table_ref[BANKS * C : (BANKS + 1) * C, :] = low_ref[...]
        table_ref[(BANKS + 1) * C :, :] = high_ref[...]
        acc_ref[...] = jnp.zeros_like(acc_ref)

    table = table_ref[...]
    for k in range(K):
        index = map_ref[k]
        product = jnp.dot(table, onehot_rows(index & (LO - 1), LO), preferred_element_type=F32)
        picked_ref[k * C : (k + 1) * C, :] = select_banks(product, index >> 8, ALL_BANKS).astype(BF)
    preact = jnp.dot(weight_ref[...], picked_ref[...], preferred_element_type=F32)
    logistic = jax.nn.sigmoid(preact)
    out_ref[...] = (preact * logistic).astype(BF)
    slope = logistic * (1.0 + preact * (1.0 - logistic))
    grad_pre = (cot_ref[...].astype(F32) * slope).astype(BF)
    pre_ref[...] = grad_pre
    acc_ref[...] += lax.dot_general(picked_ref[...], grad_pre, NT, preferred_element_type=F32)

    @pl.when(step == pl.num_programs(0) - 1)
    def _():
        for k in range(K):
            wg_ref[k] = acc_ref[k * C : (k + 1) * C, :].T


def forward_pass(owned, low, high, kernel_map, weight, cotangent):
    whole = lambda *shape: pl.BlockSpec(shape, lambda i: (0,) * len(shape))
    column = lambda rows: pl.BlockSpec((rows, VB), lambda i: (0, i))
    return pl.pallas_call(
        forward_kernel,
        grid=(V // VB,),
        in_specs=[
            whole(GROUPS, C, CAP),
            whole(C, F),
            whole(C, F),
            pl.BlockSpec((K, 1, VB), lambda i: (0, 0, i)),
            whole(C, K * C),
            column(C),
        ],
        out_specs=(column(C), column(C), whole(K, C, C)),
        out_shape=(
            jax.ShapeDtypeStruct((C, V), BF),
            jax.ShapeDtypeStruct((C, V), BF),
            jax.ShapeDtypeStruct((K, C, C), F32),
        ),
        scratch_shapes=[
            pltpu.VMEM((ALL_BANKS * C, LO), BF),
            pltpu.VMEM((K * C, VB), BF),
            pltpu.VMEM((K * C, C), F32),
        ],
        compiler_params=pltpu.CompilerParams(vmem_limit_bytes=56 << 20),
        cost_estimate=pl.CostEstimate(
            flops=2 * K * V * ALL_BANKS * C * LO, bytes_accessed=4 << 20, transcendentals=C * V
        ),
        name="gather_forward",
    )(owned, low, high, kernel_map, weight, cotangent)


def scatter_kernel(map_ref, weight_ref, pre_ref, own_ref, low_ref, high_ref, spread_ref, masked_ref, acc_ref):
    step = pl.program_id(0)

    @pl.when(step == 0)
    def _():
        acc_ref[...] = jnp.zeros_like(acc_ref)

    spread_ref[...] = jnp.dot(weight_ref[...], pre_ref[...], preferred_element_type=F32).astype(BF)
    for first in range(0, K, PER_DOT):
        hots = []
        for j in range(PER_DOT):
            k = first + j
            index = map_ref[k]
            masked_banks(spread_ref[k * C : (k + 1) * C, :], index >> 8, ALL_BANKS, masked_ref, j * VB)
            hots.append(onehot_rows(index & (LO - 1), LO))
        acc_ref[...] += lax.dot_general(
            masked_ref[...], jnp.concatenate(hots, axis=1), NT, preferred_element_type=F32
        )

    @pl.when(step == pl.num_programs(0) - 1)
    def _():
        own_ref[...] = acc_ref[: BANKS * C, :]
        low_ref[...] = acc_ref[BANKS * C : (BANKS + 1) * C, :].astype(BF)
        high_ref[...] = acc_ref[(BANKS + 1) * C :, :].astype(BF)


def scatter_pass(kernel_map, weight, grad_pre):
    whole = lambda *shape: pl.BlockSpec(shape, lambda i: (0,) * len(shape))
    column = lambda rows: pl.BlockSpec((rows, VB), lambda i: (0, i))
    return pl.pallas_call(
        scatter_kernel,
        grid=(V // VB,),
        in_specs=[pl.BlockSpec((K, 1, VB), lambda i: (0, 0, i)), whole(K * C, C), column(C)],
        out_specs=(whole(BANKS * C, LO), whole(C, F), whole(C, F)),
        out_shape=(
            jax.ShapeDtypeStruct((BANKS * C, LO), F32),
            jax.ShapeDtypeStruct((C, F), BF),
            jax.ShapeDtypeStruct((C, F), BF),
        ),
        scratch_shapes=[
            pltpu.VMEM((K * C, VB), BF),
            pltpu.VMEM((ALL_BANKS * C, PER_DOT * VB), BF),
            pltpu.VMEM((ALL_BANKS * C, LO), F32),
        ],
        compiler_params=pltpu.CompilerParams(vmem_limit_bytes=56 << 20),
        cost_estimate=pl.CostEstimate(
            flops=2 * K * V * ALL_BANKS * C * LO, bytes_accessed=2 << 20, transcendentals=0
        ),
        name="scatter_backward",
    )(kernel_map, weight, grad_pre)


def fold_kernel(grad_ref, from_low_ref, from_high_ref, rows_ref, out_ref, masked_ref):
    hots = []
    for j, part_ref in enumerate((from_low_ref, from_high_ref)):
        rows = rows_ref[j : j + 1, :]
        masked_banks(part_ref[...], rows >> 8, BANKS, masked_ref, j * F)
        hots.append(onehot_rows(rows & (LO - 1), LO))
    folded = lax.dot_general(
        masked_ref[...], jnp.concatenate(hots, axis=1), NT, preferred_element_type=F32
    )
    total = (grad_ref[...] + folded).astype(BF)
    for g in range(GROUPS):
        out_ref[g] = total[(g // 2) * C : (g // 2 + 1) * C, (g % 2) * CAP : (g % 2 + 1) * CAP]


def fold_faces(table_grad, from_low, from_high, face_rows):
    return pl.pallas_call(
        fold_kernel,
        out_shape=jax.ShapeDtypeStruct((GROUPS, C, CAP), BF),
        scratch_shapes=[pltpu.VMEM((BANKS * C, 2 * F), BF)],
        compiler_params=pltpu.CompilerParams(vmem_limit_bytes=48 << 20),
        name="fold",
    )(table_grad, from_low, from_high, face_rows)


def take_back_kernel(back_ref, owner_ref, slot_ref, out_ref):
    table = back_ref[...].reshape(GROUPS * C, CAP)
    for b in range(R // LO):
        cols = slice(b * LO, (b + 1) * LO)
        product = jnp.dot(table, onehot_rows(slot_ref[:, cols], CAP), preferred_element_type=F32)
        out_ref[:, cols] = select_banks(product, owner_ref[:, cols], GROUPS).astype(BF)


def take_back(returned, owner, slot):
    return pl.pallas_call(
        take_back_kernel,
        out_shape=jax.ShapeDtypeStruct((C, R), BF),
        compiler_params=pltpu.CompilerParams(vmem_limit_bytes=48 << 20),
        name="take_back",
    )(returned, owner, slot)


def body(points, owners, kernel_maps, face_rows, weight, cotangent):
    points, owner = points[0, 0], owners.reshape(1, R)
    kernel_map, face_list, incoming = kernel_maps.reshape(K, 1, V), face_rows[0, 0], cotangent[0, 0]
    side = lax.axis_size("sy")
    up = [(i, i + 1) for i in range(side - 1)]
    down = [(i + 1, i) for i in range(side - 1)]

    outgoing, slot = place_points(points, owner)
    owned = lax.all_to_all(outgoing, "sx", 0, 0, tiled=True)
    lower, upper = take_faces(owned, face_list)
    ghost_low = lax.ppermute(upper, "sy", up)
    ghost_high = lax.ppermute(lower, "sy", down)
    weight_rows = jnp.transpose(weight, (1, 0, 2)).reshape(C, K * C)
    output, grad_pre, weight_part = forward_pass(
        owned, ghost_low, ghost_high, kernel_map, weight_rows, incoming
    )
    weight_grad = lax.psum(weight_part, ("sx", "sy")) * (1.0 / math.sqrt(GROUPS * side * V))
    weight_columns = jnp.transpose(weight, (0, 2, 1)).reshape(K * C, C)
    table_grad, to_low, to_high = scatter_pass(kernel_map, weight_columns, grad_pre)
    from_low = lax.ppermute(to_high, "sy", up)
    from_high = lax.ppermute(to_low, "sy", down)
    owned_grad = fold_faces(table_grad, from_low, from_high, face_list)
    returned = lax.all_to_all(owned_grad, "sx", 0, 0, tiled=True)
    point_grad = take_back(returned, owner, slot)
    return (output[None, None], point_grad[None, None], weight_grad)


def solution(mesh):
    split = P("sx", "sy", None, None)
    return jax.shard_map(
        body,
        mesh=mesh,
        in_specs=(split, split, split, split, P(), split),
        out_specs=(split, split, P()),
        check_vma=False,
    )
```

time: 1340 us -> 346 us (0.26)
  local copies, waits for them, and re-layouts: 440 us -> 6.61 us
  other arithmetic: 405 us -> 2.5 us
  matrix products: 125 us -> 0 us
  waiting for transfers between devices: 317 us -> 201 us
  Pallas kernels: 0 us -> 81.1 us
    gather x18 -> x0, local copies, waits for them, and re-layouts: 389 us -> none  [the longest x9 200 us: forward(): jnp.take(table_rows, columns, axis=0)]
    scatter-add x9 -> x0, other arithmetic: 305 us -> none  [backward(): grad_rows.at[columns].add(spread.reshape(per_group * owned_len, channels))]
    dot_general x69 -> x0, matrix products: 125 us -> none  [the longest x33 47.4 us: gather_block_product(): jnp.dot(data, selector, preferred_element_type=jnp.float32, precision=lax...]
    pallas_call x0 -> x6, Pallas kernels: none -> 81.1 us  [the longest x1 40 us: forward_pass(): pl.pallas_call(forward_kernel, grid=(V // VB,), in_specs=[whole(GROUPS, C...]
    reduce_scatter x1 -> x0, waiting for transfers between devices: 79.8 us -> none  [body(): lax.psum_scatter(contrib.astype(jnp.bfloat16), 'sx', scatter_dimension=1,...]
    select_n x29 -> x0, other arithmetic: 74.9 us -> none  [the longest x9 39.3 us: forward(): jnp.take(table_rows, columns, axis=0)]
    all_gather x1 -> x0, waiting for transfers between devices: 35.7 us -> none  [body(): lax.all_gather(local_points, 'sx', axis=1, tiled=True)]
    reshape x10 -> x1, local copies, waits for them, and re-layouts: 30.5 us -> 1.09 us  [body(): weight_rows = jnp.transpose(weight, (1, 0, 2)).reshape(C, K * C)]
  transfers between devices with their start and end apart: 7 -> 5, of which waited for: 5 -> 3; matrix products, arithmetic and copies ran while one was open for 5% -> 1% of each run, Pallas kernels for 0% -> 11%
where the time goes in v1:
time: 346 us; the launch traced here: 345 us
  waiting for transfers between devices  201 us (58%)
  Pallas kernels  81.1 us (23%)
  blocking collectives  27.5 us (8%)
  between operations  14.1 us (4%)
  starting transfers between devices  12.1 us (3%)
  local copies, waits for them, and re-layouts  6.61 us (2%)
    psum x1, waiting for transfers between devices, body(): lax.psum(weight_part, ('sx', 'sy')) * (1.0 / math.sqrt(GROUPS * side * V))  196 us
    pallas_call x1, Pallas kernels, forward_pass(): pl.pallas_call(forward_kernel, grid=(V // VB,), in_specs=[whole(GROUPS, C...  40 us
    pallas_call x1, Pallas kernels, scatter_pass(): pl.pallas_call(scatter_kernel, grid=(V // VB,), in_specs=[pl.BlockSpec((K...  36.9 us
    all_to_all x1, blocking collectives, body(): owned = lax.all_to_all(outgoing, 'sx', 0, 0, tiled=True)  16.6 us
    all_to_all x1, blocking collectives, body(): returned = lax.all_to_all(owned_grad, 'sx', 0, 0, tiled=True)  11 us
  transfers between devices with their start and end apart: 5, of which 3 were waited for; matrix products, arithmetic and copies ran while one was open for 1% of the time, Pallas kernels for 11%

profile of v1, /device:TPU:1, one launch (start us, length us, event | category | flops | bytes accessed | tf_op | source)
XLA Modules:
  0.0 345.0 jit_solution(5662514576544725098)
XLA Ops:
  7.2 0.0 all-reduce.2.cloned.1.call-start
  7.2 0.0 copy-start.2
  7.2 0.9 copy-done.2
  8.1 0.0 copy-start.3
  8.1 0.7 copy-done.3
  8.8 0.0 copy-start.7
  8.8 1.6 place.1
  10.5 16.6 %all_to_all.10.owned_ref = bf16[16,96,128]{2,1,0:T(8,128)(2,1)S(1)} all-to-all(bf16[16,96,128]{2,1,0:T(8,128)(2,1)S(1)} %get-tuple-element.13), channel_id=1, replica_groups=mesh['sx'=16,'sy'=16] {'sx'}, dimensions={0} | all-to-all | bytes 786432 | tf_op jit(solution)/shard_map/all_to_all | solution.py:268
  27.0 0.0 copy-start
  27.0 0.0 copy-start.5
  27.0 0.7 copy-done.5
  27.7 0.6 faces.1
  28.3 5.3 %collective-permute-start = (bf16[96,256]{1,0:T(8,128)(2,1)S(1)}, bf16[96,256]{1,0:T(8,128)(2,1)S(1)}, u32[]{:S(2)}, u32[]{:S(2)}) collective-permute-start(bf16[96,256]{1,0:T(8,128)(2,1)S(1)} %get-tuple-element.14), channel_id=1, source_target_pairs={{0,1},{1,2},{2,3},{3,4},{4,5},{5,6},{6,7},{7,8},{8,9},{9,10},{10,1... | collective-permute-start | bytes 147464 | tf_op jit(solution)/shard_map/ppermute | solution.py:270
  33.6 1.9 collective-permute-start.1
  35.5 0.0 copy-done.7
  35.5 0.3 copy.11
  35.9 1.1 copy.12.weight_ref
  37.0 0.0 copy-done
  37.0 1.1 copy.13
  38.1 0.0 collective-permute-done.low_ref
  38.1 0.0 copy-start.8
  38.1 0.9 collective-permute-done.1.high_ref
  39.0 0.0 copy-start.9
  39.0 0.0 copy-done.8
  39.0 0.6 copy-done.9
  39.6 40.0 %gather_forward.1 = (bf16[96,2048]{1,0:T(8,128)(2,1)}, bf16[96,2048]{1,0:T(8,128)(2,1)}, f32[27,96,96]{2,1,0:T(8,128)}) custom-call(bf16[16,96,128]{2,1,0:T(8,128)(2,1)} %copy-done, bf16[96,256]{1,0:T(8,128)(2,1)} %copy-done.8, bf16[96,256]{1,0:T(8,128)(2,1)} %copy-done.9, s32[27,1,2048]{2,1,0:T(1,128)} %bitcast.22, bf16[96,2592]{1,0:T(8,128)(2,1)} %copy.12.weight_ref, ...), custom_call_target="tpu_custom_call" | custom-call | flops 27179089920 | bytes 4194304 | tf_op jit(solution)/shard_map/gather_forward/pallas_call | solution.py:137
  79.6 0.0 all-reduce.2.cloned.1.call-update
  79.7 0.0 copy-start.6
  79.7 36.9 %scatter_backward.1 = (f32[768,256]{1,0:T(8,128)}, bf16[96,256]{1,0:T(8,128)(2,1)}, bf16[96,256]{1,0:T(8,128)(2,1)}) custom-call(s32[27,1,2048]{2,1,0:T(1,128)} %bitcast.23, bf16[2592,96]{1,0:T(8,128)(2,1)} %bitcast.19, bf16[96,2048]{1,0:T(8,128)(2,1)} %get-tuple-element.17.pre_ref), custom_call_target="tpu_custom_call" | custom-call | flops 27179089920 | bytes 2097152 | tf_op jit(solution)/shard_map/scatter_backward/pallas_call | solution.py:196
  116.5 0.0 copy-start.4
  116.5 2.9 collective-permute-start.2
  119.4 1.9 collective-permute-start.3
  121.3 0.0 collective-permute-done.2.from_low_ref
  121.4 4.1 %collective-permute-done.3.from_high_ref = bf16[96,256]{1,0:T(8,128)(2,1)S(1)} collective-permute-done((bf16[96,256]{1,0:T(8,128)(2,1)}, bf16[96,256]{1,0:T(8,128)(2,1)S(1)}, u32[]{:S(2)}, u32[]{:S(2)}) %collective-permute-start.3) | collective-permute-done | bytes 49184 | tf_op jit(solution)/shard_map/ppermute | solution.py:280
  125.5 0.0 copy-done.6
  125.5 0.0 copy-start.1
  125.5 1.1 copy-done.1
  126.6 0.4 fold.1
  127.1 11.0 %all_to_all.11.back_ref = bf16[16,96,128]{2,1,0:T(8,128)(2,1)S(1)} all-to-all(bf16[16,96,128]{2,1,0:T(8,128)(2,1)S(1)} %fold.1), channel_id=1, replica_groups=mesh['sx'=16,'sy'=16] {'sx'}, dimensions={0} | all-to-all | bytes 786432 | tf_op jit(solution)/shard_map/all_to_all | solution.py:282
  138.0 0.0 copy-done.4
  138.0 1.6 take_back.1
  139.7 196.0 %all-reduce.2.cloned.1.call-done = f32[27,96,96]{2,1,0:T(8,128)} async-done(((f32[27,96,96]{2,1,0:T(8,128)}), f32[27,96,96]{2,1,0:T(8,128)}) %all-reduce.2.cloned.1.call-update) | async-done | bytes 995344 | tf_op jit(solution)/shard_map/psum | solution.py:276
  335.7 2.5 broadcast_multiply_fusion
Async XLA Ops:
  7.2 328.5 %all-reduce.2.cloned.1.call-start = ((), (), s32[]{:S(2)}) async-start(), calls=%async_computation.2 | async-start | bytes 2654208 | tf_op jit(solution)/shard_map/psum | solution.py:276
  7.2 0.9 copy-start.2
  8.1 0.7 copy-start.3
  8.8 26.7 %copy-start.7 = (bf16[27,96,96]{2,1,0:T(8,128)(2,1)S(1)}, bf16[27,96,96]{2,1,0:T(8,128)(2,1)}, u32[]{:S(2)}) copy-start(bf16[27,96,96]{2,1,0:T(8,128)(2,1)} %param.10) | copy-start | bytes 1492996
  27.0 9.9 %copy-start = (bf16[16,96,128]{2,1,0:T(8,128)(2,1)}, bf16[16,96,128]{2,1,0:T(8,128)(2,1)S(1)}, u32[]{:S(2)}) copy-start(bf16[16,96,128]{2,1,0:T(8,128)(2,1)S(1)} %all_to_all.10.owned_ref) | copy-start | bytes 1179652
  27.0 0.7 copy-start.5
  28.3 9.8 %collective-permute-start = (bf16[96,256]{1,0:T(8,128)(2,1)S(1)}, bf16[96,256]{1,0:T(8,128)(2,1)S(1)}, u32[]{:S(2)}, u32[]{:S(2)}) collective-permute-start(bf16[96,256]{1,0:T(8,128)(2,1)S(1)} %get-tuple-element.14), channel_id=1, source_target_pairs={{0,1},{1,2},{2,3},{3,4},{4,5},{5,6},{6,7},{7,8},{8,9},{9,10},{10,1... | collective-permute-start | bytes 147464 | tf_op jit(solution)/shard_map/ppermute | solution.py:270
  33.6 5.4 %collective-permute-start.1 = (bf16[96,256]{1,0:T(8,128)(2,1)S(1)}, bf16[96,256]{1,0:T(8,128)(2,1)S(1)}, u32[]{:S(2)}, u32[]{:S(2)}) collective-permute-start(bf16[96,256]{1,0:T(8,128)(2,1)S(1)} %get-tuple-element.15), channel_id=1, source_target_pairs={{1,0},{2,1},{3,2},{4,3},{5,4},{6,5},{7,6},{8,7},{9,8},{10,9},{11,1... | collective-permute-start | bytes 147464 | tf_op jit(solution)/shard_map/ppermute | solution.py:271
  38.1 0.9 copy-start.8
  39.0 0.6 copy-start.9
  79.7 45.8 %copy-start.6 = (s32[1,1,2,256]{3,2,1,0:T(2,128)S(1)}, s32[1,1,2,256]{3,2,1,0:T(2,128)}, u32[]{:S(2)}) copy-start(s32[1,1,2,256]{3,2,1,0:T(2,128)} %param.9) | copy-start | bytes 6148
  116.5 21.5 %copy-start.4 = (s32[1,1,1024,1]{2,3,1,0:T(1,128)S(1)}, s32[1,1,1024,1]{2,3,1,0:T(1,128)}, u32[]{:S(2)}) copy-start(s32[1,1,1024,1]{2,3,1,0:T(1,128)} %param.7) | copy-start | bytes 12292
  116.5 4.8 %collective-permute-start.2 = (bf16[96,256]{1,0:T(8,128)(2,1)}, bf16[96,256]{1,0:T(8,128)(2,1)S(1)}, u32[]{:S(2)}, u32[]{:S(2)}) collective-permute-start(bf16[96,256]{1,0:T(8,128)(2,1)} %get-tuple-element.19), channel_id=1, source_target_pairs={{0,1},{1,2},{2,3},{3,4},{4,5},{5,6},{6,7},{7,8},{8,9},{9,10},{10,1... | collective-permute-start | bytes 147464 | tf_op jit(solution)/shard_map/ppermute | solution.py:279
  119.4 6.1 %collective-permute-start.3 = (bf16[96,256]{1,0:T(8,128)(2,1)}, bf16[96,256]{1,0:T(8,128)(2,1)S(1)}, u32[]{:S(2)}, u32[]{:S(2)}) collective-permute-start(bf16[96,256]{1,0:T(8,128)(2,1)} %get-tuple-element.20), channel_id=1, source_target_pairs={{1,0},{2,1},{3,2},{4,3},{5,4},{6,5},{7,6},{8,7},{9,8},{10,9},{11,1... | collective-permute-start | bytes 147464 | tf_op jit(solution)/shard_map/ppermute | solution.py:280
  125.5 1.1 copy-start.1
Sparse Core Ops, SparseCore 0:
  79.8 255.8 all-reduce.1

commit v2 on v1

--- a/solution.py
+++ b/solution.py
@@ -1,3 +1,4 @@
+import functools
 import math
 
 import jax
@@ -17,17 +18,28 @@
 LO = 256
 BANKS = V // LO
 ALL_BANKS = BANKS + 2
+WIDE = 512
+WIDE_BANKS = ALL_BANKS * LO // WIDE
 VB = 256
-PER_DOT = 3
+PER_DOT = 9
+PARTS = (4, 3, 1)
+LANES = 128
+TILES = K * C // LANES
+SLOTS = C // 8 * TILES // GROUPS
 
 BF = jnp.bfloat16
 F32 = jnp.float32
 NT = (((1,), (1,)), ((), ()))
 
 
+def rows16(index):
+    return jnp.broadcast_to(index, (16, index.shape[-1])).astype(jnp.int16)
+
+
 def onehot_rows(low, rows):
-    row = lax.broadcasted_iota(jnp.int32, (rows, low.shape[-1]), 0)
-    return jnp.where(row == low, 1.0, 0.0).astype(BF)
+    n = low.shape[-1]
+    row = lax.broadcasted_iota(jnp.int16, (rows, n), 0).reshape(rows // 16, 16, n)
+    return jnp.where(row == rows16(low)[None], BF(1), BF(0)).reshape(rows, n)
 
 
 def select_banks(product, bank, banks):
@@ -42,9 +54,10 @@
 
 def masked_banks(values, bank, banks, out_ref, column):
     n = bank.shape[-1]
+    bank16 = rows16(bank)
+    values = values.reshape(C // 16, 16, n)
     for a in range(banks):
-        mask = jnp.where(jnp.broadcast_to(bank, (16, n)) == a, 1.0, 0.0).astype(BF)
-        spread = values.reshape(C // 16, 16, n) * mask[None]
+        spread = jnp.where((bank16 == a)[None], values, BF(0))
         out_ref[a * C : (a + 1) * C, column : column + n] = spread.reshape(C, n)
 
 
@@ -106,17 +119,18 @@
 
     @pl.when(step == 0)
     def _():
+        per = WIDE // CAP
         for g in range(GROUPS):
-            table_ref[(g // 2) * C : (g // 2 + 1) * C, (g % 2) * CAP : (g % 2 + 1) * CAP] = owned_ref[g]
-        table_ref[BANKS * C : (BANKS + 1) * C, :] = low_ref[...]
-        table_ref[(BANKS + 1) * C :, :] = high_ref[...]
+            table_ref[(g // per) * C : (g // per + 1) * C, (g % per) * CAP : (g % per + 1) * CAP] = owned_ref[g]
+        table_ref[(WIDE_BANKS - 1) * C :, :F] = low_ref[...]
+        table_ref[(WIDE_BANKS - 1) * C :, F:] = high_ref[...]
         acc_ref[...] = jnp.zeros_like(acc_ref)
 
     table = table_ref[...]
     for k in range(K):
         index = map_ref[k]
-        product = jnp.dot(table, onehot_rows(index & (LO - 1), LO), preferred_element_type=F32)
-        picked_ref[k * C : (k + 1) * C, :] = select_banks(product, index >> 8, ALL_BANKS).astype(BF)
+        product = jnp.dot(table, onehot_rows(index & (WIDE - 1), WIDE), preferred_element_type=F32)
+        picked_ref[k * C : (k + 1) * C, :] = select_banks(product, index >> 9, WIDE_BANKS).astype(BF)
     preact = jnp.dot(weight_ref[...], picked_ref[...], preferred_element_type=F32)
     logistic = jax.nn.sigmoid(preact)
     out_ref[...] = (preact * logistic).astype(BF)
@@ -127,8 +141,16 @@
 
     @pl.when(step == pl.num_programs(0) - 1)
     def _():
-        for k in range(K):
-            wg_ref[k] = acc_ref[k * C : (k + 1) * C, :].T
+        for t in range(TILES):
+            block = acc_ref[t * LANES : (t + 1) * LANES, :].T
+            for i in range(C // 8):
+                shard, slot = divmod(i * TILES + t, SLOTS)
+                wg_ref[shard, slot * 8 : (slot + 1) * 8, :] = block[i * 8 : (i + 1) * 8, :]
+        rest = acc_ref[TILES * LANES :, :].T
+        rest = jnp.concatenate([rest, jnp.zeros((C, LANES - rest.shape[1]), F32)], axis=1)
+        for g in range(GROUPS):
+            tail = rest[g * 8 : (g + 1) * 8, :] if g < C // 8 else jnp.zeros((8, LANES), F32)
+            wg_ref[g, SLOTS * 8 :, :] = tail
 
 
 def forward_pass(owned, low, high, kernel_map, weight, cotangent):
@@ -145,14 +167,14 @@
             whole(C, K * C),
             column(C),
         ],
-        out_specs=(column(C), column(C), whole(K, C, C)),
+        out_specs=(column(C), column(C), whole(GROUPS, LANES, LANES)),
         out_shape=(
             jax.ShapeDtypeStruct((C, V), BF),
             jax.ShapeDtypeStruct((C, V), BF),
-            jax.ShapeDtypeStruct((K, C, C), F32),
+            jax.ShapeDtypeStruct((GROUPS, LANES, LANES), F32),
         ),
         scratch_shapes=[
-            pltpu.VMEM((ALL_BANKS * C, LO), BF),
+            pltpu.VMEM((WIDE_BANKS * C, WIDE), BF),
             pltpu.VMEM((K * C, VB), BF),
             pltpu.VMEM((K * C, C), F32),
         ],
@@ -164,13 +186,7 @@
     )(owned, low, high, kernel_map, weight, cotangent)
 
 
-def scatter_kernel(map_ref, weight_ref, pre_ref, own_ref, low_ref, high_ref, spread_ref, masked_ref, acc_ref):
-    step = pl.program_id(0)
-
-    @pl.when(step == 0)
-    def _():
-        acc_ref[...] = jnp.zeros_like(acc_ref)
-
+def scatter_step(map_ref, weight_ref, pre_ref, acc_ref, spread_ref, masked_ref):
     spread_ref[...] = jnp.dot(weight_ref[...], pre_ref[...], preferred_element_type=F32).astype(BF)
     for first in range(0, K, PER_DOT):
         hots = []
@@ -183,37 +199,64 @@
             masked_ref[...], jnp.concatenate(hots, axis=1), NT, preferred_element_type=F32
         )
 
-    @pl.when(step == pl.num_programs(0) - 1)
+
+def scatter_kernel(
+    has_start, has_faces, after_ref, start_ref, map_ref, weight_ref, pre_ref, *refs
+):
+    if has_faces:
+        own_ref, low_ref, high_ref, spread_ref, masked_ref, acc_ref = refs
+    else:
+        acc_ref, spread_ref, masked_ref = refs
+
+    @pl.when(pl.program_id(0) == 0)
     def _():
-        own_ref[...] = acc_ref[: BANKS * C, :]
-        low_ref[...] = acc_ref[BANKS * C : (BANKS + 1) * C, :].astype(BF)
-        high_ref[...] = acc_ref[(BANKS + 1) * C :, :].astype(BF)
-
-
-def scatter_pass(kernel_map, weight, grad_pre):
+        acc_ref[...] = start_ref[...] if has_start else jnp.zeros_like(acc_ref)
+
+    scatter_step(map_ref, weight_ref, pre_ref, acc_ref, spread_ref, masked_ref)
+
+    if has_faces:
+
+        @pl.when(pl.program_id(0) == pl.num_programs(0) - 1)
+        def _():
+            own_ref[...] = acc_ref[: BANKS * C, :]
+            low_ref[...] = acc_ref[BANKS * C : (BANKS + 1) * C, :].astype(BF)
+            high_ref[...] = acc_ref[(BANKS + 1) * C :, :].astype(BF)
+
+
+def scatter_part(part, after, start, kernel_map, weight, grad_pre):
     whole = lambda *shape: pl.BlockSpec(shape, lambda i: (0,) * len(shape))
-    column = lambda rows: pl.BlockSpec((rows, VB), lambda i: (0, i))
-    return pl.pallas_call(
-        scatter_kernel,
-        grid=(V // VB,),
-        in_specs=[pl.BlockSpec((K, 1, VB), lambda i: (0, 0, i)), whole(K * C, C), column(C)],
-        out_specs=(whole(BANKS * C, LO), whole(C, F), whole(C, F)),
-        out_shape=(
+    sums = jax.ShapeDtypeStruct((ALL_BANKS * C, LO), F32)
+    scratch = [pltpu.VMEM((K * C, VB), BF), pltpu.VMEM((ALL_BANKS * C, PER_DOT * VB), BF)]
+    at, steps, last = sum(PARTS[:part]), PARTS[part], part == len(PARTS) - 1
+    if last:
+        out_specs = (whole(BANKS * C, LO), whole(C, F), whole(C, F))
+        out_shape = (
             jax.ShapeDtypeStruct((BANKS * C, LO), F32),
             jax.ShapeDtypeStruct((C, F), BF),
             jax.ShapeDtypeStruct((C, F), BF),
-        ),
-        scratch_shapes=[
-            pltpu.VMEM((K * C, VB), BF),
-            pltpu.VMEM((ALL_BANKS * C, PER_DOT * VB), BF),
-            pltpu.VMEM((ALL_BANKS * C, LO), F32),
+        )
+        scratch.append(pltpu.VMEM(sums.shape, F32))
+    else:
+        out_specs, out_shape = whole(*sums.shape), sums
+    return pl.pallas_call(
+        functools.partial(scatter_kernel, part > 0, last),
+        grid=(steps,),
+        in_specs=[
+            pl.BlockSpec(memory_space=pl.ANY),
+            whole(*sums.shape) if part > 0 else pl.BlockSpec(memory_space=pl.ANY),
+            pl.BlockSpec((K, 1, VB), lambda i: (0, 0, at + i)),
+            whole(K * C, C),
+            pl.BlockSpec((C, VB), lambda i: (0, at + i)),
         ],
+        out_specs=out_specs,
+        out_shape=out_shape,
+        scratch_shapes=scratch,
         compiler_params=pltpu.CompilerParams(vmem_limit_bytes=56 << 20),
         cost_estimate=pl.CostEstimate(
-            flops=2 * K * V * ALL_BANKS * C * LO, bytes_accessed=2 << 20, transcendentals=0
+            flops=2 * K * VB * steps * ALL_BANKS * C * LO, bytes_accessed=2 << 20, transcendentals=0
         ),
-        name="scatter_backward",
-    )(kernel_map, weight, grad_pre)
+        name="scatter",
+    )(after, start, kernel_map, weight, grad_pre)
 
 
 def fold_kernel(grad_ref, from_low_ref, from_high_ref, rows_ref, out_ref, masked_ref):
@@ -257,6 +300,28 @@
     )(returned, owner, slot)
 
 
+def unpack_kernel(scale, parts_ref, out_ref, flat_ref):
+    for g in range(GROUPS):
+        block = parts_ref[g] * scale
+        for slot in range(SLOTS):
+            i, t = divmod(g * SLOTS + slot, TILES)
+            flat_ref[i * 8 : (i + 1) * 8, t * LANES : (t + 1) * LANES] = block[slot * 8 : (slot + 1) * 8, :]
+        if g < C // 8:
+            flat_ref[g * 8 : (g + 1) * 8, TILES * LANES :] = block[SLOTS * 8 :, :]
+    for k in range(K):
+        out_ref[k] = flat_ref[:, k * C : (k + 1) * C]
+
+
+def unpack_weight(parts, scale):
+    return pl.pallas_call(
+        functools.partial(unpack_kernel, scale),
+        out_shape=jax.ShapeDtypeStruct((K, C, C), F32),
+        scratch_shapes=[pltpu.VMEM((C, (TILES + 1) * LANES), F32)],
+        compiler_params=pltpu.CompilerParams(vmem_limit_bytes=32 << 20),
+        name="unpack",
+    )(parts)
+
+
 def body(points, owners, kernel_maps, face_rows, weight, cotangent):
     points, owner = points[0, 0], owners.reshape(1, R)
     kernel_map, face_list, incoming = kernel_maps.reshape(K, 1, V), face_rows[0, 0], cotangent[0, 0]
@@ -273,14 +338,20 @@
     output, grad_pre, weight_part = forward_pass(
         owned, ghost_low, ghost_high, kernel_map, weight_rows, incoming
     )
-    weight_grad = lax.psum(weight_part, ("sx", "sy")) * (1.0 / math.sqrt(GROUPS * side * V))
     weight_columns = jnp.transpose(weight, (0, 2, 1)).reshape(K * C, C)
-    table_grad, to_low, to_high = scatter_pass(kernel_map, weight_columns, grad_pre)
+    scatter = functools.partial(scatter_part, kernel_map=kernel_map, weight=weight_columns, grad_pre=grad_pre)
+    row_sum = lax.psum_scatter(weight_part, "sx", scatter_dimension=0, tiled=False)
+    sums = scatter(0, grad_pre, grad_pre)
+    share = lax.psum(row_sum, "sy")
+    sums = scatter(1, row_sum, sums)
+    parts = lax.all_gather(share, "sx", axis=0)
+    table_grad, to_low, to_high = scatter(2, share, sums)
     from_low = lax.ppermute(to_high, "sy", up)
     from_high = lax.ppermute(to_low, "sy", down)
     owned_grad = fold_faces(table_grad, from_low, from_high, face_list)
     returned = lax.all_to_all(owned_grad, "sx", 0, 0, tiled=True)
     point_grad = take_back(returned, owner, slot)
+    weight_grad = unpack_weight(parts, 1.0 / math.sqrt(GROUPS * side * V))
     return (output[None, None], point_grad[None, None], weight_grad)
 
 

time: 346 us -> 331 us (0.957)
  waiting for transfers between devices: 201 us -> 179 us
  Pallas kernels: 81.1 us -> 86 us
  blocking collectives: 27.5 us -> 31.7 us
    psum x1, waiting for transfers between devices: 196 us -> 103 us  [body(): share = lax.psum(row_sum, 'sy')]
    unnamed x1 -> x4, waiting for transfers between devices: 0.02 us -> 55.1 us
    all_gather x0 -> x1, waiting for transfers between devices: none -> 15.1 us  [body(): parts = lax.all_gather(share, 'sx', axis=0)]
    pallas_call x1 -> x4, Pallas kernels: 36.9 us -> 43.1 us  [the longest x3 41.5 us: scatter_part(): pl.pallas_call(functools.partial(scatter_kernel, part > 0, last), grid=(s...]
    all_to_all x1, blocking collectives: 11 us -> 15.2 us  [body(): returned = lax.all_to_all(owned_grad, 'sx', 0, 0, tiled=True)]
  transfers between devices with their start and end apart: 5 -> 7, of which waited for: 3 -> 5; matrix products, arithmetic and copies ran while one was open for 1% -> 1% of each run, Pallas kernels for 11% -> 9%
where the time goes in v2:
time: 331 us; the launch traced here: 330 us
  waiting for transfers between devices  179 us (54%)
  Pallas kernels  86 us (26%)
  blocking collectives  31.7 us (10%)
  between operations  13.8 us (4%)
  starting transfers between devices  12 us (4%)
  local copies, waits for them, and re-layouts  7.83 us (2%)
    psum x1, waiting for transfers between devices, body(): share = lax.psum(row_sum, 'sy')  103 us
    unnamed x4, waiting for transfers between devices  55.1 us
    pallas_call x3, Pallas kernels, scatter_part(): pl.pallas_call(functools.partial(scatter_kernel, part > 0, last), grid=(s...  41.5 us
    pallas_call x1, Pallas kernels, forward_pass(): pl.pallas_call(forward_kernel, grid=(V // VB,), in_specs=[whole(GROUPS, C...  38.7 us
    all_to_all x1, blocking collectives, body(): owned = lax.all_to_all(outgoing, 'sx', 0, 0, tiled=True)  16.6 us
    all_to_all x1, blocking collectives, body(): returned = lax.all_to_all(owned_grad, 'sx', 0, 0, tiled=True)  15.2 us
    all_gather x1, waiting for transfers between devices, body(): parts = lax.all_gather(share, 'sx', axis=0)  15.1 us
  transfers between devices with their start and end apart: 7, of which 5 were waited for; matrix products, arithmetic and copies ran while one was open for 1% of the time, Pallas kernels for 9%

profile of v2, /device:TPU:1, one launch (start us, length us, event | category | flops | bytes accessed | tf_op | source)
XLA Modules:
  0.0 330.0 jit_solution(79054914024067774)
XLA Ops:
  7.2 0.0 reduce-scatter.4.cloned.1.call-start
  7.2 0.0 copy-start.3
  7.2 0.9 copy-done.3
  8.1 0.0 copy-start.4
  8.1 0.7 copy-done.4
  8.8 0.0 copy-start.8
  8.8 1.6 place.1
  10.5 16.6 %all_to_all.10.owned_ref = bf16[16,96,128]{2,1,0:T(8,128)(2,1)S(1)} all-to-all(bf16[16,96,128]{2,1,0:T(8,128)(2,1)S(1)} %get-tuple-element.13), channel_id=1, replica_groups=mesh['sx'=16,'sy'=16] {'sx'}, dimensions={0} | all-to-all | bytes 786432 | tf_op jit(solution)/shard_map/all_to_all | solution.py:333
  27.0 0.0 copy-start
  27.0 0.0 copy-start.6
  27.0 0.7 copy-done.6
  27.7 0.6 faces.1
  28.3 5.3 %collective-permute-start = (bf16[96,256]{1,0:T(8,128)(2,1)S(1)}, bf16[96,256]{1,0:T(8,128)(2,1)S(1)}, u32[]{:S(2)}, u32[]{:S(2)}) collective-permute-start(bf16[96,256]{1,0:T(8,128)(2,1)S(1)} %get-tuple-element.14), channel_id=1, source_target_pairs={{0,1},{1,2},{2,3},{3,4},{4,5},{5,6},{6,7},{7,8},{8,9},{9,10},{10,1... | collective-permute-start | bytes 147464 | tf_op jit(solution)/shard_map/ppermute | solution.py:335
  33.6 1.9 collective-permute-start.1
  35.5 0.0 copy-done.8
  35.5 0.3 copy.14
  35.8 1.1 copy.15.weight_ref
  36.9 0.0 copy-done
  36.9 0.0 collective-permute-done.low_ref
  36.9 2.0 collective-permute-done.1.high_ref
  39.0 0.0 copy-done.9
  39.0 0.6 copy-done.10
  39.6 38.7 %gather_forward.1 = (bf16[96,2048]{1,0:T(8,128)(2,1)}, bf16[96,2048]{1,0:T(8,128)(2,1)}, f32[16,128,128]{2,1,0:T(8,128)}) custom-call(bf16[16,96,128]{2,1,0:T(8,128)(2,1)} %copy-done, bf16[96,256]{1,0:T(8,128)(2,1)} %copy-done.9, bf16[96,256]{1,0:T(8,128)(2,1)} %copy-done.10, s32[27,1,2048]{2,1,0:T(1,128)} %bitcast.30, bf16[96,2592]{1,0:T(8,128)(2,1)} %copy.15.weight_ref, ...), custom_call_target="tpu_custom_call" | custom-call | flops 27179089920 | bytes 4194304 | tf_op jit(solution)/shard_map/gather_forward/pallas_call | solution.py:159
  78.3 0.0 reduce-scatter.4.cloned.1.call-update
  78.3 1.1 copy.16
  79.5 19.5 %scatter.3.start_ref = f32[960,256]{1,0:T(8,128)} custom-call(bf16[96,2048]{1,0:T(8,128)(2,1)} %get-tuple-element.18.after_ref.start_ref.pre_ref, bf16[96,2048]{1,0:T(8,128)(2,1)} %get-tuple-element.18.after_ref.start_ref.pre_ref, s32[27,1,2048]{2,1,0:T(1,128)} %bitcast.31, bf16[2592,96]{1,0:T(8,128)(2,1)} %bitcast.23, ...), custom_call_target="tpu_custom_call" | custom-call | flops 13589544960 | bytes 2097152 | tf_op jit(solution)/shard_map/scatter/pallas_call | solution.py:241
  99.0 54.3 %reduce-scatter.4.cloned.1.call-done = f32[1,128,128]{2,1,0:T(8,128)} async-done(((f32[16,128,128]{2,1,0:T(8,128)}), f32[1,128,128]{2,1,0:T(8,128)}) %reduce-scatter.4.cloned.1.call-update) | async-done | bytes 65552
  153.3 15.4 %scatter.4.start_ref = f32[960,256]{1,0:T(8,128)} custom-call(f32[128,128]{1,0:T(8,128)} %bitcast.27, f32[960,256]{1,0:T(8,128)} %scatter.3.start_ref, s32[27,1,2048]{2,1,0:T(1,128)} %bitcast.32, bf16[2592,96]{1,0:T(8,128)(2,1)} %bitcast.24, bf16[96,2048]{1,0:T(8,128)(2,1)} %get-tuple-element.18.after_ref.start_ref.pre_ref), custom_call_target="tpu_custom_call" | custom-call | flops 10192158720 | bytes 2097152 | tf_op jit(solution)/shard_map/scatter/pallas_call | solution.py:241
  168.7 0.0 all-reduce.3.cloned.1.call-start
  168.7 0.7 all-reduce.3.cloned.1.call-update
  169.5 0.3 all-gather.3.cloned.1.call-start
  169.7 102.6 %all-reduce.3.cloned.1.call-done.after_ref = f32[128,128]{1,0:T(8,128)} async-done(((f32[128,128]{1,0:T(8,128)}), f32[128,128]{1,0:T(8,128)}) %all-reduce.3.cloned.1.call-update) | async-done | bytes 65552 | tf_op jit(solution)/shard_map/psum | solution.py:345
  272.4 0.0 all-gather.3.cloned.1.call-update
  272.4 0.0 copy-start.7
  272.4 6.6 %scatter.5 = (f32[768,256]{1,0:T(8,128)}, bf16[96,256]{1,0:T(8,128)(2,1)}, bf16[96,256]{1,0:T(8,128)(2,1)}) custom-call(f32[128,128]{1,0:T(8,128)} %all-reduce.3.cloned.1.call-done.after_ref, f32[960,256]{1,0:T(8,128)} %scatter.4.start_ref, s32[27,1,2048]{2,1,0:T(1,128)} %bitcast.33, bf16[2592,96]{1,0:T(8,128)(2,1)} %bitcast.25, ...), custom_call_target="tpu_custom_call" | custom-call | flops 3397386240 | bytes 2097152 | tf_op jit(solution)/shard_map/scatter/pallas_call | solution.py:241
  279.0 2.6 collective-permute-start.2
  281.6 1.9 collective-permute-start.3
  283.5 0.0 collective-permute-done.2.from_low_ref
  283.6 3.7 %collective-permute-done.3.from_high_ref = bf16[96,256]{1,0:T(8,128)(2,1)S(1)} collective-permute-done((bf16[96,256]{1,0:T(8,128)(2,1)}, bf16[96,256]{1,0:T(8,128)(2,1)S(1)}, u32[]{:S(2)}, u32[]{:S(2)}) %collective-permute-start.3) | collective-permute-done | bytes 49184 | tf_op jit(solution)/shard_map/ppermute | solution.py:350
  287.2 0.0 copy-done.7
  287.2 1.1 copy-done.2
  288.4 0.4 fold.1
  288.8 15.2 %all_to_all.11.back_ref = bf16[16,96,128]{2,1,0:T(8,128)(2,1)S(1)} all-to-all(bf16[16,96,128]{2,1,0:T(8,128)(2,1)S(1)} %fold.1), channel_id=1, replica_groups=mesh['sx'=16,'sy'=16] {'sx'}, dimensions={0} | all-to-all | bytes 786432 | tf_op jit(solution)/shard_map/all_to_all | solution.py:352
  303.9 0.0 copy-done.5
  303.9 1.6 take_back.1
  305.6 15.1 %all-gather.3.cloned.1.call-done = f32[2048,128]{1,0:T(8,128)} async-done(((f32[128,128]{1,0:T(8,128)}), f32[2048,128]{1,0:T(8,128)}) %all-gather.3.cloned.1.call-update) | async-done | bytes 1048592 | tf_op jit(solution)/shard_map/all_gather | solution.py:347
  320.7 1.2 copy-done.1
  321.9 1.6 unpack.1
  (5 shorter events, 0.0 us)
Async XLA Ops:
  7.2 146.1 %reduce-scatter.4.cloned.1.call-start = ((), (), s32[]{:S(2)}) async-start(), calls=%async_computation.5 | async-start | bytes 1114112
  7.2 0.9 copy-start.3
  8.1 0.7 copy-start.4
  8.8 26.7 %copy-start.8 = (bf16[27,96,96]{2,1,0:T(8,128)(2,1)S(1)}, bf16[27,96,96]{2,1,0:T(8,128)(2,1)}, u32[]{:S(2)}) copy-start(bf16[27,96,96]{2,1,0:T(8,128)(2,1)} %param.10) | copy-start | bytes 1492996
  27.0 9.9 %copy-start = (bf16[16,96,128]{2,1,0:T(8,128)(2,1)}, bf16[16,96,128]{2,1,0:T(8,128)(2,1)S(1)}, u32[]{:S(2)}) copy-start(bf16[16,96,128]{2,1,0:T(8,128)(2,1)S(1)} %all_to_all.10.owned_ref) | copy-start | bytes 1179652
  27.0 0.7 copy-start.6
  28.3 8.7 %collective-permute-start = (bf16[96,256]{1,0:T(8,128)(2,1)S(1)}, bf16[96,256]{1,0:T(8,128)(2,1)S(1)}, u32[]{:S(2)}, u32[]{:S(2)}) collective-permute-start(bf16[96,256]{1,0:T(8,128)(2,1)S(1)} %get-tuple-element.14), channel_id=1, source_target_pairs={{0,1},{1,2},{2,3},{3,4},{4,5},{5,6},{6,7},{7,8},{8,9},{9,10},{10,1... | collective-permute-start | bytes 147464 | tf_op jit(solution)/shard_map/ppermute | solution.py:335
  33.6 5.4 %collective-permute-start.1 = (bf16[96,256]{1,0:T(8,128)(2,1)S(1)}, bf16[96,256]{1,0:T(8,128)(2,1)S(1)}, u32[]{:S(2)}, u32[]{:S(2)}) collective-permute-start(bf16[96,256]{1,0:T(8,128)(2,1)S(1)} %get-tuple-element.15), channel_id=1, source_target_pairs={{1,0},{2,1},{3,2},{4,3},{5,4},{6,5},{7,6},{8,7},{9,8},{10,9},{11,1... | collective-permute-start | bytes 147464 | tf_op jit(solution)/shard_map/ppermute | solution.py:336
  36.9 2.0 copy-start.9
  39.0 0.6 copy-start.10
  168.7 103.6 %all-reduce.3.cloned.1.call-start = ((), (), s32[]{:S(2)}) async-start(), calls=%async_computation.3 | async-start | bytes 131072 | tf_op jit(solution)/shard_map/psum | solution.py:345
  169.5 151.3 %all-gather.3.cloned.1.call-start = ((), (), s32[]{:S(2)}) async-start(), calls=%async_computation.4 | async-start | bytes 1114112 | tf_op jit(solution)/shard_map/all_gather | solution.py:347
  272.4 14.8 %copy-start.7 = (s32[1,1,2,256]{3,2,1,0:T(2,128)S(1)}, s32[1,1,2,256]{3,2,1,0:T(2,128)}, u32[]{:S(2)}) copy-start(s32[1,1,2,256]{3,2,1,0:T(2,128)} %param.9) | copy-start | bytes 6148
  279.0 25.0 %copy-start.5 = (s32[1,1,1024,1]{2,3,1,0:T(1,128)S(1)}, s32[1,1,1024,1]{2,3,1,0:T(1,128)}, u32[]{:S(2)}) copy-start(s32[1,1,1024,1]{2,3,1,0:T(1,128)} %param.7) | copy-start | bytes 12292
  279.0 4.6 %collective-permute-start.2 = (bf16[96,256]{1,0:T(8,128)(2,1)}, bf16[96,256]{1,0:T(8,128)(2,1)S(1)}, u32[]{:S(2)}, u32[]{:S(2)}) collective-permute-start(bf16[96,256]{1,0:T(8,128)(2,1)} %get-tuple-element.20), channel_id=1, source_target_pairs={{0,1},{1,2},{2,3},{3,4},{4,5},{5,6},{6,7},{7,8},{8,9},{9,10},{10,1... | collective-permute-start | bytes 147464 | tf_op jit(solution)/shard_map/ppermute | solution.py:349
  281.6 5.6 %collective-permute-start.3 = (bf16[96,256]{1,0:T(8,128)(2,1)}, bf16[96,256]{1,0:T(8,128)(2,1)S(1)}, u32[]{:S(2)}, u32[]{:S(2)}) collective-permute-start(bf16[96,256]{1,0:T(8,128)(2,1)} %get-tuple-element.21), channel_id=1, source_target_pairs={{1,0},{2,1},{3,2},{4,3},{5,4},{6,5},{7,6},{8,7},{9,8},{10,9},{11,1... | collective-permute-start | bytes 147464 | tf_op jit(solution)/shard_map/ppermute | solution.py:350
  287.2 1.1 copy-start.2
  320.7 1.2 copy-start.1
Sparse Core Ops, SparseCore 0:
  78.5 74.7 reduce-scatter.3
  172.0 100.3 all-reduce.2
  274.8 45.8 all-gather.2

commit v3 on v1

--- a/solution.py
+++ b/solution.py
@@ -17,6 +17,8 @@
 LO = 256
 BANKS = V // LO
 ALL_BANKS = BANKS + 2
+WIDE = 512
+WIDE_BANKS = ALL_BANKS * LO // WIDE
 VB = 256
 PER_DOT = 3
 
@@ -25,9 +27,14 @@
 NT = (((1,), (1,)), ((), ()))
 
 
+def rows16(index):
+    return jnp.broadcast_to(index, (16, index.shape[-1])).astype(jnp.int16)
+
+
 def onehot_rows(low, rows):
-    row = lax.broadcasted_iota(jnp.int32, (rows, low.shape[-1]), 0)
-    return jnp.where(row == low, 1.0, 0.0).astype(BF)
+    n = low.shape[-1]
+    row = lax.broadcasted_iota(jnp.int16, (rows, n), 0).reshape(rows // 16, 16, n)
+    return jnp.where(row == rows16(low)[None], BF(1), BF(0)).reshape(rows, n)
 
 
 def select_banks(product, bank, banks):
@@ -42,9 +49,10 @@
 
 def masked_banks(values, bank, banks, out_ref, column):
     n = bank.shape[-1]
+    bank16 = rows16(bank)
+    values = values.reshape(C // 16, 16, n)
     for a in range(banks):
-        mask = jnp.where(jnp.broadcast_to(bank, (16, n)) == a, 1.0, 0.0).astype(BF)
-        spread = values.reshape(C // 16, 16, n) * mask[None]
+        spread = jnp.where((bank16 == a)[None], values, BF(0))
         out_ref[a * C : (a + 1) * C, column : column + n] = spread.reshape(C, n)
 
 
@@ -77,7 +85,7 @@
             jax.ShapeDtypeStruct((1, R), jnp.int32),
         ),
         scratch_shapes=[pltpu.VMEM((GROUPS * C, R), BF)],
-        compiler_params=pltpu.CompilerParams(vmem_limit_bytes=48 << 20),
+        compiler_params=pltpu.CompilerParams(vmem_limit_bytes=16 << 20),
         name="place",
     )(points, owner)
 
@@ -94,7 +102,7 @@
     return pl.pallas_call(
         faces_kernel,
         out_shape=(jax.ShapeDtypeStruct((C, F), BF),) * 2,
-        compiler_params=pltpu.CompilerParams(vmem_limit_bytes=48 << 20),
+        compiler_params=pltpu.CompilerParams(vmem_limit_bytes=16 << 20),
         name="faces",
     )(owned, face_rows)
 
@@ -106,17 +114,18 @@
 
     @pl.when(step == 0)
     def _():
+        per = WIDE // CAP
         for g in range(GROUPS):
-            table_ref[(g // 2) * C : (g // 2 + 1) * C, (g % 2) * CAP : (g % 2 + 1) * CAP] = owned_ref[g]
-        table_ref[BANKS * C : (BANKS + 1) * C, :] = low_ref[...]
-        table_ref[(BANKS + 1) * C :, :] = high_ref[...]
+            table_ref[(g // per) * C : (g // per + 1) * C, (g % per) * CAP : (g % per + 1) * CAP] = owned_ref[g]
+        table_ref[(WIDE_BANKS - 1) * C :, :F] = low_ref[...]
+        table_ref[(WIDE_BANKS - 1) * C :, F:] = high_ref[...]
         acc_ref[...] = jnp.zeros_like(acc_ref)
 
     table = table_ref[...]
     for k in range(K):
         index = map_ref[k]
-        product = jnp.dot(table, onehot_rows(index & (LO - 1), LO), preferred_element_type=F32)
-        picked_ref[k * C : (k + 1) * C, :] = select_banks(product, index >> 8, ALL_BANKS).astype(BF)
+        product = jnp.dot(table, onehot_rows(index & (WIDE - 1), WIDE), preferred_element_type=F32)
+        picked_ref[k * C : (k + 1) * C, :] = select_banks(product, index >> 9, WIDE_BANKS).astype(BF)
     preact = jnp.dot(weight_ref[...], picked_ref[...], preferred_element_type=F32)
     logistic = jax.nn.sigmoid(preact)
     out_ref[...] = (preact * logistic).astype(BF)
@@ -152,11 +161,11 @@
             jax.ShapeDtypeStruct((K, C, C), F32),
         ),
         scratch_shapes=[
-            pltpu.VMEM((ALL_BANKS * C, LO), BF),
+            pltpu.VMEM((WIDE_BANKS * C, WIDE), BF),
             pltpu.VMEM((K * C, VB), BF),
             pltpu.VMEM((K * C, C), F32),
         ],
-        compiler_params=pltpu.CompilerParams(vmem_limit_bytes=56 << 20),
+        compiler_params=pltpu.CompilerParams(vmem_limit_bytes=20 << 20),
         cost_estimate=pl.CostEstimate(
             flops=2 * K * V * ALL_BANKS * C * LO, bytes_accessed=4 << 20, transcendentals=C * V
         ),
@@ -164,13 +173,7 @@
     )(owned, low, high, kernel_map, weight, cotangent)
 
 
-def scatter_kernel(map_ref, weight_ref, pre_ref, own_ref, low_ref, high_ref, spread_ref, masked_ref, acc_ref):
-    step = pl.program_id(0)
-
-    @pl.when(step == 0)
-    def _():
-        acc_ref[...] = jnp.zeros_like(acc_ref)
-
+def scatter_step(map_ref, weight_ref, pre_ref, acc_ref, spread_ref, masked_ref):
     spread_ref[...] = jnp.dot(weight_ref[...], pre_ref[...], preferred_element_type=F32).astype(BF)
     for first in range(0, K, PER_DOT):
         hots = []
@@ -183,7 +186,15 @@
             masked_ref[...], jnp.concatenate(hots, axis=1), NT, preferred_element_type=F32
         )
 
-    @pl.when(step == pl.num_programs(0) - 1)
+
+def scatter_kernel(map_ref, weight_ref, pre_ref, own_ref, low_ref, high_ref, spread_ref, masked_ref, acc_ref):
+    @pl.when(pl.program_id(0) == 0)
+    def _():
+        acc_ref[...] = jnp.zeros_like(acc_ref)
+
+    scatter_step(map_ref, weight_ref, pre_ref, acc_ref, spread_ref, masked_ref)
+
+    @pl.when(pl.program_id(0) == pl.num_programs(0) - 1)
     def _():
         own_ref[...] = acc_ref[: BANKS * C, :]
         low_ref[...] = acc_ref[BANKS * C : (BANKS + 1) * C, :].astype(BF)
@@ -192,11 +203,14 @@
 
 def scatter_pass(kernel_map, weight, grad_pre):
     whole = lambda *shape: pl.BlockSpec(shape, lambda i: (0,) * len(shape))
-    column = lambda rows: pl.BlockSpec((rows, VB), lambda i: (0, i))
     return pl.pallas_call(
         scatter_kernel,
         grid=(V // VB,),
-        in_specs=[pl.BlockSpec((K, 1, VB), lambda i: (0, 0, i)), whole(K * C, C), column(C)],
+        in_specs=[
+            pl.BlockSpec((K, 1, VB), lambda i: (0, 0, i)),
+            whole(K * C, C),
+            pl.BlockSpec((C, VB), lambda i: (0, i)),
+        ],
         out_specs=(whole(BANKS * C, LO), whole(C, F), whole(C, F)),
         out_shape=(
             jax.ShapeDtypeStruct((BANKS * C, LO), F32),
@@ -208,11 +222,11 @@
             pltpu.VMEM((ALL_BANKS * C, PER_DOT * VB), BF),
             pltpu.VMEM((ALL_BANKS * C, LO), F32),
         ],
-        compiler_params=pltpu.CompilerParams(vmem_limit_bytes=56 << 20),
+        compiler_params=pltpu.CompilerParams(vmem_limit_bytes=20 << 20),
         cost_estimate=pl.CostEstimate(
             flops=2 * K * V * ALL_BANKS * C * LO, bytes_accessed=2 << 20, transcendentals=0
         ),
-        name="scatter_backward",
+        name="scatter",
     )(kernel_map, weight, grad_pre)
 
 
@@ -235,7 +249,7 @@
         fold_kernel,
         out_shape=jax.ShapeDtypeStruct((GROUPS, C, CAP), BF),
         scratch_shapes=[pltpu.VMEM((BANKS * C, 2 * F), BF)],
-        compiler_params=pltpu.CompilerParams(vmem_limit_bytes=48 << 20),
+        compiler_params=pltpu.CompilerParams(vmem_limit_bytes=16 << 20),
         name="fold",
     )(table_grad, from_low, from_high, face_rows)
 
@@ -252,7 +266,7 @@
     return pl.pallas_call(
         take_back_kernel,
         out_shape=jax.ShapeDtypeStruct((C, R), BF),
-        compiler_params=pltpu.CompilerParams(vmem_limit_bytes=48 << 20),
+        compiler_params=pltpu.CompilerParams(vmem_limit_bytes=16 << 20),
         name="take_back",
     )(returned, owner, slot)
 
@@ -273,7 +287,6 @@
     output, grad_pre, weight_part = forward_pass(
         owned, ghost_low, ghost_high, kernel_map, weight_rows, incoming
     )
-    weight_grad = lax.psum(weight_part, ("sx", "sy")) * (1.0 / math.sqrt(GROUPS * side * V))
     weight_columns = jnp.transpose(weight, (0, 2, 1)).reshape(K * C, C)
     table_grad, to_low, to_high = scatter_pass(kernel_map, weight_columns, grad_pre)
     from_low = lax.ppermute(to_high, "sy", up)
@@ -281,6 +294,8 @@
     owned_grad = fold_faces(table_grad, from_low, from_high, face_list)
     returned = lax.all_to_all(owned_grad, "sx", 0, 0, tiled=True)
     point_grad = take_back(returned, owner, slot)
+    weight_sum = lax.psum(weight_part, ("sx", "sy")).astype(BF)
+    weight_grad = weight_sum.astype(F32) * (1.0 / math.sqrt(GROUPS * side * V))
     return (output[None, None], point_grad[None, None], weight_grad)
 
 

time: 346 us -> 211 us (0.61)
  waiting for transfers between devices: 201 us -> 4.23 us
  blocking collectives: 27.5 us -> 105 us
  between operations: 14.1 us -> 0.78 us
  Pallas kernels: 81.1 us -> 77 us
  starting transfers between devices: 12.1 us -> 15.6 us
    psum x1 -> x0, waiting for transfers between devices: 196 us -> none  [body(): lax.psum(weight_part, ('sx', 'sy')) * (1.0 / math.sqrt(GROUPS * side * V))]
    psum x0 -> x1, blocking collectives: none -> 88.3 us  [body(): weight_sum = lax.psum(weight_part, ('sx', 'sy')).astype(BF)]
    all_to_all x1 -> x0, blocking collectives: 11 us -> none  [body(): returned = lax.all_to_all(owned_grad, 'sx', 0, 0, tiled=True)]
    all_to_all x0 -> x1, starting transfers between devices: none -> 3.55 us  [body(): returned = lax.all_to_all(owned_grad, 'sx', 0, 0, tiled=True)]
  transfers between devices with their start and end apart: 5 -> 5, of which waited for: 3 -> 2; matrix products, arithmetic and copies ran while one was open for 1% -> 2% of each run, Pallas kernels for 11% -> 0%
where the time goes in v3:
time: 211 us
  blocking collectives  105 us (50%)
  Pallas kernels  77 us (36%)
  starting transfers between devices  15.6 us (7%)
  local copies, waits for them, and re-layouts  7.2 us (3%)
  waiting for transfers between devices  4.23 us (2%)
    psum x1, blocking collectives, body(): weight_sum = lax.psum(weight_part, ('sx', 'sy')).astype(BF)  88.3 us
    pallas_call x1, Pallas kernels, forward_pass(): pl.pallas_call(forward_kernel, grid=(V // VB,), in_specs=[whole(GROUPS, C...  37.2 us
    pallas_call x1, Pallas kernels, scatter_pass(): pl.pallas_call(scatter_kernel, grid=(V // VB,), in_specs=[pl.BlockSpec((K...  34.8 us
    all_to_all x1, blocking collectives, body(): owned = lax.all_to_all(outgoing, 'sx', 0, 0, tiled=True)  16.6 us
    ppermute x1, starting transfers between devices, body(): ghost_low = lax.ppermute(upper, 'sy', up)  5.3 us
    unnamed x24, local copies, waits for them, and re-layouts  5.15 us
  transfers between devices with their start and end apart: 5, of which 2 were waited for; matrix products, arithmetic and copies ran while one was open for 2% of the time, Pallas kernels for 0%

profile of v3, /device:TPU:1, one launch (start us, length us, event | category | flops | bytes accessed | tf_op | source)
XLA Modules:
  0.0 210.9 jit_solution(10310254539076172610)
XLA Ops:
  0.6 0.0 copy-start
  0.6 0.9 copy-done
  1.6 0.0 copy-start.1
  1.6 0.7 copy-done.1
  2.2 0.0 copy-start.11
  2.2 1.6 place.1
  3.9 16.6 %all_to_all.10.owned_ref = bf16[16,96,128]{2,1,0:T(8,128)(2,1)S(1)} all-to-all(bf16[16,96,128]{2,1,0:T(8,128)(2,1)S(1)} %get-tuple-element.13), channel_id=1, replica_groups=mesh['sx'=16,'sy'=16] {'sx'}, dimensions={0} | all-to-all | bytes 786432 | tf_op jit(solution)/shard_map/all_to_all | solution.py:282
  20.4 0.0 copy-start.3
  20.4 0.7 copy-done.3
  21.1 0.6 faces.1
  21.7 5.3 %collective-permute-start = (bf16[96,256]{1,0:T(8,128)(2,1)S(1)}, bf16[96,256]{1,0:T(8,128)(2,1)S(1)}, u32[]{:S(2)}, u32[]{:S(2)}) collective-permute-start(bf16[96,256]{1,0:T(8,128)(2,1)S(1)} %get-tuple-element.14), channel_id=1, source_target_pairs={{0,1},{1,2},{2,3},{3,4},{4,5},{5,6},{6,7},{7,8},{8,9},{9,10},{10,1... | collective-permute-start | bytes 147464 | tf_op jit(solution)/shard_map/ppermute | solution.py:284
  27.0 1.9 collective-permute-start.1
  28.9 0.0 copy-done.11
  28.9 0.3 copy.11
  29.3 0.0 copy-start.5
  29.3 0.0 copy-start.6
  29.3 0.3 copy.12.weight_ref
  29.6 1.4 copy.13
  31.0 0.0 collective-permute-done.low_ref
  31.0 0.0 copy-start.7
  31.0 0.6 copy-done.7
  31.7 0.8 collective-permute-done.1.high_ref
  32.4 0.0 copy-start.9
  32.4 0.6 copy-done.9
  33.0 0.0 copy-done.5
  33.0 0.0 copy-done.6
  33.0 0.0 copy-start.8
  33.0 0.8 copy-done.8
  33.8 0.0 copy-start.10
  33.8 0.8 copy-done.10
  34.6 37.2 %gather_forward.1 = (bf16[96,2048]{1,0:T(8,128)(2,1)}, bf16[96,2048]{1,0:T(8,128)(2,1)S(1)}, f32[27,96,96]{2,1,0:T(8,128)S(1)}) custom-call(bf16[16,96,128]{2,1,0:T(8,128)(2,1)S(1)} %all_to_all.10.owned_ref, bf16[96,256]{1,0:T(8,128)(2,1)S(1)} %copy-done.8, bf16[96,256]{1,0:T(8,128)(2,1)S(1)} %copy-done.10, s32[27,1,2048]{2,1,0:T(1,128)S(1)} %bitcast.18, ...), custom_call_target="tpu_custom_call" | custom-call | flops 27179089920 | bytes 4194304 | tf_op jit(solution)/shard_map/gather_forward/pallas_call | solution.py:146
  71.8 0.0 copy-start.4
  71.8 34.8 %scatter.1 = (f32[768,256]{1,0:T(8,128)S(1)}, bf16[96,256]{1,0:T(8,128)(2,1)S(1)}, bf16[96,256]{1,0:T(8,128)(2,1)S(1)}) custom-call(s32[27,1,2048]{2,1,0:T(1,128)S(1)} %bitcast.19, bf16[2592,96]{1,0:T(8,128)(2,1)S(1)} %bitcast.11, bf16[96,2048]{1,0:T(8,128)(2,1)S(1)} %get-tuple-element.17.pre_ref), custom_call_target="tpu_custom_call" | custom-call | flops 27179089920 | bytes 2097152 | tf_op jit(solution)/shard_map/scatter/pallas_call | solution.py:206
  106.7 2.9 %collective-permute-start.2 = (bf16[96,256]{1,0:T(8,128)(2,1)S(1)}, bf16[96,256]{1,0:T(8,128)(2,1)S(1)}, u32[]{:S(2)}, u32[]{:S(2)}) collective-permute-start(bf16[96,256]{1,0:T(8,128)(2,1)S(1)} %get-tuple-element.19), channel_id=1, source_target_pairs={{0,1},{1,2},{2,3},{3,4},{4,5},{5,6},{6,7},{7,8},{8,9},{9,10},{10,1... | collective-permute-start | bytes 147464 | tf_op jit(solution)/shard_map/ppermute | solution.py:292
  109.6 1.9 collective-permute-start.3
  111.5 0.0 collective-permute-done.2.from_low_ref
  111.5 3.5 %collective-permute-done.3.from_high_ref = bf16[96,256]{1,0:T(8,128)(2,1)S(1)} collective-permute-done((bf16[96,256]{1,0:T(8,128)(2,1)S(1)}, bf16[96,256]{1,0:T(8,128)(2,1)S(1)}, u32[]{:S(2)}, u32[]{:S(2)}) %collective-permute-start.3) | collective-permute-done | bytes 49184 | tf_op jit(solution)/shard_map/ppermute | solution.py:293
  115.0 0.0 copy-done.4
  115.0 1.2 fold.1
  116.1 3.6 %all-to-all-start.1 = ((bf16[16,96,128]{2,1,0:T(8,128)(2,1)}), bf16[16,96,128]{2,1,0:T(8,128)(2,1)S(1)}, u32[]{:S(2)}, u32[]{:S(2)}) async-start(bf16[16,96,128]{2,1,0:T(8,128)(2,1)} %fold.1), calls=%async_computation.1 | async-start | bytes 786432 | tf_op jit(solution)/shard_map/all_to_all | solution.py:295
  119.7 88.3 %all-reduce.1 = bf16[27,96,96]{2,1,0:T(8,128)(2,1)S(1)} all-reduce(f32[27,96,96]{2,1,0:T(8,128)S(1)} %get-tuple-element.22), channel_id=1, replica_groups=mesh['sx'=16,'sy'=16] {'sx','sy'}, use_global_device_ids=true, to_apply=%region_0.0 | all-reduce | flops 248832 | bytes 1492992 | tf_op jit(solution)/shard_map/psum | solution.py:297
  208.0 0.0 copy-start.2
  208.0 1.2 convert_multiply_fusion
  209.2 0.0 all-to-all-done.1.back_ref
  209.2 0.0 copy-done.2
  209.2 1.6 take_back.1
Async XLA Ops:
  0.6 0.9 copy-start
  1.6 0.7 copy-start.1
  2.2 26.7 %copy-start.11 = (bf16[27,96,96]{2,1,0:T(8,128)(2,1)S(1)}, bf16[27,96,96]{2,1,0:T(8,128)(2,1)}, u32[]{:S(2)}) copy-start(bf16[27,96,96]{2,1,0:T(8,128)(2,1)} %param.10) | copy-start | bytes 1492996
  20.4 0.7 copy-start.3
  21.7 9.3 %collective-permute-start = (bf16[96,256]{1,0:T(8,128)(2,1)S(1)}, bf16[96,256]{1,0:T(8,128)(2,1)S(1)}, u32[]{:S(2)}, u32[]{:S(2)}) collective-permute-start(bf16[96,256]{1,0:T(8,128)(2,1)S(1)} %get-tuple-element.14), channel_id=1, source_target_pairs={{0,1},{1,2},{2,3},{3,4},{4,5},{5,6},{6,7},{7,8},{8,9},{9,10},{10,1... | collective-permute-start | bytes 147464 | tf_op jit(solution)/shard_map/ppermute | solution.py:284
  27.0 5.4 %collective-permute-start.1 = (bf16[96,256]{1,0:T(8,128)(2,1)S(1)}, bf16[96,256]{1,0:T(8,128)(2,1)S(1)}, u32[]{:S(2)}, u32[]{:S(2)}) collective-permute-start(bf16[96,256]{1,0:T(8,128)(2,1)S(1)} %get-tuple-element.15), channel_id=1, source_target_pairs={{1,0},{2,1},{3,2},{4,3},{5,4},{6,5},{7,6},{8,7},{9,8},{10,9},{11,1... | collective-permute-start | bytes 147464 | tf_op jit(solution)/shard_map/ppermute | solution.py:285
  29.3 3.8 %copy-start.5 = (bf16[1,1,96,2048]{3,2,1,0:T(8,128)(2,1)S(1)}, bf16[1,1,96,2048]{3,2,1,0:T(8,128)(2,1)}, u32[]{:S(2)}) copy-start(bf16[1,1,96,2048]{3,2,1,0:T(8,128)(2,1)} %param.11) | copy-start | bytes 1179652
  29.3 3.8 %copy-start.6 = (s32[1,1,27,2048]{3,1,2,0:T(1,128)S(1)}, s32[1,1,27,2048]{3,1,2,0:T(1,128)}, u32[]{:S(2)}) copy-start(s32[1,1,27,2048]{3,1,2,0:T(1,128)} %param.8) | copy-start | bytes 663556
  31.0 0.6 copy-start.7
  32.4 0.6 copy-start.9
  33.0 0.8 copy-start.8
  33.8 0.8 copy-start.10
  71.8 43.2 %copy-start.4 = (s32[1,1,2,256]{3,2,1,0:T(2,128)S(1)}, s32[1,1,2,256]{3,2,1,0:T(2,128)}, u32[]{:S(2)}) copy-start(s32[1,1,2,256]{3,2,1,0:T(2,128)} %param.9) | copy-start | bytes 6148
  106.7 4.8 %collective-permute-start.2 = (bf16[96,256]{1,0:T(8,128)(2,1)S(1)}, bf16[96,256]{1,0:T(8,128)(2,1)S(1)}, u32[]{:S(2)}, u32[]{:S(2)}) collective-permute-start(bf16[96,256]{1,0:T(8,128)(2,1)S(1)} %get-tuple-element.19), channel_id=1, source_target_pairs={{0,1},{1,2},{2,3},{3,4},{4,5},{5,6},{6,7},{7,8},{8,9},{9,10},{10,1... | collective-permute-start | bytes 147464 | tf_op jit(solution)/shard_map/ppermute | solution.py:292
  109.6 5.4 %collective-permute-start.3 = (bf16[96,256]{1,0:T(8,128)(2,1)S(1)}, bf16[96,256]{1,0:T(8,128)(2,1)S(1)}, u32[]{:S(2)}, u32[]{:S(2)}) collective-permute-start(bf16[96,256]{1,0:T(8,128)(2,1)S(1)} %get-tuple-element.20), channel_id=1, source_target_pairs={{1,0},{2,1},{3,2},{4,3},{5,4},{6,5},{7,6},{8,7},{9,8},{10,9},{11,1... | collective-permute-start | bytes 147464 | tf_op jit(solution)/shard_map/ppermute | solution.py:293
  116.1 93.1 %all-to-all-start.1 = ((bf16[16,96,128]{2,1,0:T(8,128)(2,1)}), bf16[16,96,128]{2,1,0:T(8,128)(2,1)S(1)}, u32[]{:S(2)}, u32[]{:S(2)}) async-start(bf16[16,96,128]{2,1,0:T(8,128)(2,1)} %fold.1), calls=%async_computation.1 | async-start | bytes 786432 | tf_op jit(solution)/shard_map/all_to_all | solution.py:295
  208.0 1.2 copy-start.2

commit v4 on v2

--- a/solution.py
+++ b/solution.py
@@ -21,11 +21,12 @@
 WIDE = 512
 WIDE_BANKS = ALL_BANKS * LO // WIDE
 VB = 256
-PER_DOT = 9
-PARTS = (4, 3, 1)
+FORWARD_VB = 512
+PER_DOT = 3
+PARTS = (3, 3, 2)
 LANES = 128
 TILES = K * C // LANES
-SLOTS = C // 8 * TILES // GROUPS
+SHARD_TILES = 8
 
 BF = jnp.bfloat16
 F32 = jnp.float32
@@ -59,6 +60,10 @@
     for a in range(banks):
         spread = jnp.where((bank16 == a)[None], values, BF(0))
         out_ref[a * C : (a + 1) * C, column : column + n] = spread.reshape(C, n)
+
+
+def tile_place(i, t):
+    return divmod(i * TILES + t if t < TILES else (C // 16) * TILES + i, SHARD_TILES)
 
 
 def place_kernel(points_ref, owner_ref, out_ref, slot_ref, masked_ref):
@@ -90,7 +95,7 @@
             jax.ShapeDtypeStruct((1, R), jnp.int32),
         ),
         scratch_shapes=[pltpu.VMEM((GROUPS * C, R), BF)],
-        compiler_params=pltpu.CompilerParams(vmem_limit_bytes=48 << 20),
+        compiler_params=pltpu.CompilerParams(vmem_limit_bytes=16 << 20),
         name="place",
     )(points, owner)
 
@@ -107,7 +112,7 @@
     return pl.pallas_call(
         faces_kernel,
         out_shape=(jax.ShapeDtypeStruct((C, F), BF),) * 2,
-        compiler_params=pltpu.CompilerParams(vmem_limit_bytes=48 << 20),
+        compiler_params=pltpu.CompilerParams(vmem_limit_bytes=16 << 20),
         name="faces",
     )(owned, face_rows)
 
@@ -141,29 +146,29 @@
 
     @pl.when(step == pl.num_programs(0) - 1)
     def _():
-        for t in range(TILES):
-            block = acc_ref[t * LANES : (t + 1) * LANES, :].T
-            for i in range(C // 8):
-                shard, slot = divmod(i * TILES + t, SLOTS)
-                wg_ref[shard, slot * 8 : (slot + 1) * 8, :] = block[i * 8 : (i + 1) * 8, :]
-        rest = acc_ref[TILES * LANES :, :].T
-        rest = jnp.concatenate([rest, jnp.zeros((C, LANES - rest.shape[1]), F32)], axis=1)
-        for g in range(GROUPS):
-            tail = rest[g * 8 : (g + 1) * 8, :] if g < C // 8 else jnp.zeros((8, LANES), F32)
-            wg_ref[g, SLOTS * 8 :, :] = tail
+        for t in range(TILES + 1):
+            block = acc_ref[t * LANES : min((t + 1) * LANES, K * C), :].T
+            if t == TILES:
+                block = jnp.concatenate([block, jnp.zeros((C, LANES - block.shape[1]), F32)], axis=1)
+            block = block.astype(BF)
+            for i in range(C // 16):
+                shard, slot = tile_place(i, t)
+                wg_ref[shard, slot * 16 : (slot + 1) * 16, :] = block[i * 16 : (i + 1) * 16, :]
+        used = (TILES + 1) * (C // 16) - (GROUPS - 1) * SHARD_TILES
+        wg_ref[GROUPS - 1, used * 16 :, :] = jnp.zeros((LANES - used * 16, LANES), BF)
 
 
 def forward_pass(owned, low, high, kernel_map, weight, cotangent):
     whole = lambda *shape: pl.BlockSpec(shape, lambda i: (0,) * len(shape))
-    column = lambda rows: pl.BlockSpec((rows, VB), lambda i: (0, i))
+    column = lambda rows: pl.BlockSpec((rows, FORWARD_VB), lambda i: (0, i))
     return pl.pallas_call(
         forward_kernel,
-        grid=(V // VB,),
+        grid=(V // FORWARD_VB,),
         in_specs=[
             whole(GROUPS, C, CAP),
             whole(C, F),
             whole(C, F),
-            pl.BlockSpec((K, 1, VB), lambda i: (0, 0, i)),
+            pl.BlockSpec((K, 1, FORWARD_VB), lambda i: (0, 0, i)),
             whole(C, K * C),
             column(C),
         ],
@@ -171,14 +176,14 @@
         out_shape=(
             jax.ShapeDtypeStruct((C, V), BF),
             jax.ShapeDtypeStruct((C, V), BF),
-            jax.ShapeDtypeStruct((GROUPS, LANES, LANES), F32),
+            jax.ShapeDtypeStruct((GROUPS, LANES, LANES), BF),
         ),
         scratch_shapes=[
             pltpu.VMEM((WIDE_BANKS * C, WIDE), BF),
-            pltpu.VMEM((K * C, VB), BF),
+            pltpu.VMEM((K * C, FORWARD_VB), BF),
             pltpu.VMEM((K * C, C), F32),
         ],
-        compiler_params=pltpu.CompilerParams(vmem_limit_bytes=56 << 20),
+        compiler_params=pltpu.CompilerParams(vmem_limit_bytes=32 << 20),
         cost_estimate=pl.CostEstimate(
             flops=2 * K * V * ALL_BANKS * C * LO, bytes_accessed=4 << 20, transcendentals=C * V
         ),
@@ -188,21 +193,20 @@
 
 def scatter_step(map_ref, weight_ref, pre_ref, acc_ref, spread_ref, masked_ref):
     spread_ref[...] = jnp.dot(weight_ref[...], pre_ref[...], preferred_element_type=F32).astype(BF)
-    for first in range(0, K, PER_DOT):
+    for turn in range(K // PER_DOT):
         hots = []
+        slot = masked_ref.at[turn % 2]
         for j in range(PER_DOT):
-            k = first + j
+            k = turn * PER_DOT + j
             index = map_ref[k]
-            masked_banks(spread_ref[k * C : (k + 1) * C, :], index >> 8, ALL_BANKS, masked_ref, j * VB)
+            masked_banks(spread_ref[k * C : (k + 1) * C, :], index >> 8, ALL_BANKS, slot, j * VB)
             hots.append(onehot_rows(index & (LO - 1), LO))
         acc_ref[...] += lax.dot_general(
-            masked_ref[...], jnp.concatenate(hots, axis=1), NT, preferred_element_type=F32
+            slot[...], jnp.concatenate(hots, axis=1), NT, preferred_element_type=F32
         )
 
 
-def scatter_kernel(
-    has_start, has_faces, after_ref, start_ref, map_ref, weight_ref, pre_ref, *refs
-):
+def scatter_kernel(has_start, has_faces, after_ref, start_ref, map_ref, weight_ref, pre_ref, *refs):
     if has_faces:
         own_ref, low_ref, high_ref, spread_ref, masked_ref, acc_ref = refs
     else:
@@ -226,7 +230,7 @@
 def scatter_part(part, after, start, kernel_map, weight, grad_pre):
     whole = lambda *shape: pl.BlockSpec(shape, lambda i: (0,) * len(shape))
     sums = jax.ShapeDtypeStruct((ALL_BANKS * C, LO), F32)
-    scratch = [pltpu.VMEM((K * C, VB), BF), pltpu.VMEM((ALL_BANKS * C, PER_DOT * VB), BF)]
+    scratch = [pltpu.VMEM((K * C, VB), BF), pltpu.VMEM((2, ALL_BANKS * C, PER_DOT * VB), BF)]
     at, steps, last = sum(PARTS[:part]), PARTS[part], part == len(PARTS) - 1
     if last:
         out_specs = (whole(BANKS * C, LO), whole(C, F), whole(C, F))
@@ -251,12 +255,50 @@
         out_specs=out_specs,
         out_shape=out_shape,
         scratch_shapes=scratch,
-        compiler_params=pltpu.CompilerParams(vmem_limit_bytes=56 << 20),
+        compiler_params=pltpu.CompilerParams(vmem_limit_bytes=24 << 20),
         cost_estimate=pl.CostEstimate(
             flops=2 * K * VB * steps * ALL_BANKS * C * LO, bytes_accessed=2 << 20, transcendentals=0
         ),
         name="scatter",
     )(after, start, kernel_map, weight, grad_pre)
+
+
+def sum_parts_kernel(parts_ref, out_ref):
+    total = parts_ref[0].astype(F32)
+    for g in range(1, GROUPS):
+        total = total + parts_ref[g].astype(F32)
+    total = total.astype(BF)
+    for g in range(GROUPS):
+        out_ref[g] = total
+
+
+def sum_parts(parts):
+    return pl.pallas_call(
+        sum_parts_kernel,
+        out_shape=jax.ShapeDtypeStruct(parts.shape, BF),
+        compiler_params=pltpu.CompilerParams(vmem_limit_bytes=8 << 20),
+        name="sum_parts",
+    )(parts)
+
+
+def unpack_kernel(scale, parts_ref, out_ref, flat_ref):
+    for t in range(TILES + 1):
+        for i in range(C // 16):
+            shard, slot = tile_place(i, t)
+            tile = parts_ref[shard, slot * 16 : (slot + 1) * 16, :].astype(F32) * scale
+            flat_ref[i * 16 : (i + 1) * 16, t * LANES : (t + 1) * LANES] = tile
+    for k in range(K):
+        out_ref[k] = flat_ref[:, k * C : (k + 1) * C]
+
+
+def unpack_weight(parts, scale):
+    return pl.pallas_call(
+        functools.partial(unpack_kernel, scale),
+        out_shape=jax.ShapeDtypeStruct((K, C, C), F32),
+        scratch_shapes=[pltpu.VMEM((C, (TILES + 1) * LANES), F32)],
+        compiler_params=pltpu.CompilerParams(vmem_limit_bytes=16 << 20),
+        name="unpack",
+    )(parts)
 
 
 def fold_kernel(grad_ref, from_low_ref, from_high_ref, rows_ref, out_ref, masked_ref):
@@ -278,7 +320,7 @@
         fold_kernel,
         out_shape=jax.ShapeDtypeStruct((GROUPS, C, CAP), BF),
         scratch_shapes=[pltpu.VMEM((BANKS * C, 2 * F), BF)],
-        compiler_params=pltpu.CompilerParams(vmem_limit_bytes=48 << 20),
+        compiler_params=pltpu.CompilerParams(vmem_limit_bytes=16 << 20),
         name="fold",
     )(table_grad, from_low, from_high, face_rows)
 
@@ -295,31 +337,9 @@
     return pl.pallas_call(
         take_back_kernel,
         out_shape=jax.ShapeDtypeStruct((C, R), BF),
-        compiler_params=pltpu.CompilerParams(vmem_limit_bytes=48 << 20),
+        compiler_params=pltpu.CompilerParams(vmem_limit_bytes=16 << 20),
         name="take_back",
     )(returned, owner, slot)
-
-
-def unpack_kernel(scale, parts_ref, out_ref, flat_ref):
-    for g in range(GROUPS):
-        block = parts_ref[g] * scale
-        for slot in range(SLOTS):
-            i, t = divmod(g * SLOTS + slot, TILES)
-            flat_ref[i * 8 : (i + 1) * 8, t * LANES : (t + 1) * LANES] = block[slot * 8 : (slot + 1) * 8, :]
-        if g < C // 8:
-            flat_ref[g * 8 : (g + 1) * 8, TILES * LANES :] = block[SLOTS * 8 :, :]
-    for k in range(K):
-        out_ref[k] = flat_ref[:, k * C : (k + 1) * C]
-
-
-def unpack_weight(parts, scale):
-    return pl.pallas_call(
-        functools.partial(unpack_kernel, scale),
-        out_shape=jax.ShapeDtypeStruct((K, C, C), F32),
-        scratch_shapes=[pltpu.VMEM((C, (TILES + 1) * LANES), F32)],
-        compiler_params=pltpu.CompilerParams(vmem_limit_bytes=32 << 20),
-        name="unpack",
-    )(parts)
 
 
 def body(points, owners, kernel_maps, face_rows, weight, cotangent):
@@ -340,12 +360,13 @@
     )
     weight_columns = jnp.transpose(weight, (0, 2, 1)).reshape(K * C, C)
     scatter = functools.partial(scatter_part, kernel_map=kernel_map, weight=weight_columns, grad_pre=grad_pre)
-    row_sum = lax.psum_scatter(weight_part, "sx", scatter_dimension=0, tiled=False)
+    across = lambda array, axis: lax.all_to_all(array, axis, 0, 0, tiled=True)
+    row_sums = sum_parts(across(weight_part, "sx"))
     sums = scatter(0, grad_pre, grad_pre)
-    share = lax.psum(row_sum, "sy")
-    sums = scatter(1, row_sum, sums)
-    parts = lax.all_gather(share, "sx", axis=0)
-    table_grad, to_low, to_high = scatter(2, share, sums)
+    all_sums = sum_parts(across(row_sums, "sy"))
+    sums = scatter(1, row_sums, sums)
+    parts = across(all_sums, "sx")
+    table_grad, to_low, to_high = scatter(2, all_sums, sums)
     from_low = lax.ppermute(to_high, "sy", up)
     from_high = lax.ppermute(to_low, "sy", down)
     owned_grad = fold_faces(table_grad, from_low, from_high, face_list)

time: 331 us -> 167 us (0.50)
  waiting for transfers between devices: 179 us -> 26.1 us
  starting transfers between devices: 12 us -> 30.2 us
  between operations: 13.8 us -> 0.81 us
  Pallas kernels: 86 us -> 77.5 us
  local copies, waits for them, and re-layouts: 7.83 us -> 3.31 us
  blocking collectives: 31.7 us -> 28 us
    psum x1 -> x0, waiting for transfers between devices: 103 us -> none  [body(): share = lax.psum(row_sum, 'sy')]
    unnamed x4 -> x0, waiting for transfers between devices: 55.1 us -> none
    all_to_all x0 -> x3, waiting for transfers between devices: none -> 19.8 us  [body(): across = lambda array, axis: lax.all_to_all(array, axis, 0, 0, tiled=True)]
    all_to_all x0 -> x3, starting transfers between devices: none -> 17.4 us  [body(): across = lambda array, axis: lax.all_to_all(array, axis, 0, 0, tiled=True)]
    all_gather x1 -> x0, waiting for transfers between devices: 15.1 us -> none  [body(): parts = lax.all_gather(share, 'sx', axis=0)]
    pallas_call x3, Pallas kernels: 41.5 us -> 35 us  [scatter_part(): pl.pallas_call(functools.partial(scatter_kernel, part > 0, last), grid=(s...]
    all_to_all x1, blocking collectives: 15.2 us -> 11.4 us  [body(): returned = lax.all_to_all(owned_grad, 'sx', 0, 0, tiled=True)]
    pallas_call x1 -> x3, Pallas kernels: 38.7 us -> 36.7 us  [the longest x1 34.9 us: forward_pass(): pl.pallas_call(forward_kernel, grid=(V // FORWARD_VB,), in_specs=[whole(G...]
  transfers between devices with their start and end apart: 7 -> 7, of which waited for: 5 -> 4; matrix products, arithmetic and copies ran while one was open for 1% -> 1% of each run, Pallas kernels for 9% -> 17%
where the time goes in v4:
time: 167 us; the launch traced here: 166 us
  Pallas kernels  77.5 us (46%)
  starting transfers between devices  30.2 us (18%)
  blocking collectives  28 us (17%)
  waiting for transfers between devices  26.1 us (16%)
  local copies, waits for them, and re-layouts  3.31 us (2%)
    pallas_call x3, Pallas kernels, scatter_part(): pl.pallas_call(functools.partial(scatter_kernel, part > 0, last), grid=(s...  35 us
    pallas_call x1, Pallas kernels, forward_pass(): pl.pallas_call(forward_kernel, grid=(V // FORWARD_VB,), in_specs=[whole(G...  34.9 us
    all_to_all x3, waiting for transfers between devices, body(): across = lambda array, axis: lax.all_to_all(array, axis, 0, 0, tiled=True)  19.8 us
    all_to_all x3, starting transfers between devices, body(): across = lambda array, axis: lax.all_to_all(array, axis, 0, 0, tiled=True)  17.4 us
    all_to_all x1, blocking collectives, body(): owned = lax.all_to_all(outgoing, 'sx', 0, 0, tiled=True)  16.6 us
    all_to_all x1, blocking collectives, body(): returned = lax.all_to_all(owned_grad, 'sx', 0, 0, tiled=True)  11.4 us
    ppermute x1, starting transfers between devices, body(): ghost_low = lax.ppermute(upper, 'sy', up)  5.43 us
    ppermute x1, starting transfers between devices, body(): from_low = lax.ppermute(to_high, 'sy', up)  3.54 us
  transfers between devices with their start and end apart: 7, of which 4 were waited for; matrix products, arithmetic and copies ran while one was open for 1% of the time, Pallas kernels for 17%

profile of v4, /device:TPU:1, one launch (start us, length us, event | category | flops | bytes accessed | tf_op | source)
XLA Modules:
  0.0 165.9 jit_solution(10892721081517964404)
XLA Ops:
  0.6 0.0 copy-start
  0.6 0.9 copy-done
  1.6 0.0 copy-start.1
  1.6 0.7 copy-done.1
  2.2 0.0 copy-start.7
  2.2 1.6 place.1
  3.9 16.6 %all_to_all.25.owned_ref = bf16[16,96,128]{2,1,0:T(8,128)(2,1)S(1)} all-to-all(bf16[16,96,128]{2,1,0:T(8,128)(2,1)S(1)} %get-tuple-element.13), channel_id=1, replica_groups=mesh['sx'=16,'sy'=16] {'sx'}, dimensions={0} | all-to-all | bytes 786432 | tf_op jit(solution)/shard_map/all_to_all | solution.py:353
  20.4 0.0 copy-start.3
  20.4 0.7 copy-done.3
  21.1 0.6 faces.1
  21.7 0.0 copy-start.5
  21.7 0.0 copy-start.6
  21.7 5.4 %collective-permute-start = (bf16[96,256]{1,0:T(8,128)(2,1)S(1)}, bf16[96,256]{1,0:T(8,128)(2,1)S(1)}, u32[]{:S(2)}, u32[]{:S(2)}) collective-permute-start(bf16[96,256]{1,0:T(8,128)(2,1)S(1)} %get-tuple-element.14), channel_id=1, source_target_pairs={{0,1},{1,2},{2,3},{3,4},{4,5},{5,6},{6,7},{7,8},{8,9},{9,10},{10,1... | collective-permute-start | bytes 147464 | tf_op jit(solution)/shard_map/ppermute | solution.py:355
  27.1 1.9 %collective-permute-start.1 = (bf16[96,256]{1,0:T(8,128)(2,1)S(1)}, bf16[96,256]{1,0:T(8,128)(2,1)S(1)}, u32[]{:S(2)}, u32[]{:S(2)}) collective-permute-start(bf16[96,256]{1,0:T(8,128)(2,1)S(1)} %get-tuple-element.15), channel_id=1, source_target_pairs={{1,0},{2,1},{3,2},{4,3},{5,4},{6,5},{7,6},{8,7},{9,8},{10,9},{11,1... | collective-permute-start | bytes 147464 | tf_op jit(solution)/shard_map/ppermute | solution.py:356
  29.1 0.0 copy-done.7
  29.1 0.3 copy.11
  29.4 0.3 copy.12.weight_ref
  29.7 0.0 collective-permute-done.low_ref
  29.8 2.8 %collective-permute-done.1.high_ref = bf16[96,256]{1,0:T(8,128)(2,1)S(1)} collective-permute-done((bf16[96,256]{1,0:T(8,128)(2,1)S(1)}, bf16[96,256]{1,0:T(8,128)(2,1)S(1)}, u32[]{:S(2)}, u32[]{:S(2)}) %collective-permute-start.1) | collective-permute-done | bytes 49184 | tf_op jit(solution)/shard_map/ppermute | solution.py:356
  32.6 0.0 copy-done.5
  32.6 0.0 copy-done.6
  32.6 34.9 %gather_forward.1 = (bf16[96,2048]{1,0:T(8,128)(2,1)}, bf16[96,2048]{1,0:T(8,128)(2,1)S(1)}, bf16[16,128,128]{2,1,0:T(8,128)(2,1)}) custom-call(bf16[16,96,128]{2,1,0:T(8,128)(2,1)S(1)} %all_to_all.25.owned_ref, bf16[96,256]{1,0:T(8,128)(2,1)S(1)} %collective-permute-done.low_ref, bf16[96,256]{1,0:T(8,128)(2,1)S(1)} %collective-permute-done.1.high_ref, ...), custom_call_target="tpu_custom_call" | custom-call | flops 27179089920 | bytes 4194304 | tf_op jit(solution)/shard_map/gather_forward/pallas_call | solution.py:164
  67.5 0.0 copy-start.8
  67.5 3.7 %all-to-all-start.1 = ((bf16[16,128,128]{2,1,0:T(8,128)(2,1)}), bf16[16,128,128]{2,1,0:T(8,128)(2,1)S(1)}, u32[]{:S(2)}, u32[]{:S(2)}) async-start(bf16[16,128,128]{2,1,0:T(8,128)(2,1)} %get-tuple-element.17), calls=%async_computation.1 | async-start | bytes 1048576 | tf_op jit(solution)/shard_map/all_to_all | solution.py:363
  71.2 0.0 copy-done.8
  71.2 0.3 copy.13
  71.5 9.6 %all-to-all-done.1.parts_ref = bf16[16,128,128]{2,1,0:T(8,128)(2,1)S(1)} async-done(((bf16[16,128,128]{2,1,0:T(8,128)(2,1)}), bf16[16,128,128]{2,1,0:T(8,128)(2,1)S(1)}, u32[]{:S(2)}, u32[]{:S(2)}) %all-to-all-start.1) | async-done | bytes 524320 | tf_op jit(solution)/shard_map/all_to_all | solution.py:363
  81.2 0.9 sum_parts.2.after_ref
  82.0 10.1 %all-to-all-start.2 = ((bf16[16,128,128]{2,1,0:T(8,128)(2,1)}), bf16[16,128,128]{2,1,0:T(8,128)(2,1)S(1)}, u32[]{:S(2)}, u32[]{:S(2)}) async-start(bf16[16,128,128]{2,1,0:T(8,128)(2,1)} %sum_parts.2.after_ref), calls=%async_computation.2 | async-start | bytes 1048576 | tf_op jit(solution)/shard_map/all_to_all | solution.py:363
  92.1 13.1 %scatter.3.start_ref = f32[960,256]{1,0:T(8,128)S(1)} custom-call(bf16[96,2048]{1,0:T(8,128)(2,1)S(1)} %get-tuple-element.18.after_ref.start_ref.pre_ref, bf16[96,2048]{1,0:T(8,128)(2,1)S(1)} %get-tuple-element.18.after_ref.start_ref.pre_ref, s32[27,1,2048]{2,1,0:T(1,128)S(1)} %bitcast.21, bf16[2592,96]{1,0:T(8,128)(2,1)S(1)} %bitcast.11, ...), custom_call_target="tpu_custom_call" | custom-call | flops 10192158720 | bytes 2097152 | tf_op jit(solution)/shard_map/scatter/pallas_call | solution.py:245
  105.2 13.1 %scatter.4.start_ref = f32[960,256]{1,0:T(8,128)S(1)} custom-call(bf16[16,128,128]{2,1,0:T(8,128)(2,1)} %sum_parts.2.after_ref, f32[960,256]{1,0:T(8,128)S(1)} %scatter.3.start_ref, s32[27,1,2048]{2,1,0:T(1,128)S(1)} %bitcast.22, bf16[2592,96]{1,0:T(8,128)(2,1)S(1)} %bitcast.12, bf16[96,2048]{1,0:T(8,128)(2,1)S(1)} %get-tuple-element.18.after_ref.start_ref.pre_ref), custom_call_target="tpu_custom_call" | custom-call | flops 10192158720 | bytes 2097152 | tf_op jit(solution)/shard_map/scatter/pallas_call | solution.py:245
  118.4 0.0 all-to-all-done.2.parts_ref
  118.4 0.9 sum_parts.3.after_ref
  119.3 0.0 copy-start.4
  119.3 8.8 %scatter.5 = (f32[768,256]{1,0:T(8,128)S(1)}, bf16[96,256]{1,0:T(8,128)(2,1)S(1)}, bf16[96,256]{1,0:T(8,128)(2,1)S(1)}) custom-call(bf16[16,128,128]{2,1,0:T(8,128)(2,1)} %sum_parts.3.after_ref, f32[960,256]{1,0:T(8,128)S(1)} %scatter.4.start_ref, s32[27,1,2048]{2,1,0:T(1,128)S(1)} %bitcast.23, bf16[2592,96]{1,0:T(8,128)(2,1)S(1)} %bitcast.13, ...), custom_call_target="tpu_custom_call" | custom-call | flops 6794772480 | bytes 2097152 | tf_op jit(solution)/shard_map/scatter/pallas_call | solution.py:245
  128.1 3.5 %collective-permute-start.2 = (bf16[96,256]{1,0:T(8,128)(2,1)S(1)}, bf16[96,256]{1,0:T(8,128)(2,1)S(1)}, u32[]{:S(2)}, u32[]{:S(2)}) collective-permute-start(bf16[96,256]{1,0:T(8,128)(2,1)S(1)} %get-tuple-element.20), channel_id=1, source_target_pairs={{0,1},{1,2},{2,3},{3,4},{4,5},{5,6},{6,7},{7,8},{8,9},{9,10},{10,1... | collective-permute-start | bytes 147464 | tf_op jit(solution)/shard_map/ppermute | solution.py:370
  131.6 1.9 %collective-permute-start.3 = (bf16[96,256]{1,0:T(8,128)(2,1)S(1)}, bf16[96,256]{1,0:T(8,128)(2,1)S(1)}, u32[]{:S(2)}, u32[]{:S(2)}) collective-permute-start(bf16[96,256]{1,0:T(8,128)(2,1)S(1)} %get-tuple-element.21), channel_id=1, source_target_pairs={{1,0},{2,1},{3,2},{4,3},{5,4},{6,5},{7,6},{8,7},{9,8},{10,9},{11,1... | collective-permute-start | bytes 147464 | tf_op jit(solution)/shard_map/ppermute | solution.py:371
  133.6 0.0 collective-permute-done.2.from_low_ref
  133.6 3.5 %collective-permute-done.3.from_high_ref = bf16[96,256]{1,0:T(8,128)(2,1)S(1)} collective-permute-done((bf16[96,256]{1,0:T(8,128)(2,1)S(1)}, bf16[96,256]{1,0:T(8,128)(2,1)S(1)}, u32[]{:S(2)}, u32[]{:S(2)}) %collective-permute-start.3) | collective-permute-done | bytes 49184 | tf_op jit(solution)/shard_map/ppermute | solution.py:371
  137.0 0.0 copy-done.4
  137.0 0.0 copy-start.2
  137.1 0.4 fold.1
  137.5 11.4 %all_to_all.26.back_ref = bf16[16,96,128]{2,1,0:T(8,128)(2,1)S(1)} all-to-all(bf16[16,96,128]{2,1,0:T(8,128)(2,1)S(1)} %fold.1), channel_id=1, replica_groups=mesh['sx'=16,'sy'=16] {'sx'}, dimensions={0} | all-to-all | bytes 786432 | tf_op jit(solution)/shard_map/all_to_all | solution.py:373
  148.9 3.6 %all-to-all-start.4 = ((bf16[16,128,128]{2,1,0:T(8,128)(2,1)}), bf16[16,128,128]{2,1,0:T(8,128)(2,1)S(1)}, u32[]{:S(2)}, u32[]{:S(2)}) async-start(bf16[16,128,128]{2,1,0:T(8,128)(2,1)} %sum_parts.3.after_ref), calls=%async_computation.4 | async-start | bytes 1048576 | tf_op jit(solution)/shard_map/all_to_all | solution.py:363
  152.5 0.0 copy-done.2
  152.5 1.6 take_back.1
  154.1 10.2 %all-to-all-done.4.parts_ref = bf16[16,128,128]{2,1,0:T(8,128)(2,1)S(1)} async-done(((bf16[16,128,128]{2,1,0:T(8,128)(2,1)}), bf16[16,128,128]{2,1,0:T(8,128)(2,1)S(1)}, u32[]{:S(2)}, u32[]{:S(2)}) %all-to-all-start.4) | async-done | bytes 524320 | tf_op jit(solution)/shard_map/all_to_all | solution.py:363
  164.3 1.6 unpack.1
Async XLA Ops:
  0.6 0.9 copy-start
  1.6 0.7 copy-start.1
  2.2 26.8 %copy-start.7 = (bf16[27,96,96]{2,1,0:T(8,128)(2,1)S(1)}, bf16[27,96,96]{2,1,0:T(8,128)(2,1)}, u32[]{:S(2)}) copy-start(bf16[27,96,96]{2,1,0:T(8,128)(2,1)} %param.10) | copy-start | bytes 1492996
  20.4 0.7 copy-start.3
  21.7 10.9 %copy-start.5 = (bf16[1,1,96,2048]{3,2,1,0:T(8,128)(2,1)S(1)}, bf16[1,1,96,2048]{3,2,1,0:T(8,128)(2,1)}, u32[]{:S(2)}) copy-start(bf16[1,1,96,2048]{3,2,1,0:T(8,128)(2,1)} %param.11) | copy-start | bytes 1179652
  21.7 10.9 %copy-start.6 = (s32[1,1,27,2048]{3,1,2,0:T(1,128)S(1)}, s32[1,1,27,2048]{3,1,2,0:T(1,128)}, u32[]{:S(2)}) copy-start(s32[1,1,27,2048]{3,1,2,0:T(1,128)} %param.8) | copy-start | bytes 663556
  21.7 8.0 %collective-permute-start = (bf16[96,256]{1,0:T(8,128)(2,1)S(1)}, bf16[96,256]{1,0:T(8,128)(2,1)S(1)}, u32[]{:S(2)}, u32[]{:S(2)}) collective-permute-start(bf16[96,256]{1,0:T(8,128)(2,1)S(1)} %get-tuple-element.14), channel_id=1, source_target_pairs={{0,1},{1,2},{2,3},{3,4},{4,5},{5,6},{6,7},{7,8},{8,9},{9,10},{10,1... | collective-permute-start | bytes 147464 | tf_op jit(solution)/shard_map/ppermute | solution.py:355
  27.1 5.4 %collective-permute-start.1 = (bf16[96,256]{1,0:T(8,128)(2,1)S(1)}, bf16[96,256]{1,0:T(8,128)(2,1)S(1)}, u32[]{:S(2)}, u32[]{:S(2)}) collective-permute-start(bf16[96,256]{1,0:T(8,128)(2,1)S(1)} %get-tuple-element.15), channel_id=1, source_target_pairs={{1,0},{2,1},{3,2},{4,3},{5,4},{6,5},{7,6},{8,7},{9,8},{10,9},{11,1... | collective-permute-start | bytes 147464 | tf_op jit(solution)/shard_map/ppermute | solution.py:356
  67.5 3.7 %copy-start.8 = (bf16[27,96,96]{2,1,0:T(8,128)(2,1)S(1)}, bf16[27,96,96]{2,1,0:T(8,128)(2,1)}, u32[]{:S(2)}) copy-start(bf16[27,96,96]{2,1,0:T(8,128)(2,1)} %param.10) | copy-start | bytes 1492996
  67.5 13.7 %all-to-all-start.1 = ((bf16[16,128,128]{2,1,0:T(8,128)(2,1)}), bf16[16,128,128]{2,1,0:T(8,128)(2,1)S(1)}, u32[]{:S(2)}, u32[]{:S(2)}) async-start(bf16[16,128,128]{2,1,0:T(8,128)(2,1)} %get-tuple-element.17), calls=%async_computation.1 | async-start | bytes 1048576 | tf_op jit(solution)/shard_map/all_to_all | solution.py:363
  82.0 36.3 %all-to-all-start.2 = ((bf16[16,128,128]{2,1,0:T(8,128)(2,1)}), bf16[16,128,128]{2,1,0:T(8,128)(2,1)S(1)}, u32[]{:S(2)}, u32[]{:S(2)}) async-start(bf16[16,128,128]{2,1,0:T(8,128)(2,1)} %sum_parts.2.after_ref), calls=%async_computation.2 | async-start | bytes 1048576 | tf_op jit(solution)/shard_map/all_to_all | solution.py:363
  119.3 17.8 %copy-start.4 = (s32[1,1,2,256]{3,2,1,0:T(2,128)S(1)}, s32[1,1,2,256]{3,2,1,0:T(2,128)}, u32[]{:S(2)}) copy-start(s32[1,1,2,256]{3,2,1,0:T(2,128)} %param.9) | copy-start | bytes 6148
  128.1 5.5 %collective-permute-start.2 = (bf16[96,256]{1,0:T(8,128)(2,1)S(1)}, bf16[96,256]{1,0:T(8,128)(2,1)S(1)}, u32[]{:S(2)}, u32[]{:S(2)}) collective-permute-start(bf16[96,256]{1,0:T(8,128)(2,1)S(1)} %get-tuple-element.20), channel_id=1, source_target_pairs={{0,1},{1,2},{2,3},{3,4},{4,5},{5,6},{6,7},{7,8},{8,9},{9,10},{10,1... | collective-permute-start | bytes 147464 | tf_op jit(solution)/shard_map/ppermute | solution.py:370
  131.6 5.4 %collective-permute-start.3 = (bf16[96,256]{1,0:T(8,128)(2,1)S(1)}, bf16[96,256]{1,0:T(8,128)(2,1)S(1)}, u32[]{:S(2)}, u32[]{:S(2)}) collective-permute-start(bf16[96,256]{1,0:T(8,128)(2,1)S(1)} %get-tuple-element.21), channel_id=1, source_target_pairs={{1,0},{2,1},{3,2},{4,3},{5,4},{6,5},{7,6},{8,7},{9,8},{10,9},{11,1... | collective-permute-start | bytes 147464 | tf_op jit(solution)/shard_map/ppermute | solution.py:371
  137.0 15.4 %copy-start.2 = (s32[1,1,1024,1]{2,3,1,0:T(1,128)S(1)}, s32[1,1,1024,1]{2,3,1,0:T(1,128)}, u32[]{:S(2)}) copy-start(s32[1,1,1024,1]{2,3,1,0:T(1,128)} %param.7) | copy-start | bytes 12292
  148.9 15.4 %all-to-all-start.4 = ((bf16[16,128,128]{2,1,0:T(8,128)(2,1)}), bf16[16,128,128]{2,1,0:T(8,128)(2,1)S(1)}, u32[]{:S(2)}, u32[]{:S(2)}) async-start(bf16[16,128,128]{2,1,0:T(8,128)(2,1)} %sum_parts.3.after_ref), calls=%async_computation.4 | async-start | bytes 1048576 | tf_op jit(solution)/shard_map/all_to_all | solution.py:363

commit v5 on v4

--- a/solution.py
+++ b/solution.py
@@ -20,10 +20,10 @@
 ALL_BANKS = BANKS + 2
 WIDE = 512
 WIDE_BANKS = ALL_BANKS * LO // WIDE
-VB = 256
-FORWARD_VB = 512
+VB = 512
+FORWARD_VB = 1024
 PER_DOT = 3
-PARTS = (3, 3, 2)
+PARTS = (2, 1, 1)
 LANES = 128
 TILES = K * C // LANES
 SHARD_TILES = 8
@@ -255,7 +255,7 @@
         out_specs=out_specs,
         out_shape=out_shape,
         scratch_shapes=scratch,
-        compiler_params=pltpu.CompilerParams(vmem_limit_bytes=24 << 20),
+        compiler_params=pltpu.CompilerParams(vmem_limit_bytes=32 << 20),
         cost_estimate=pl.CostEstimate(
             flops=2 * K * VB * steps * ALL_BANKS * C * LO, bytes_accessed=2 << 20, transcendentals=0
         ),
@@ -263,45 +263,31 @@
     )(after, start, kernel_map, weight, grad_pre)
 
 
-def sum_parts_kernel(parts_ref, out_ref):
+def total_of(parts_ref):
     total = parts_ref[0].astype(F32)
     for g in range(1, GROUPS):
         total = total + parts_ref[g].astype(F32)
-    total = total.astype(BF)
+    return total.astype(BF)
+
+
+def sum_parts_kernel(after_ref, parts_ref, out_ref):
+    total = total_of(parts_ref)
     for g in range(GROUPS):
         out_ref[g] = total
 
 
-def sum_parts(parts):
+def sum_parts(after, parts):
     return pl.pallas_call(
         sum_parts_kernel,
+        in_specs=[pl.BlockSpec(memory_space=pl.ANY), pl.BlockSpec(memory_space=pltpu.VMEM)],
         out_shape=jax.ShapeDtypeStruct(parts.shape, BF),
         compiler_params=pltpu.CompilerParams(vmem_limit_bytes=8 << 20),
         name="sum_parts",
-    )(parts)
-
-
-def unpack_kernel(scale, parts_ref, out_ref, flat_ref):
-    for t in range(TILES + 1):
-        for i in range(C // 16):
-            shard, slot = tile_place(i, t)
-            tile = parts_ref[shard, slot * 16 : (slot + 1) * 16, :].astype(F32) * scale
-            flat_ref[i * 16 : (i + 1) * 16, t * LANES : (t + 1) * LANES] = tile
-    for k in range(K):
-        out_ref[k] = flat_ref[:, k * C : (k + 1) * C]
-
-
-def unpack_weight(parts, scale):
-    return pl.pallas_call(
-        functools.partial(unpack_kernel, scale),
-        out_shape=jax.ShapeDtypeStruct((K, C, C), F32),
-        scratch_shapes=[pltpu.VMEM((C, (TILES + 1) * LANES), F32)],
-        compiler_params=pltpu.CompilerParams(vmem_limit_bytes=16 << 20),
-        name="unpack",
-    )(parts)
-
-
-def fold_kernel(grad_ref, from_low_ref, from_high_ref, rows_ref, out_ref, masked_ref):
+    )(after, parts)
+
+
+def fold_kernel(grad_ref, from_low_ref, from_high_ref, rows_ref, parts_ref, out_ref, masked_ref):
+    share = total_of(parts_ref)
     hots = []
     for j, part_ref in enumerate((from_low_ref, from_high_ref)):
         rows = rows_ref[j : j + 1, :]
@@ -312,33 +298,42 @@
     )
     total = (grad_ref[...] + folded).astype(BF)
     for g in range(GROUPS):
-        out_ref[g] = total[(g // 2) * C : (g // 2 + 1) * C, (g % 2) * CAP : (g % 2 + 1) * CAP]
-
-
-def fold_faces(table_grad, from_low, from_high, face_rows):
+        out_ref[g, :C, :] = total[(g // 2) * C : (g // 2 + 1) * C, (g % 2) * CAP : (g % 2 + 1) * CAP]
+        out_ref[g, C:, :] = share
+
+
+def fold_faces(table_grad, from_low, from_high, face_rows, parts):
     return pl.pallas_call(
         fold_kernel,
-        out_shape=jax.ShapeDtypeStruct((GROUPS, C, CAP), BF),
+        out_shape=jax.ShapeDtypeStruct((GROUPS, C + LANES, CAP), BF),
         scratch_shapes=[pltpu.VMEM((BANKS * C, 2 * F), BF)],
         compiler_params=pltpu.CompilerParams(vmem_limit_bytes=16 << 20),
         name="fold",
-    )(table_grad, from_low, from_high, face_rows)
-
-
-def take_back_kernel(back_ref, owner_ref, slot_ref, out_ref):
-    table = back_ref[...].reshape(GROUPS * C, CAP)
+    )(table_grad, from_low, from_high, face_rows, parts)
+
+
+def finish_kernel(scale, back_ref, owner_ref, slot_ref, out_ref, wg_ref, flat_ref):
+    table = back_ref[:, :C, :].reshape(GROUPS * C, CAP)
     for b in range(R // LO):
         cols = slice(b * LO, (b + 1) * LO)
         product = jnp.dot(table, onehot_rows(slot_ref[:, cols], CAP), preferred_element_type=F32)
         out_ref[:, cols] = select_banks(product, owner_ref[:, cols], GROUPS).astype(BF)
-
-
-def take_back(returned, owner, slot):
-    return pl.pallas_call(
-        take_back_kernel,
-        out_shape=jax.ShapeDtypeStruct((C, R), BF),
-        compiler_params=pltpu.CompilerParams(vmem_limit_bytes=16 << 20),
-        name="take_back",
+    for t in range(TILES + 1):
+        for i in range(C // 16):
+            shard, slot = tile_place(i, t)
+            tile = back_ref[shard, C + slot * 16 : C + (slot + 1) * 16, :].astype(F32) * scale
+            flat_ref[i * 16 : (i + 1) * 16, t * LANES : (t + 1) * LANES] = tile
+    for k in range(K):
+        wg_ref[k] = flat_ref[:, k * C : (k + 1) * C]
+
+
+def finish(returned, owner, slot, scale):
+    return pl.pallas_call(
+        functools.partial(finish_kernel, scale),
+        out_shape=(jax.ShapeDtypeStruct((C, R), BF), jax.ShapeDtypeStruct((K, C, C), F32)),
+        scratch_shapes=[pltpu.VMEM((C, (TILES + 1) * LANES), F32)],
+        compiler_params=pltpu.CompilerParams(vmem_limit_bytes=24 << 20),
+        name="finish",
     )(returned, owner, slot)
 
 
@@ -361,18 +356,18 @@
     weight_columns = jnp.transpose(weight, (0, 2, 1)).reshape(K * C, C)
     scatter = functools.partial(scatter_part, kernel_map=kernel_map, weight=weight_columns, grad_pre=grad_pre)
     across = lambda array, axis: lax.all_to_all(array, axis, 0, 0, tiled=True)
-    row_sums = sum_parts(across(weight_part, "sx"))
+    parts = across(weight_part, "sx")
     sums = scatter(0, grad_pre, grad_pre)
-    all_sums = sum_parts(across(row_sums, "sy"))
+    row_sums = sum_parts(sums, parts)
+    parts = across(row_sums, "sy")
     sums = scatter(1, row_sums, sums)
-    parts = across(all_sums, "sx")
-    table_grad, to_low, to_high = scatter(2, all_sums, sums)
+    table_grad, to_low, to_high = scatter(2, parts, sums)
     from_low = lax.ppermute(to_high, "sy", up)
     from_high = lax.ppermute(to_low, "sy", down)
-    owned_grad = fold_faces(table_grad, from_low, from_high, face_list)
-    returned = lax.all_to_all(owned_grad, "sx", 0, 0, tiled=True)
-    point_grad = take_back(returned, owner, slot)
-    weight_grad = unpack_weight(parts, 1.0 / math.sqrt(GROUPS * side * V))
+    owned_grad = fold_faces(table_grad, from_low, from_high, face_list, parts)
+    returned = across(owned_grad, "sx")
+    scale = 1.0 / math.sqrt(GROUPS * side * V)
+    point_grad, weight_grad = finish(returned, owner, slot, scale)
     return (output[None, None], point_grad[None, None], weight_grad)
 
 

time: 167 us -> 159 us (0.952); the launches traced: 166 us -> 156 us
  waiting for transfers between devices: 26.1 us -> 12.9 us
  blocking collectives: 28 us -> 37.9 us
  starting transfers between devices: 30.2 us -> 23.8 us
  Pallas kernels: 77.5 us -> 74.9 us
  local copies, waits for them, and re-layouts: 3.31 us -> 5.3 us
    all_to_all x3 -> x2, waiting for transfers between devices: 19.8 us -> 7.52 us  [body(): across = lambda array, axis: lax.all_to_all(array, axis, 0, 0, tiled=True)]
    all_to_all x1, blocking collectives: 11.4 us -> 21.4 us  [body(): across = lambda array, axis: lax.all_to_all(array, axis, 0, 0, tiled=True)]
    all_to_all x3 -> x2, starting transfers between devices: 17.4 us -> 12.2 us  [body(): across = lambda array, axis: lax.all_to_all(array, axis, 0, 0, tiled=True)]
    unnamed x18 -> x22, local copies, waits for them, and re-layouts: 2.32 us -> 4.31 us
    pallas_call x5 -> x3, Pallas kernels: 5.39 us -> 3.4 us  [the longest x1 2.1 us: finish(): pl.pallas_call(functools.partial(finish_kernel, scale), out_shape=(jax.Sh...]
  transfers between devices with their start and end apart: 7 -> 6, of which waited for: 4 -> 3; matrix products, arithmetic and copies ran while one was open for 1% -> 1% of each run, Pallas kernels for 17% -> 17%
where the time goes in v5:
time: 159 us; the launch traced here: 156 us
  Pallas kernels  74.9 us (47%)
  blocking collectives  37.9 us (24%)
  starting transfers between devices  23.8 us (15%)
  waiting for transfers between devices  12.9 us (8%)
  local copies, waits for them, and re-layouts  5.3 us (3%)
    pallas_call x3, Pallas kernels, scatter_part(): pl.pallas_call(functools.partial(scatter_kernel, part > 0, last), grid=(s...  34.8 us
    pallas_call x1, Pallas kernels, forward_pass(): pl.pallas_call(forward_kernel, grid=(V // FORWARD_VB,), in_specs=[whole(G...  34.5 us
    all_to_all x1, blocking collectives, body(): across = lambda array, axis: lax.all_to_all(array, axis, 0, 0, tiled=True)  21.4 us
    all_to_all x1, blocking collectives, body(): owned = lax.all_to_all(outgoing, 'sx', 0, 0, tiled=True)  16.6 us
    all_to_all x2, starting transfers between devices, body(): across = lambda array, axis: lax.all_to_all(array, axis, 0, 0, tiled=True)  12.2 us
    all_to_all x2, waiting for transfers between devices, body(): across = lambda array, axis: lax.all_to_all(array, axis, 0, 0, tiled=True)  7.52 us
    ppermute x1, starting transfers between devices, body(): ghost_low = lax.ppermute(upper, 'sy', up)  5.3 us
    unnamed x22, local copies, waits for them, and re-layouts  4.31 us
  transfers between devices with their start and end apart: 6, of which 3 were waited for; matrix products, arithmetic and copies ran while one was open for 1% of the time, Pallas kernels for 17%

profile of v5, /device:TPU:1, one launch (start us, length us, event | category | flops | bytes accessed | tf_op | source)
XLA Modules:
  0.0 155.9 jit_solution(7605770096123032357)
XLA Ops:
  0.6 0.0 copy-start
  0.6 0.9 copy-done
  1.6 0.0 copy-start.1
  1.6 0.7 copy-done.1
  2.2 0.0 copy-start.10
  2.2 1.6 %place.1 = (bf16[16,96,128]{2,1,0:T(8,128)(2,1)S(1)}, s32[1,1024]{1,0:T(1,128)S(1)}) custom-call(bf16[96,1024]{1,0:T(8,128)(2,1)S(1)} %bitcast.14, s32[1,1024]{1,0:T(1,128)S(1)} %bitcast.15), custom_call_target="tpu_custom_call" | custom-call | tf_op jit(solution)/shard_map/place/pallas_call | solution.py:91
  3.9 16.6 %all_to_all.20.owned_ref = bf16[16,96,128]{2,1,0:T(8,128)(2,1)S(1)} all-to-all(bf16[16,96,128]{2,1,0:T(8,128)(2,1)S(1)} %get-tuple-element.15), channel_id=1, replica_groups=mesh['sx'=16,'sy'=16] {'sx'}, dimensions={0} | all-to-all | bytes 786432 | tf_op jit(solution)/shard_map/all_to_all | solution.py:348
  20.4 0.0 copy-start.3
  20.4 0.7 copy-done.3
  21.1 0.6 faces.1
  21.7 5.3 %collective-permute-start = (bf16[96,256]{1,0:T(8,128)(2,1)S(1)}, bf16[96,256]{1,0:T(8,128)(2,1)S(1)}, u32[]{:S(2)}, u32[]{:S(2)}) collective-permute-start(bf16[96,256]{1,0:T(8,128)(2,1)S(1)} %get-tuple-element.16), channel_id=1, source_target_pairs={{0,1},{1,2},{2,3},{3,4},{4,5},{5,6},{6,7},{7,8},{8,9},{9,10},{10,1... | collective-permute-start | bytes 147464 | tf_op jit(solution)/shard_map/ppermute | solution.py:350
  27.0 1.9 %collective-permute-start.1 = (bf16[96,256]{1,0:T(8,128)(2,1)S(1)}, bf16[96,256]{1,0:T(8,128)(2,1)S(1)}, u32[]{:S(2)}, u32[]{:S(2)}) collective-permute-start(bf16[96,256]{1,0:T(8,128)(2,1)S(1)} %get-tuple-element.17), channel_id=1, source_target_pairs={{1,0},{2,1},{3,2},{4,3},{5,4},{6,5},{7,6},{8,7},{9,8},{10,9},{11,1... | collective-permute-start | bytes 147464 | tf_op jit(solution)/shard_map/ppermute | solution.py:351
  28.9 0.0 copy-done.10
  28.9 0.3 copy.11
  29.3 0.0 copy-start.5
  29.3 0.0 copy-start.6
  29.3 0.3 copy.12.weight_ref
  29.6 0.3 copy.13
  30.0 0.0 collective-permute-done.low_ref
  30.0 2.4 %collective-permute-done.1.high_ref = bf16[96,256]{1,0:T(8,128)(2,1)S(1)} collective-permute-done((bf16[96,256]{1,0:T(8,128)(2,1)S(1)}, bf16[96,256]{1,0:T(8,128)(2,1)S(1)}, u32[]{:S(2)}, u32[]{:S(2)}) %collective-permute-start.1) | collective-permute-done | bytes 49184 | tf_op jit(solution)/shard_map/ppermute | solution.py:351
  32.4 0.0 copy-done.5
  32.4 0.0 copy-done.6
  32.4 34.5 %gather_forward.1 = (bf16[96,2048]{1,0:T(8,128)(2,1)}, bf16[96,2048]{1,0:T(8,128)(2,1)S(1)}, bf16[16,128,128]{2,1,0:T(8,128)(2,1)}) custom-call(bf16[16,96,128]{2,1,0:T(8,128)(2,1)S(1)} %all_to_all.20.owned_ref, bf16[96,256]{1,0:T(8,128)(2,1)S(1)} %collective-permute-done.low_ref, bf16[96,256]{1,0:T(8,128)(2,1)S(1)} %collective-permute-done.1.high_ref, ...), custom_call_target="tpu_custom_call" | custom-call | flops 27179089920 | bytes 4194304 | tf_op jit(solution)/shard_map/gather_forward/pallas_call | solution.py:164
  66.9 0.0 copy-start.7
  66.9 3.6 %all-to-all-start.1 = ((bf16[16,128,128]{2,1,0:T(8,128)(2,1)}), bf16[16,128,128]{2,1,0:T(8,128)(2,1)S(1)}, u32[]{:S(2)}, u32[]{:S(2)}) async-start(bf16[16,128,128]{2,1,0:T(8,128)(2,1)} %get-tuple-element.20), calls=%async_computation.1 | async-start | bytes 1048576 | tf_op jit(solution)/shard_map/all_to_all | solution.py:358
  70.5 17.3 %scatter.3.after_ref.start_ref = f32[960,256]{1,0:T(8,128)S(1)} custom-call(bf16[96,2048]{1,0:T(8,128)(2,1)S(1)} %get-tuple-element.19.after_ref.start_ref.pre_ref, bf16[96,2048]{1,0:T(8,128)(2,1)S(1)} %get-tuple-element.19.after_ref.start_ref.pre_ref, s32[27,1,2048]{2,1,0:T(1,128)S(1)} %bitcast.21, bf16[2592,96]{1,0:T(8,128)(2,1)S(1)} %bitcast.11, ...), custom_call_target="tpu_custom_call" | custom-call | flops 13589544960 | bytes 2097152 | tf_op jit(solution)/shard_map/scatter/pallas_call | solution.py:245
  87.9 0.0 copy-done.7
  87.9 0.0 all-to-all-done.1.parts_ref
  87.9 0.9 sum_parts.1.after_ref
  88.8 8.6 %all-to-all-start.2 = ((bf16[16,128,128]{2,1,0:T(8,128)(2,1)}), bf16[16,128,128]{2,1,0:T(8,128)(2,1)S(1)}, u32[]{:S(2)}, u32[]{:S(2)}) async-start(bf16[16,128,128]{2,1,0:T(8,128)(2,1)} %sum_parts.1.after_ref), calls=%async_computation.2 | async-start | bytes 1048576 | tf_op jit(solution)/shard_map/all_to_all | solution.py:358
  97.4 0.0 copy-start.8
  97.4 1.0 copy-done.8
  98.4 8.6 %scatter.4.start_ref = f32[960,256]{1,0:T(8,128)S(1)} custom-call(bf16[16,128,128]{2,1,0:T(8,128)(2,1)} %sum_parts.1.after_ref, f32[960,256]{1,0:T(8,128)S(1)} %scatter.3.after_ref.start_ref, s32[27,1,2048]{2,1,0:T(1,128)S(1)} %bitcast.22, bf16[2592,96]{1,0:T(8,128)(2,1)S(1)} %bitcast.12, bf16[96,2048]{1,0:T(8,128)(2,1)S(1)} %copy-done.8), custom_call_target="tpu_custom_call" | custom-call | flops 6794772480 | bytes 2097152 | tf_op jit(solution)/shard_map/scatter/pallas_call | solution.py:245
  107.0 0.0 copy-start.4
  107.0 7.5 %all-to-all-done.2.after_ref.parts_ref = bf16[16,128,128]{2,1,0:T(8,128)(2,1)S(1)} async-done(((bf16[16,128,128]{2,1,0:T(8,128)(2,1)}), bf16[16,128,128]{2,1,0:T(8,128)(2,1)S(1)}, u32[]{:S(2)}, u32[]{:S(2)}) %all-to-all-start.2) | async-done | bytes 524320 | tf_op jit(solution)/shard_map/all_to_all | solution.py:358
  114.6 0.0 copy-start.9
  114.6 1.0 copy-done.9
  115.6 8.9 %scatter.5 = (f32[768,256]{1,0:T(8,128)S(1)}, bf16[96,256]{1,0:T(8,128)(2,1)S(1)}, bf16[96,256]{1,0:T(8,128)(2,1)S(1)}) custom-call(bf16[16,128,128]{2,1,0:T(8,128)(2,1)S(1)} %all-to-all-done.2.after_ref.parts_ref, f32[960,256]{1,0:T(8,128)S(1)} %scatter.4.start_ref, s32[27,1,2048]{2,1,0:T(1,128)S(1)} %bitcast.23, bf16[2592,96]{1,0:T(8,128)(2,1)S(1)} %bitcast.13, ...), custom_call_target="tpu_custom_call" | custom-call | flops 6794772480 | bytes 2097152 | tf_op jit(solution)/shard_map/scatter/pallas_call | solution.py:245
  124.4 1.9 %collective-permute-start.2 = (bf16[96,256]{1,0:T(8,128)(2,1)S(1)}, bf16[96,256]{1,0:T(8,128)(2,1)S(1)}, u32[]{:S(2)}, u32[]{:S(2)}) collective-permute-start(bf16[96,256]{1,0:T(8,128)(2,1)S(1)} %get-tuple-element.22), channel_id=1, source_target_pairs={{0,1},{1,2},{2,3},{3,4},{4,5},{5,6},{6,7},{7,8},{8,9},{9,10},{10,1... | collective-permute-start | bytes 147464 | tf_op jit(solution)/shard_map/ppermute | solution.py:365
  126.4 2.4 %collective-permute-start.3 = (bf16[96,256]{1,0:T(8,128)(2,1)S(1)}, bf16[96,256]{1,0:T(8,128)(2,1)S(1)}, u32[]{:S(2)}, u32[]{:S(2)}) collective-permute-start(bf16[96,256]{1,0:T(8,128)(2,1)S(1)} %get-tuple-element.23), channel_id=1, source_target_pairs={{1,0},{2,1},{3,2},{4,3},{5,4},{6,5},{7,6},{8,7},{9,8},{10,9},{11,1... | collective-permute-start | bytes 147464 | tf_op jit(solution)/shard_map/ppermute | solution.py:366
  128.8 0.0 collective-permute-done.2.from_low_ref
  128.8 3.0 %collective-permute-done.3.from_high_ref = bf16[96,256]{1,0:T(8,128)(2,1)S(1)} collective-permute-done((bf16[96,256]{1,0:T(8,128)(2,1)S(1)}, bf16[96,256]{1,0:T(8,128)(2,1)S(1)}, u32[]{:S(2)}, u32[]{:S(2)}) %collective-permute-start.3) | collective-permute-done | bytes 49184 | tf_op jit(solution)/shard_map/ppermute | solution.py:366
  131.8 0.0 copy-done.4
  131.8 0.4 fold.1
  132.2 0.0 copy-start.2
  132.2 21.4 %all_to_all.21.back_ref = bf16[16,224,128]{2,1,0:T(8,128)(2,1)S(1)} all-to-all(bf16[16,224,128]{2,1,0:T(8,128)(2,1)S(1)} %fold.1), channel_id=1, replica_groups=mesh['sx'=16,'sy'=16] {'sx'}, dimensions={0} | all-to-all | bytes 1835008 | tf_op jit(solution)/shard_map/all_to_all | solution.py:358
  153.6 0.0 copy-done.2
  153.6 2.1 %finish.1 = (bf16[96,1024]{1,0:T(8,128)(2,1)}, f32[27,96,96]{2,1,0:T(8,128)}) custom-call(bf16[16,224,128]{2,1,0:T(8,128)(2,1)S(1)} %all_to_all.21.back_ref, s32[1,1024]{1,0:T(1,128)S(1)} %bitcast.16, s32[1,1024]{1,0:T(1,128)S(1)} %get-tuple-element.24.slot_ref), custom_call_target="tpu_custom_call" | custom-call | tf_op jit(solution)/shard_map/finish/pallas_call | solution.py:331
Async XLA Ops:
  0.6 0.9 copy-start
  1.6 0.7 copy-start.1
  2.2 26.7 %copy-start.10 = (bf16[27,96,96]{2,1,0:T(8,128)(2,1)S(1)}, bf16[27,96,96]{2,1,0:T(8,128)(2,1)}, u32[]{:S(2)}) copy-start(bf16[27,96,96]{2,1,0:T(8,128)(2,1)} %param.10) | copy-start | bytes 1492996
  20.4 0.7 copy-start.3
  21.7 8.3 %collective-permute-start = (bf16[96,256]{1,0:T(8,128)(2,1)S(1)}, bf16[96,256]{1,0:T(8,128)(2,1)S(1)}, u32[]{:S(2)}, u32[]{:S(2)}) collective-permute-start(bf16[96,256]{1,0:T(8,128)(2,1)S(1)} %get-tuple-element.16), channel_id=1, source_target_pairs={{0,1},{1,2},{2,3},{3,4},{4,5},{5,6},{6,7},{7,8},{8,9},{9,10},{10,1... | collective-permute-start | bytes 147464 | tf_op jit(solution)/shard_map/ppermute | solution.py:350
  27.0 5.4 %collective-permute-start.1 = (bf16[96,256]{1,0:T(8,128)(2,1)S(1)}, bf16[96,256]{1,0:T(8,128)(2,1)S(1)}, u32[]{:S(2)}, u32[]{:S(2)}) collective-permute-start(bf16[96,256]{1,0:T(8,128)(2,1)S(1)} %get-tuple-element.17), channel_id=1, source_target_pairs={{1,0},{2,1},{3,2},{4,3},{5,4},{6,5},{7,6},{8,7},{9,8},{10,9},{11,1... | collective-permute-start | bytes 147464 | tf_op jit(solution)/shard_map/ppermute | solution.py:351
  29.3 3.1 %copy-start.5 = (bf16[1,1,96,2048]{3,2,1,0:T(8,128)(2,1)S(1)}, bf16[1,1,96,2048]{3,2,1,0:T(8,128)(2,1)}, u32[]{:S(2)}) copy-start(bf16[1,1,96,2048]{3,2,1,0:T(8,128)(2,1)} %param.11) | copy-start | bytes 1179652
  29.3 3.1 %copy-start.6 = (s32[1,1,27,2048]{3,1,2,0:T(1,128)S(1)}, s32[1,1,27,2048]{3,1,2,0:T(1,128)}, u32[]{:S(2)}) copy-start(s32[1,1,27,2048]{3,1,2,0:T(1,128)} %param.8) | copy-start | bytes 663556
  66.9 20.9 %copy-start.7 = (bf16[96,2048]{1,0:T(8,128)(2,1)}, bf16[96,2048]{1,0:T(8,128)(2,1)S(1)}, u32[]{:S(2)}) copy-start(bf16[96,2048]{1,0:T(8,128)(2,1)S(1)} %get-tuple-element.19.after_ref.start_ref.pre_ref) | copy-start | bytes 1179652
  66.9 20.9 %all-to-all-start.1 = ((bf16[16,128,128]{2,1,0:T(8,128)(2,1)}), bf16[16,128,128]{2,1,0:T(8,128)(2,1)S(1)}, u32[]{:S(2)}, u32[]{:S(2)}) async-start(bf16[16,128,128]{2,1,0:T(8,128)(2,1)} %get-tuple-element.20), calls=%async_computation.1 | async-start | bytes 1048576 | tf_op jit(solution)/shard_map/all_to_all | solution.py:358
  88.8 25.8 %all-to-all-start.2 = ((bf16[16,128,128]{2,1,0:T(8,128)(2,1)}), bf16[16,128,128]{2,1,0:T(8,128)(2,1)S(1)}, u32[]{:S(2)}, u32[]{:S(2)}) async-start(bf16[16,128,128]{2,1,0:T(8,128)(2,1)} %sum_parts.1.after_ref), calls=%async_computation.2 | async-start | bytes 1048576 | tf_op jit(solution)/shard_map/all_to_all | solution.py:358
  97.4 1.0 copy-start.8
  107.0 24.7 %copy-start.4 = (s32[1,1,2,256]{3,2,1,0:T(2,128)S(1)}, s32[1,1,2,256]{3,2,1,0:T(2,128)}, u32[]{:S(2)}) copy-start(s32[1,1,2,256]{3,2,1,0:T(2,128)} %param.9) | copy-start | bytes 6148
  114.6 1.0 copy-start.9
  124.4 4.3 %collective-permute-start.2 = (bf16[96,256]{1,0:T(8,128)(2,1)S(1)}, bf16[96,256]{1,0:T(8,128)(2,1)S(1)}, u32[]{:S(2)}, u32[]{:S(2)}) collective-permute-start(bf16[96,256]{1,0:T(8,128)(2,1)S(1)} %get-tuple-element.22), channel_id=1, source_target_pairs={{0,1},{1,2},{2,3},{3,4},{4,5},{5,6},{6,7},{7,8},{8,9},{9,10},{10,1... | collective-permute-start | bytes 147464 | tf_op jit(solution)/shard_map/ppermute | solution.py:365
  126.4 5.4 %collective-permute-start.3 = (bf16[96,256]{1,0:T(8,128)(2,1)S(1)}, bf16[96,256]{1,0:T(8,128)(2,1)S(1)}, u32[]{:S(2)}, u32[]{:S(2)}) collective-permute-start(bf16[96,256]{1,0:T(8,128)(2,1)S(1)} %get-tuple-element.23), channel_id=1, source_target_pairs={{1,0},{2,1},{3,2},{4,3},{5,4},{6,5},{7,6},{8,7},{9,8},{10,9},{11,1... | collective-permute-start | bytes 147464 | tf_op jit(solution)/shard_map/ppermute | solution.py:366
  132.2 21.4 %copy-start.2 = (s32[1,1,1024,1]{2,3,1,0:T(1,128)S(1)}, s32[1,1,1024,1]{2,3,1,0:T(1,128)}, u32[]{:S(2)}) copy-start(s32[1,1,1024,1]{2,3,1,0:T(1,128)} %param.7) | copy-start | bytes 12292

commit v6 on v5

--- a/solution.py
+++ b/solution.py
@@ -20,13 +20,14 @@
 ALL_BANKS = BANKS + 2
 WIDE = 512
 WIDE_BANKS = ALL_BANKS * LO // WIDE
-VB = 512
-FORWARD_VB = 1024
+VB = 256
+FORWARD_VB = 512
 PER_DOT = 3
-PARTS = (2, 1, 1)
+PARTS = (1, 2, 2, 2, 1)
 LANES = 128
 TILES = K * C // LANES
-SHARD_TILES = 8
+SHARD_TILES = 4
+HALF = SHARD_TILES * 16
 
 BF = jnp.bfloat16
 F32 = jnp.float32
@@ -63,7 +64,8 @@
 
 
 def tile_place(i, t):
-    return divmod(i * TILES + t if t < TILES else (C // 16) * TILES + i, SHARD_TILES)
+    rest, slot = divmod(i * TILES + t if t < TILES else (C // 16) * TILES + i, SHARD_TILES)
+    return *divmod(rest, GROUPS), slot
 
 
 def place_kernel(points_ref, owner_ref, out_ref, slot_ref, masked_ref):
@@ -152,10 +154,10 @@
                 block = jnp.concatenate([block, jnp.zeros((C, LANES - block.shape[1]), F32)], axis=1)
             block = block.astype(BF)
             for i in range(C // 16):
-                shard, slot = tile_place(i, t)
-                wg_ref[shard, slot * 16 : (slot + 1) * 16, :] = block[i * 16 : (i + 1) * 16, :]
-        used = (TILES + 1) * (C // 16) - (GROUPS - 1) * SHARD_TILES
-        wg_ref[GROUPS - 1, used * 16 :, :] = jnp.zeros((LANES - used * 16, LANES), BF)
+                half, shard, slot = tile_place(i, t)
+                wg_ref[half, shard, slot * 16 : (slot + 1) * 16, :] = block[i * 16 : (i + 1) * 16, :]
+        used = (TILES + 1) * (C // 16) - (2 * GROUPS - 1) * SHARD_TILES
+        wg_ref[1, GROUPS - 1, used * 16 :, :] = jnp.zeros((HALF - used * 16, LANES), BF)
 
 
 def forward_pass(owned, low, high, kernel_map, weight, cotangent):
@@ -172,18 +174,18 @@
             whole(C, K * C),
             column(C),
         ],
-        out_specs=(column(C), column(C), whole(GROUPS, LANES, LANES)),
+        out_specs=(column(C), column(C), whole(2, GROUPS, HALF, LANES)),
         out_shape=(
             jax.ShapeDtypeStruct((C, V), BF),
             jax.ShapeDtypeStruct((C, V), BF),
-            jax.ShapeDtypeStruct((GROUPS, LANES, LANES), BF),
+            jax.ShapeDtypeStruct((2, GROUPS, HALF, LANES), BF),
         ),
         scratch_shapes=[
             pltpu.VMEM((WIDE_BANKS * C, WIDE), BF),
             pltpu.VMEM((K * C, FORWARD_VB), BF),
             pltpu.VMEM((K * C, C), F32),
         ],
-        compiler_params=pltpu.CompilerParams(vmem_limit_bytes=32 << 20),
+        compiler_params=pltpu.CompilerParams(vmem_limit_bytes=24 << 20),
         cost_estimate=pl.CostEstimate(
             flops=2 * K * V * ALL_BANKS * C * LO, bytes_accessed=4 << 20, transcendentals=C * V
         ),
@@ -255,7 +257,7 @@
         out_specs=out_specs,
         out_shape=out_shape,
         scratch_shapes=scratch,
-        compiler_params=pltpu.CompilerParams(vmem_limit_bytes=32 << 20),
+        compiler_params=pltpu.CompilerParams(vmem_limit_bytes=18 << 20),
         cost_estimate=pl.CostEstimate(
             flops=2 * K * VB * steps * ALL_BANKS * C * LO, bytes_accessed=2 << 20, transcendentals=0
         ),
@@ -263,31 +265,32 @@
     )(after, start, kernel_map, weight, grad_pre)
 
 
-def total_of(parts_ref):
+def sum_parts_kernel(after_ref, parts_ref, out_ref):
     total = parts_ref[0].astype(F32)
-    for g in range(1, GROUPS):
+    for g in range(1, parts_ref.shape[0]):
         total = total + parts_ref[g].astype(F32)
-    return total.astype(BF)
-
-
-def sum_parts_kernel(after_ref, parts_ref, out_ref):
-    total = total_of(parts_ref)
-    for g in range(GROUPS):
-        out_ref[g] = total
-
-
-def sum_parts(after, parts):
+    total = total.astype(BF)
+    if len(out_ref.shape) == len(total.shape):
+        out_ref[...] = total
+    else:
+        for g in range(out_ref.shape[0]):
+            out_ref[g] = total
+
+
+def sum_parts(after, parts, copies=None):
+    shape = parts.shape[1:] if copies is None else (copies, *parts.shape[1:])
     return pl.pallas_call(
         sum_parts_kernel,
         in_specs=[pl.BlockSpec(memory_space=pl.ANY), pl.BlockSpec(memory_space=pltpu.VMEM)],
-        out_shape=jax.ShapeDtypeStruct(parts.shape, BF),
+        out_shape=jax.ShapeDtypeStruct(shape, BF),
         compiler_params=pltpu.CompilerParams(vmem_limit_bytes=8 << 20),
         name="sum_parts",
     )(after, parts)
 
 
-def fold_kernel(grad_ref, from_low_ref, from_high_ref, rows_ref, parts_ref, out_ref, masked_ref):
-    share = total_of(parts_ref)
+def fold_kernel(grad_ref, from_low_ref, from_high_ref, rows_ref, parts_ref, out_ref, both_ref, masked_ref):
+    for half in range(2):
+        both_ref[half] = parts_ref[...]
     hots = []
     for j, part_ref in enumerate((from_low_ref, from_high_ref)):
         rows = rows_ref[j : j + 1, :]
@@ -298,43 +301,45 @@
     )
     total = (grad_ref[...] + folded).astype(BF)
     for g in range(GROUPS):
-        out_ref[g, :C, :] = total[(g // 2) * C : (g // 2 + 1) * C, (g % 2) * CAP : (g % 2 + 1) * CAP]
-        out_ref[g, C:, :] = share
+        out_ref[g] = total[(g // 2) * C : (g // 2 + 1) * C, (g % 2) * CAP : (g % 2 + 1) * CAP]
 
 
 def fold_faces(table_grad, from_low, from_high, face_rows, parts):
     return pl.pallas_call(
         fold_kernel,
-        out_shape=jax.ShapeDtypeStruct((GROUPS, C + LANES, CAP), BF),
+        out_shape=(
+            jax.ShapeDtypeStruct((GROUPS, C, CAP), BF),
+            jax.ShapeDtypeStruct((2, *parts.shape), BF),
+        ),
         scratch_shapes=[pltpu.VMEM((BANKS * C, 2 * F), BF)],
         compiler_params=pltpu.CompilerParams(vmem_limit_bytes=16 << 20),
         name="fold",
     )(table_grad, from_low, from_high, face_rows, parts)
 
 
-def finish_kernel(scale, back_ref, owner_ref, slot_ref, out_ref, wg_ref, flat_ref):
-    table = back_ref[:, :C, :].reshape(GROUPS * C, CAP)
+def finish_kernel(scale, back_ref, owner_ref, slot_ref, parts_ref, out_ref, wg_ref, flat_ref):
+    table = back_ref[...].reshape(GROUPS * C, CAP)
     for b in range(R // LO):
         cols = slice(b * LO, (b + 1) * LO)
         product = jnp.dot(table, onehot_rows(slot_ref[:, cols], CAP), preferred_element_type=F32)
         out_ref[:, cols] = select_banks(product, owner_ref[:, cols], GROUPS).astype(BF)
     for t in range(TILES + 1):
         for i in range(C // 16):
-            shard, slot = tile_place(i, t)
-            tile = back_ref[shard, C + slot * 16 : C + (slot + 1) * 16, :].astype(F32) * scale
+            half, shard, slot = tile_place(i, t)
+            tile = parts_ref[half, shard, slot * 16 : (slot + 1) * 16, :].astype(F32) * scale
             flat_ref[i * 16 : (i + 1) * 16, t * LANES : (t + 1) * LANES] = tile
     for k in range(K):
         wg_ref[k] = flat_ref[:, k * C : (k + 1) * C]
 
 
-def finish(returned, owner, slot, scale):
+def finish(returned, owner, slot, parts, scale):
     return pl.pallas_call(
         functools.partial(finish_kernel, scale),
         out_shape=(jax.ShapeDtypeStruct((C, R), BF), jax.ShapeDtypeStruct((K, C, C), F32)),
         scratch_shapes=[pltpu.VMEM((C, (TILES + 1) * LANES), F32)],
         compiler_params=pltpu.CompilerParams(vmem_limit_bytes=24 << 20),
         name="finish",
-    )(returned, owner, slot)
+    )(returned, owner, slot, parts)
 
 
 def body(points, owners, kernel_maps, face_rows, weight, cotangent):
@@ -355,19 +360,31 @@
     )
     weight_columns = jnp.transpose(weight, (0, 2, 1)).reshape(K * C, C)
     scatter = functools.partial(scatter_part, kernel_map=kernel_map, weight=weight_columns, grad_pre=grad_pre)
-    across = lambda array, axis: lax.all_to_all(array, axis, 0, 0, tiled=True)
-    parts = across(weight_part, "sx")
+
+    def across(array, axis, groups=None):
+        return lax.all_to_all(array, axis, 0, 0, axis_index_groups=groups, tiled=True)
+
+    pairs = [[2 * i, 2 * i + 1] for i in range(side // 2)]
+    chips = [list(range(core, side, 2)) for core in range(2)]
+    parts = across(weight_part, "sy", pairs)
     sums = scatter(0, grad_pre, grad_pre)
-    row_sums = sum_parts(sums, parts)
-    parts = across(row_sums, "sy")
-    sums = scatter(1, row_sums, sums)
-    table_grad, to_low, to_high = scatter(2, parts, sums)
+    pair_sum = sum_parts(sums, parts)
+    parts = across(pair_sum, "sx")
+    sums = scatter(1, pair_sum, sums)
+    row_sums = sum_parts(sums, parts, side // 2)
+    parts = across(row_sums, "sy", chips)
+    sums = scatter(2, row_sums, sums)
+    all_sums = sum_parts(sums, parts, GROUPS)
+    parts = across(all_sums, "sx")
+    sums = scatter(3, all_sums, sums)
+    table_grad, to_low, to_high = scatter(4, parts, sums)
     from_low = lax.ppermute(to_high, "sy", up)
     from_high = lax.ppermute(to_low, "sy", down)
-    owned_grad = fold_faces(table_grad, from_low, from_high, face_list, parts)
+    owned_grad, both = fold_faces(table_grad, from_low, from_high, face_list, parts)
+    parts = across(both, "sy", pairs)
     returned = across(owned_grad, "sx")
     scale = 1.0 / math.sqrt(GROUPS * side * V)
-    point_grad, weight_grad = finish(returned, owner, slot, scale)
+    point_grad, weight_grad = finish(returned, owner, slot, parts, scale)
     return (output[None, None], point_grad[None, None], weight_grad)
 
 

time: 159 us -> 165 us (1.038)
  starting transfers between devices: 23.8 us -> 35.6 us
  waiting for transfers between devices: 12.9 us -> 4.86 us
  local copies, waits for them, and re-layouts: 5.3 us -> 8.34 us
  Pallas kernels: 74.9 us -> 76.8 us
    all_to_all x2 -> x4, starting transfers between devices: 12.2 us -> 21.9 us  [across(): lax.all_to_all(array, axis, 0, 0, axis_index_groups=groups, tiled=True)]
    all_to_all x2 -> x4, waiting for transfers between devices: 7.52 us -> 0.01 us  [across(): lax.all_to_all(array, axis, 0, 0, axis_index_groups=groups, tiled=True)]
    ppermute x1, starting transfers between devices: 1.92 us -> 4.57 us  [body(): from_low = lax.ppermute(to_high, 'sy', up)]
    unnamed x22 -> x26, local copies, waits for them, and re-layouts: 4.31 us -> 6.28 us
    all_to_all x1 -> x2, blocking collectives: 21.4 us -> 20 us  [across(): lax.all_to_all(array, axis, 0, 0, axis_index_groups=groups, tiled=True)]
    pallas_call x3 -> x5, Pallas kernels: 34.8 us -> 34.9 us  [scatter_part(): pl.pallas_call(functools.partial(scatter_kernel, part > 0, last), grid=(s...]
  transfers between devices with their start and end apart: 6 -> 8, of which waited for: 3 -> 2; matrix products, arithmetic and copies ran while one was open for 1% -> 1% of each run, Pallas kernels for 17% -> 19%
where the time goes in v6:
time: 165 us; the launch traced here: 163 us
  Pallas kernels  76.8 us (47%)
  blocking collectives  36.6 us (22%)
  starting transfers between devices  35.6 us (22%)
  local copies, waits for them, and re-layouts  8.34 us (5%)
  waiting for transfers between devices  4.86 us (3%)
    pallas_call x1, Pallas kernels, forward_pass(): pl.pallas_call(forward_kernel, grid=(V // FORWARD_VB,), in_specs=[whole(G...  34.9 us
    pallas_call x5, Pallas kernels, scatter_part(): pl.pallas_call(functools.partial(scatter_kernel, part > 0, last), grid=(s...  34.9 us
    all_to_all x4, starting transfers between devices, across(): lax.all_to_all(array, axis, 0, 0, axis_index_groups=groups, tiled=True)  21.9 us
    all_to_all x2, blocking collectives, across(): lax.all_to_all(array, axis, 0, 0, axis_index_groups=groups, tiled=True)  20 us
    all_to_all x1, blocking collectives, body(): owned = lax.all_to_all(outgoing, 'sx', 0, 0, tiled=True)  16.6 us
    unnamed x26, local copies, waits for them, and re-layouts  6.28 us
    ppermute x1, starting transfers between devices, body(): ghost_low = lax.ppermute(upper, 'sy', up)  5.3 us
    ppermute x1, starting transfers between devices, body(): from_low = lax.ppermute(to_high, 'sy', up)  4.57 us
  transfers between devices with their start and end apart: 8, of which 2 were waited for; matrix products, arithmetic and copies ran while one was open for 1% of the time, Pallas kernels for 19%

profile of v6, /device:TPU:1, one launch (start us, length us, event | category | flops | bytes accessed | tf_op | source)
XLA Modules:
  0.0 163.1 jit_solution(1175328804276570508)
XLA Ops:
  0.6 0.0 copy-start
  0.6 0.9 copy-done
  1.6 0.7 copy-done.1
  2.2 1.6 %place.1 = (bf16[16,96,128]{2,1,0:T(8,128)(2,1)S(1)}, s32[1,1024]{1,0:T(1,128)S(1)}) custom-call(bf16[96,1024]{1,0:T(8,128)(2,1)S(1)} %bitcast.16, s32[1,1024]{1,0:T(1,128)S(1)} %bitcast.17), custom_call_target="tpu_custom_call" | custom-call | tf_op jit(solution)/shard_map/place/pallas_call | solution.py:93
  3.9 16.6 %all_to_all.35.owned_ref = bf16[16,96,128]{2,1,0:T(8,128)(2,1)S(1)} all-to-all(bf16[16,96,128]{2,1,0:T(8,128)(2,1)S(1)} %get-tuple-element.17), channel_id=1, replica_groups=mesh['sx'=16,'sy'=16] {'sx'}, dimensions={0} | all-to-all | bytes 786432 | tf_op jit(solution)/shard_map/all_to_all | solution.py:353
  20.4 0.7 copy-done.3
  21.1 0.6 faces.1
  21.7 5.3 %collective-permute-start = (bf16[96,256]{1,0:T(8,128)(2,1)S(1)}, bf16[96,256]{1,0:T(8,128)(2,1)S(1)}, u32[]{:S(2)}, u32[]{:S(2)}) collective-permute-start(bf16[96,256]{1,0:T(8,128)(2,1)S(1)} %get-tuple-element.18), channel_id=1, source_target_pairs={{0,1},{1,2},{2,3},{3,4},{4,5},{5,6},{6,7},{7,8},{8,9},{9,10},{10,1... | collective-permute-start | bytes 147464 | tf_op jit(solution)/shard_map/ppermute | solution.py:355
  27.0 1.9 %collective-permute-start.1 = (bf16[96,256]{1,0:T(8,128)(2,1)S(1)}, bf16[96,256]{1,0:T(8,128)(2,1)S(1)}, u32[]{:S(2)}, u32[]{:S(2)}) collective-permute-start(bf16[96,256]{1,0:T(8,128)(2,1)S(1)} %get-tuple-element.19), channel_id=1, source_target_pairs={{1,0},{2,1},{3,2},{4,3},{5,4},{6,5},{7,6},{8,7},{9,8},{10,9},{11,1... | collective-permute-start | bytes 147464 | tf_op jit(solution)/shard_map/ppermute | solution.py:356
  28.9 0.3 copy.11
  29.3 0.0 copy-start.5
  29.3 0.0 copy-start.6
  29.3 0.3 copy.12.weight_ref
  29.6 1.4 copy.13
  31.0 0.0 collective-permute-done.low_ref
  31.0 1.4 collective-permute-done.1.high_ref
  32.4 34.9 %gather_forward.1 = (bf16[96,2048]{1,0:T(8,128)(2,1)}, bf16[96,2048]{1,0:T(8,128)(2,1)S(1)}, bf16[2,16,64,128]{3,2,1,0:T(8,128)(2,1)}) custom-call(bf16[16,96,128]{2,1,0:T(8,128)(2,1)S(1)} %all_to_all.35.owned_ref, bf16[96,256]{1,0:T(8,128)(2,1)S(1)} %collective-permute-done.low_ref, bf16[96,256]{1,0:T(8,128)(2,1)S(1)} %collective-permute-done.1.high_ref, ...), custom_call_target="tpu_custom_call" | custom-call | flops 27179089920 | bytes 4194304 | tf_op jit(solution)/shard_map/gather_forward/pallas_call | solution.py:166
  67.3 3.7 %all-to-all-start.1 = ((bf16[2,16,64,128]{3,2,1,0:T(8,128)(2,1)}), bf16[2,16,64,128]{3,2,1,0:T(8,128)(2,1)S(1)}, u32[]{:S(2)}, u32[]{:S(2)}) async-start(bf16[2,16,64,128]{3,2,1,0:T(8,128)(2,1)} %get-tuple-element.22), calls=%async_computation.1 | async-start | bytes 1048576 | tf_op jit(solution)/shard_map/all_to_all | solution.py:365
  71.0 4.3 %scatter.5.after_ref.start_ref = f32[960,256]{1,0:T(8,128)S(1)} custom-call(bf16[96,2048]{1,0:T(8,128)(2,1)S(1)} %get-tuple-element.21.after_ref.start_ref.pre_ref, bf16[96,2048]{1,0:T(8,128)(2,1)S(1)} %get-tuple-element.21.after_ref.start_ref.pre_ref, s32[27,1,2048]{2,1,0:T(1,128)S(1)} %bitcast.23, bf16[2592,96]{1,0:T(8,128)(2,1)S(1)} %bitcast.11, ...), custom_call_target="tpu_custom_call" | custom-call | flops 3397386240 | bytes 2097152 | tf_op jit(solution)/shard_map/scatter/pallas_call | solution.py:247
  75.3 0.0 all-to-all-done.1.parts_ref
  75.4 0.8 sum_parts.3.after_ref
  76.1 3.5 %all-to-all-start.2 = ((bf16[16,64,128]{2,1,0:T(8,128)(2,1)}), bf16[16,64,128]{2,1,0:T(8,128)(2,1)S(1)}, u32[]{:S(2)}, u32[]{:S(2)}) async-start(bf16[16,64,128]{2,1,0:T(8,128)(2,1)} %sum_parts.3.after_ref), calls=%async_computation.2 | async-start | bytes 524288 | tf_op jit(solution)/shard_map/all_to_all | solution.py:365
  79.7 0.0 copy-start.8
  79.7 1.0 copy-done.8
  80.7 8.8 %scatter.6.after_ref.start_ref = f32[960,256]{1,0:T(8,128)S(1)} custom-call(bf16[16,64,128]{2,1,0:T(8,128)(2,1)} %sum_parts.3.after_ref, f32[960,256]{1,0:T(8,128)S(1)} %scatter.5.after_ref.start_ref, s32[27,1,2048]{2,1,0:T(1,128)S(1)} %bitcast.24, bf16[2592,96]{1,0:T(8,128)(2,1)S(1)} %bitcast.12, bf16[96,2048]{1,0:T(8,128)(2,1)S(1)} %copy-done.8), custom_call_target="tpu_custom_call" | custom-call | flops 6794772480 | bytes 2097152 | tf_op jit(solution)/shard_map/scatter/pallas_call | solution.py:247
  89.4 0.0 all-to-all-done.2.parts_ref
  89.4 0.7 sum_parts.4.after_ref
  90.1 8.1 %all-to-all-start.3 = ((bf16[8,64,128]{2,1,0:T(8,128)(2,1)}), bf16[8,64,128]{2,1,0:T(8,128)(2,1)S(1)}, u32[]{:S(2)}, u32[]{:S(2)}) async-start(bf16[8,64,128]{2,1,0:T(8,128)(2,1)} %sum_parts.4.after_ref), calls=%async_computation.3 | async-start | bytes 262144 | tf_op jit(solution)/shard_map/all_to_all | solution.py:365
  98.2 1.0 copy-done.9
  99.2 8.8 %scatter.7.after_ref.start_ref = f32[960,256]{1,0:T(8,128)S(1)} custom-call(bf16[8,64,128]{2,1,0:T(8,128)(2,1)} %sum_parts.4.after_ref, f32[960,256]{1,0:T(8,128)S(1)} %scatter.6.after_ref.start_ref, s32[27,1,2048]{2,1,0:T(1,128)S(1)} %bitcast.25, bf16[2592,96]{1,0:T(8,128)(2,1)S(1)} %bitcast.13, bf16[96,2048]{1,0:T(8,128)(2,1)S(1)} %copy-done.9), custom_call_target="tpu_custom_call" | custom-call | flops 6794772480 | bytes 2097152 | tf_op jit(solution)/shard_map/scatter/pallas_call | solution.py:247
  108.0 0.0 all-to-all-done.3.parts_ref
  108.0 0.7 sum_parts.5.after_ref
  108.7 6.6 %all-to-all-start.4 = ((bf16[16,64,128]{2,1,0:T(8,128)(2,1)}), bf16[16,64,128]{2,1,0:T(8,128)(2,1)S(1)}, u32[]{:S(2)}, u32[]{:S(2)}) async-start(bf16[16,64,128]{2,1,0:T(8,128)(2,1)} %sum_parts.5.after_ref), calls=%async_computation.4 | async-start | bytes 524288 | tf_op jit(solution)/shard_map/all_to_all | solution.py:365
  115.3 0.0 copy-start.10
  115.4 1.0 copy-done.10
  116.3 8.8 %scatter.8.start_ref = f32[960,256]{1,0:T(8,128)S(1)} custom-call(bf16[16,64,128]{2,1,0:T(8,128)(2,1)} %sum_parts.5.after_ref, f32[960,256]{1,0:T(8,128)S(1)} %scatter.7.after_ref.start_ref, s32[27,1,2048]{2,1,0:T(1,128)S(1)} %bitcast.26, bf16[2592,96]{1,0:T(8,128)(2,1)S(1)} %bitcast.14, bf16[96,2048]{1,0:T(8,128)(2,1)S(1)} %copy-done.10), custom_call_target="tpu_custom_call" | custom-call | flops 6794772480 | bytes 2097152 | tf_op jit(solution)/shard_map/scatter/pallas_call | solution.py:247
  125.1 0.0 copy-start.4
  125.1 0.0 all-to-all-done.4.after_ref.parts_ref
  125.2 1.0 copy-done.11
  126.1 4.3 %scatter.9 = (f32[768,256]{1,0:T(8,128)S(1)}, bf16[96,256]{1,0:T(8,128)(2,1)S(1)}, bf16[96,256]{1,0:T(8,128)(2,1)S(1)}) custom-call(bf16[16,64,128]{2,1,0:T(8,128)(2,1)S(1)} %all-to-all-done.4.after_ref.parts_ref, f32[960,256]{1,0:T(8,128)S(1)} %scatter.8.start_ref, s32[27,1,2048]{2,1,0:T(1,128)S(1)} %bitcast.27, bf16[2592,96]{1,0:T(8,128)(2,1)S(1)} %bitcast.15, ...), custom_call_target="tpu_custom_call" | custom-call | flops 3397386240 | bytes 2097152 | tf_op jit(solution)/shard_map/scatter/pallas_call | solution.py:247
  130.5 4.6 %collective-permute-start.2 = (bf16[96,256]{1,0:T(8,128)(2,1)S(1)}, bf16[96,256]{1,0:T(8,128)(2,1)S(1)}, u32[]{:S(2)}, u32[]{:S(2)}) collective-permute-start(bf16[96,256]{1,0:T(8,128)(2,1)S(1)} %get-tuple-element.24), channel_id=1, source_target_pairs={{0,1},{1,2},{2,3},{3,4},{4,5},{5,6},{6,7},{7,8},{8,9},{9,10},{10,1... | collective-permute-start | bytes 147464 | tf_op jit(solution)/shard_map/ppermute | solution.py:381
  135.0 1.9 %collective-permute-start.3 = (bf16[96,256]{1,0:T(8,128)(2,1)S(1)}, bf16[96,256]{1,0:T(8,128)(2,1)S(1)}, u32[]{:S(2)}, u32[]{:S(2)}) collective-permute-start(bf16[96,256]{1,0:T(8,128)(2,1)S(1)} %get-tuple-element.25), channel_id=1, source_target_pairs={{1,0},{2,1},{3,2},{4,3},{5,4},{6,5},{7,6},{8,7},{9,8},{10,9},{11,1... | collective-permute-start | bytes 147464 | tf_op jit(solution)/shard_map/ppermute | solution.py:382
  137.0 0.0 collective-permute-done.2.from_low_ref
  137.0 3.5 %collective-permute-done.3.from_high_ref = bf16[96,256]{1,0:T(8,128)(2,1)S(1)} collective-permute-done((bf16[96,256]{1,0:T(8,128)(2,1)S(1)}, bf16[96,256]{1,0:T(8,128)(2,1)S(1)}, u32[]{:S(2)}, u32[]{:S(2)}) %collective-permute-start.3) | collective-permute-done | bytes 49184 | tf_op jit(solution)/shard_map/ppermute | solution.py:382
  140.5 0.5 fold.1
  140.9 3.8 %all_to_all.36.parts_ref = bf16[2,16,64,128]{3,2,1,0:T(8,128)(2,1)S(1)} all-to-all(bf16[2,16,64,128]{3,2,1,0:T(8,128)(2,1)S(1)} %get-tuple-element.28), channel_id=1, replica_groups={{0,1},{2,3},{4,5},{6,7},{8,9},{10,11},{12,13},{14,15},{16,17},{18,19},{..., dimensions={0} | all-to-all | bytes 1048576 | tf_op jit(solution)/shard_map/all_to_all | solution.py:365
  144.7 16.2 %all_to_all.37.back_ref = bf16[16,96,128]{2,1,0:T(8,128)(2,1)S(1)} all-to-all(bf16[16,96,128]{2,1,0:T(8,128)(2,1)S(1)} %get-tuple-element.26), channel_id=1, replica_groups=mesh['sx'=16,'sy'=16] {'sx'}, dimensions={0} | all-to-all | bytes 786432 | tf_op jit(solution)/shard_map/all_to_all | solution.py:365
  161.0 2.1 %finish.1 = (bf16[96,1024]{1,0:T(8,128)(2,1)}, f32[27,96,96]{2,1,0:T(8,128)}) custom-call(bf16[16,96,128]{2,1,0:T(8,128)(2,1)S(1)} %all_to_all.37.back_ref, s32[1,1024]{1,0:T(1,128)S(1)} %bitcast.18, s32[1,1024]{1,0:T(1,128)S(1)} %get-tuple-element.27.slot_ref, bf16[2,16,64,128]{3,2,1,0:T(8,128)(2,1)S(1)} %all_to_all.36.parts_ref), custom_call_target="tpu_custom_call" | custom-call | tf_op jit(solution)/shard_map/finish/pallas_call | solution.py:336
  (13 shorter events, 0.0 us)
Async XLA Ops:
  0.6 0.9 copy-start
  1.6 0.7 copy-start.1
  2.2 26.7 %copy-start.12 = (bf16[27,96,96]{2,1,0:T(8,128)(2,1)S(1)}, bf16[27,96,96]{2,1,0:T(8,128)(2,1)}, u32[]{:S(2)}) copy-start(bf16[27,96,96]{2,1,0:T(8,128)(2,1)} %param.10) | copy-start | bytes 1492996
  20.4 0.7 copy-start.3
  21.7 9.3 %collective-permute-start = (bf16[96,256]{1,0:T(8,128)(2,1)S(1)}, bf16[96,256]{1,0:T(8,128)(2,1)S(1)}, u32[]{:S(2)}, u32[]{:S(2)}) collective-permute-start(bf16[96,256]{1,0:T(8,128)(2,1)S(1)} %get-tuple-element.18), channel_id=1, source_target_pairs={{0,1},{1,2},{2,3},{3,4},{4,5},{5,6},{6,7},{7,8},{8,9},{9,10},{10,1... | collective-permute-start | bytes 147464 | tf_op jit(solution)/shard_map/ppermute | solution.py:355
  27.0 5.4 %collective-permute-start.1 = (bf16[96,256]{1,0:T(8,128)(2,1)S(1)}, bf16[96,256]{1,0:T(8,128)(2,1)S(1)}, u32[]{:S(2)}, u32[]{:S(2)}) collective-permute-start(bf16[96,256]{1,0:T(8,128)(2,1)S(1)} %get-tuple-element.19), channel_id=1, source_target_pairs={{1,0},{2,1},{3,2},{4,3},{5,4},{6,5},{7,6},{8,7},{9,8},{10,9},{11,1... | collective-permute-start | bytes 147464 | tf_op jit(solution)/shard_map/ppermute | solution.py:356
  29.3 3.1 %copy-start.5 = (bf16[1,1,96,2048]{3,2,1,0:T(8,128)(2,1)S(1)}, bf16[1,1,96,2048]{3,2,1,0:T(8,128)(2,1)}, u32[]{:S(2)}) copy-start(bf16[1,1,96,2048]{3,2,1,0:T(8,128)(2,1)} %param.11) | copy-start | bytes 1179652
  29.3 3.1 %copy-start.6 = (s32[1,1,27,2048]{3,1,2,0:T(1,128)S(1)}, s32[1,1,27,2048]{3,1,2,0:T(1,128)}, u32[]{:S(2)}) copy-start(s32[1,1,27,2048]{3,1,2,0:T(1,128)} %param.8) | copy-start | bytes 663556
  67.3 8.0 %copy-start.7 = (bf16[96,2048]{1,0:T(8,128)(2,1)}, bf16[96,2048]{1,0:T(8,128)(2,1)S(1)}, u32[]{:S(2)}) copy-start(bf16[96,2048]{1,0:T(8,128)(2,1)S(1)} %get-tuple-element.21.after_ref.start_ref.pre_ref) | copy-start | bytes 1179652
  67.3 8.0 %all-to-all-start.1 = ((bf16[2,16,64,128]{3,2,1,0:T(8,128)(2,1)}), bf16[2,16,64,128]{3,2,1,0:T(8,128)(2,1)S(1)}, u32[]{:S(2)}, u32[]{:S(2)}) async-start(bf16[2,16,64,128]{3,2,1,0:T(8,128)(2,1)} %get-tuple-element.22), calls=%async_computation.1 | async-start | bytes 1048576 | tf_op jit(solution)/shard_map/all_to_all | solution.py:365
  76.1 13.3 %all-to-all-start.2 = ((bf16[16,64,128]{2,1,0:T(8,128)(2,1)}), bf16[16,64,128]{2,1,0:T(8,128)(2,1)S(1)}, u32[]{:S(2)}, u32[]{:S(2)}) async-start(bf16[16,64,128]{2,1,0:T(8,128)(2,1)} %sum_parts.3.after_ref), calls=%async_computation.2 | async-start | bytes 524288 | tf_op jit(solution)/shard_map/all_to_all | solution.py:365
  79.7 1.0 copy-start.8
  90.1 17.9 %all-to-all-start.3 = ((bf16[8,64,128]{2,1,0:T(8,128)(2,1)}), bf16[8,64,128]{2,1,0:T(8,128)(2,1)S(1)}, u32[]{:S(2)}, u32[]{:S(2)}) async-start(bf16[8,64,128]{2,1,0:T(8,128)(2,1)} %sum_parts.4.after_ref), calls=%async_computation.3 | async-start | bytes 262144 | tf_op jit(solution)/shard_map/all_to_all | solution.py:365
  98.2 1.0 copy-start.9
  108.7 16.4 %all-to-all-start.4 = ((bf16[16,64,128]{2,1,0:T(8,128)(2,1)}), bf16[16,64,128]{2,1,0:T(8,128)(2,1)S(1)}, u32[]{:S(2)}, u32[]{:S(2)}) async-start(bf16[16,64,128]{2,1,0:T(8,128)(2,1)} %sum_parts.5.after_ref), calls=%async_computation.4 | async-start | bytes 524288 | tf_op jit(solution)/shard_map/all_to_all | solution.py:365
  115.3 1.0 copy-start.10
  125.1 15.3 %copy-start.4 = (s32[1,1,2,256]{3,2,1,0:T(2,128)S(1)}, s32[1,1,2,256]{3,2,1,0:T(2,128)}, u32[]{:S(2)}) copy-start(s32[1,1,2,256]{3,2,1,0:T(2,128)} %param.9) | copy-start | bytes 6148
  125.1 1.0 copy-start.11
  130.5 6.5 %collective-permute-start.2 = (bf16[96,256]{1,0:T(8,128)(2,1)S(1)}, bf16[96,256]{1,0:T(8,128)(2,1)S(1)}, u32[]{:S(2)}, u32[]{:S(2)}) collective-permute-start(bf16[96,256]{1,0:T(8,128)(2,1)S(1)} %get-tuple-element.24), channel_id=1, source_target_pairs={{0,1},{1,2},{2,3},{3,4},{4,5},{5,6},{6,7},{7,8},{8,9},{9,10},{10,1... | collective-permute-start | bytes 147464 | tf_op jit(solution)/shard_map/ppermute | solution.py:381
  135.0 5.4 %collective-permute-start.3 = (bf16[96,256]{1,0:T(8,128)(2,1)S(1)}, bf16[96,256]{1,0:T(8,128)(2,1)S(1)}, u32[]{:S(2)}, u32[]{:S(2)}) collective-permute-start(bf16[96,256]{1,0:T(8,128)(2,1)S(1)} %get-tuple-element.25), channel_id=1, source_target_pairs={{1,0},{2,1},{3,2},{4,3},{5,4},{6,5},{7,6},{8,7},{9,8},{10,9},{11,1... | collective-permute-start | bytes 147464 | tf_op jit(solution)/shard_map/ppermute | solution.py:382
  140.5 20.5 %copy-start.2 = (s32[1,1,1024,1]{2,3,1,0:T(1,128)S(1)}, s32[1,1,1024,1]{2,3,1,0:T(1,128)}, u32[]{:S(2)}) copy-start(s32[1,1,1024,1]{2,3,1,0:T(1,128)} %param.7) | copy-start | bytes 12292

commit v7 on v5

--- a/solution.py
+++ b/solution.py
@@ -20,10 +20,11 @@
 ALL_BANKS = BANKS + 2
 WIDE = 512
 WIDE_BANKS = ALL_BANKS * LO // WIDE
-VB = 512
-FORWARD_VB = 1024
+VB = 256
+FORWARD_VB = 512
+MAIN = 80
 PER_DOT = 3
-PARTS = (2, 1, 1)
+PARTS = (3, 3, 2)
 LANES = 128
 TILES = K * C // LANES
 SHARD_TILES = 8
@@ -43,14 +44,34 @@
     return jnp.where(row == rows16(low)[None], BF(1), BF(0)).reshape(rows, n)
 
 
-def select_banks(product, bank, banks):
+def select_banks(product, bank, banks, channels=C):
     n = bank.shape[-1]
     bank8 = jnp.broadcast_to(bank, (8, n))
-    kept = jnp.zeros((C // 8, 8, n), F32)
+    kept = jnp.zeros((channels // 8, 8, n), F32)
     for a in range(banks):
-        part = product[a * C : (a + 1) * C].reshape(C // 8, 8, n)
+        part = product[a * channels : (a + 1) * channels].reshape(channels // 8, 8, n)
         kept = jnp.where((bank8 == a)[None], part, kept)
-    return kept.reshape(C, n)
+    return kept.reshape(channels, n)
+
+
+LANE_GATHER = lax.GatherDimensionNumbers(
+    offset_dims=(),
+    collapsed_slice_dims=(1,),
+    start_index_map=(1,),
+    operand_batching_dims=(0,),
+    start_indices_batching_dims=(0,),
+)
+
+
+def gather_lanes(tiles_ref, index):
+    lane, tile = rows16(index & (CAP - 1)), rows16(index >> 7)
+    kept = jnp.zeros((16, CAP), BF)
+    for t in range(tiles_ref.shape[0]):
+        read = lax.gather(
+            tiles_ref[t], lane[..., None], LANE_GATHER, (1, 1), mode=lax.GatherScatterMode.PROMISE_IN_BOUNDS
+        )
+        kept = jnp.where(tile == t, read, kept)
+    return kept
 
 
 def masked_banks(values, bank, banks, out_ref, column):
@@ -118,7 +139,7 @@
 
 
 def forward_kernel(
-    owned_ref, low_ref, high_ref, map_ref, weight_ref, cot_ref, out_ref, pre_ref, wg_ref, table_ref, picked_ref, acc_ref
+    owned_ref, low_ref, high_ref, map_ref, weight_ref, cot_ref, out_ref, pre_ref, wg_ref, table_ref, tail_ref, picked_ref, acc_ref
 ):
     step = pl.program_id(0)
 
@@ -126,16 +147,25 @@
     def _():
         per = WIDE // CAP
         for g in range(GROUPS):
-            table_ref[(g // per) * C : (g // per + 1) * C, (g % per) * CAP : (g % per + 1) * CAP] = owned_ref[g]
-        table_ref[(WIDE_BANKS - 1) * C :, :F] = low_ref[...]
-        table_ref[(WIDE_BANKS - 1) * C :, F:] = high_ref[...]
+            rows = slice((g // per) * MAIN, (g // per + 1) * MAIN)
+            table_ref[rows, (g % per) * CAP : (g % per + 1) * CAP] = owned_ref[g, :MAIN, :]
+            tail_ref[g] = owned_ref[g, MAIN:, :]
+        table_ref[(WIDE_BANKS - 1) * MAIN :, :F] = low_ref[:MAIN, :]
+        table_ref[(WIDE_BANKS - 1) * MAIN :, F:] = high_ref[:MAIN, :]
+        for j, ghost_ref in enumerate((low_ref, high_ref)):
+            for i in range(F // CAP):
+                tail_ref[GROUPS + j * (F // CAP) + i] = ghost_ref[MAIN:, i * CAP : (i + 1) * CAP]
         acc_ref[...] = jnp.zeros_like(acc_ref)
 
     table = table_ref[...]
     for k in range(K):
         index = map_ref[k]
         product = jnp.dot(table, onehot_rows(index & (WIDE - 1), WIDE), preferred_element_type=F32)
-        picked_ref[k * C : (k + 1) * C, :] = select_banks(product, index >> 9, WIDE_BANKS).astype(BF)
+        main = select_banks(product, index >> 9, WIDE_BANKS, MAIN)
+        picked_ref[k * C : k * C + MAIN, :] = main.astype(BF)
+        for i in range(FORWARD_VB // CAP):
+            cols = slice(i * CAP, (i + 1) * CAP)
+            picked_ref[k * C + MAIN : (k + 1) * C, cols] = gather_lanes(tail_ref, index[:, cols])
     preact = jnp.dot(weight_ref[...], picked_ref[...], preferred_element_type=F32)
     logistic = jax.nn.sigmoid(preact)
     out_ref[...] = (preact * logistic).astype(BF)
@@ -179,7 +209,8 @@
             jax.ShapeDtypeStruct((GROUPS, LANES, LANES), BF),
         ),
         scratch_shapes=[
-            pltpu.VMEM((WIDE_BANKS * C, WIDE), BF),
+            pltpu.VMEM((WIDE_BANKS * MAIN, WIDE), BF),
+            pltpu.VMEM((V // CAP + 2 * F // CAP, C - MAIN, CAP), BF),
             pltpu.VMEM((K * C, FORWARD_VB), BF),
             pltpu.VMEM((K * C, C), F32),
         ],
@@ -191,32 +222,38 @@
     )(owned, low, high, kernel_map, weight, cotangent)
 
 
-def scatter_step(map_ref, weight_ref, pre_ref, acc_ref, spread_ref, masked_ref):
+def bank_rows(values, bank):
+    n = bank.shape[-1]
+    bank16 = rows16(bank)
+    values = values.reshape(C // 16, 16, n)
+    banks = [jnp.where((bank16 == a)[None], values, BF(0)).reshape(C, n) for a in range(ALL_BANKS)]
+    return jnp.concatenate(banks, axis=0)
+
+
+def scatter_step(map_ref, weight_ref, pre_ref, acc_ref, spread_ref):
     spread_ref[...] = jnp.dot(weight_ref[...], pre_ref[...], preferred_element_type=F32).astype(BF)
-    for turn in range(K // PER_DOT):
-        hots = []
-        slot = masked_ref.at[turn % 2]
-        for j in range(PER_DOT):
-            k = turn * PER_DOT + j
+    for first in range(0, K, PER_DOT):
+        spreads, hots = [], []
+        for k in range(first, first + PER_DOT):
             index = map_ref[k]
-            masked_banks(spread_ref[k * C : (k + 1) * C, :], index >> 8, ALL_BANKS, slot, j * VB)
+            spreads.append(bank_rows(spread_ref[k * C : (k + 1) * C, :], index >> 8))
             hots.append(onehot_rows(index & (LO - 1), LO))
         acc_ref[...] += lax.dot_general(
-            slot[...], jnp.concatenate(hots, axis=1), NT, preferred_element_type=F32
+            jnp.concatenate(spreads, axis=1), jnp.concatenate(hots, axis=1), NT, preferred_element_type=F32
         )
 
 
 def scatter_kernel(has_start, has_faces, after_ref, start_ref, map_ref, weight_ref, pre_ref, *refs):
     if has_faces:
-        own_ref, low_ref, high_ref, spread_ref, masked_ref, acc_ref = refs
+        own_ref, low_ref, high_ref, spread_ref, acc_ref = refs
     else:
-        acc_ref, spread_ref, masked_ref = refs
+        acc_ref, spread_ref = refs
 
     @pl.when(pl.program_id(0) == 0)
     def _():
         acc_ref[...] = start_ref[...] if has_start else jnp.zeros_like(acc_ref)
 
-    scatter_step(map_ref, weight_ref, pre_ref, acc_ref, spread_ref, masked_ref)
+    scatter_step(map_ref, weight_ref, pre_ref, acc_ref, spread_ref)
 
     if has_faces:
 
@@ -230,7 +267,7 @@
 def scatter_part(part, after, start, kernel_map, weight, grad_pre):
     whole = lambda *shape: pl.BlockSpec(shape, lambda i: (0,) * len(shape))
     sums = jax.ShapeDtypeStruct((ALL_BANKS * C, LO), F32)
-    scratch = [pltpu.VMEM((K * C, VB), BF), pltpu.VMEM((2, ALL_BANKS * C, PER_DOT * VB), BF)]
+    scratch = [pltpu.VMEM((K * C, VB), BF)]
     at, steps, last = sum(PARTS[:part]), PARTS[part], part == len(PARTS) - 1
     if last:
         out_specs = (whole(BANKS * C, LO), whole(C, F), whole(C, F))
@@ -255,7 +292,7 @@
         out_specs=out_specs,
         out_shape=out_shape,
         scratch_shapes=scratch,
-        compiler_params=pltpu.CompilerParams(vmem_limit_bytes=32 << 20),
+        compiler_params=pltpu.CompilerParams(vmem_limit_bytes=24 << 20),
         cost_estimate=pl.CostEstimate(
             flops=2 * K * VB * steps * ALL_BANKS * C * LO, bytes_accessed=2 << 20, transcendentals=0
         ),

time: 159 us -> 148 us (0.931); the launches traced: 156 us -> 147 us
  waiting for transfers between devices: 12.9 us -> 8.63 us
  Pallas kernels: 74.9 us -> 70.9 us
    all_to_all x2, waiting for transfers between devices: 7.52 us -> 3.2 us  [body(): across = lambda array, axis: lax.all_to_all(array, axis, 0, 0, tiled=True)]
    pallas_call x1, Pallas kernels: 34.5 us -> 30.3 us  [forward_pass(): pl.pallas_call(forward_kernel, grid=(V // FORWARD_VB,), in_specs=[whole(G...]
  transfers between devices with their start and end apart: 6 -> 6, of which waited for: 3 -> 3; matrix products, arithmetic and copies ran while one was open for 1% -> 1% of each run, Pallas kernels for 17% -> 18%
where the time goes in v7:
time: 148 us; the launch traced here: 147 us
  Pallas kernels  70.9 us (48%)
  blocking collectives  37.7 us (25%)
  starting transfers between devices  23.7 us (16%)
  waiting for transfers between devices  8.63 us (6%)
  local copies, waits for them, and re-layouts  5.3 us (4%)
    pallas_call x3, Pallas kernels, scatter_part(): pl.pallas_call(functools.partial(scatter_kernel, part > 0, last), grid=(s...  35 us
    pallas_call x1, Pallas kernels, forward_pass(): pl.pallas_call(forward_kernel, grid=(V // FORWARD_VB,), in_specs=[whole(G...  30.3 us
    all_to_all x1, blocking collectives, body(): across = lambda array, axis: lax.all_to_all(array, axis, 0, 0, tiled=True)  21.2 us
    all_to_all x1, blocking collectives, body(): owned = lax.all_to_all(outgoing, 'sx', 0, 0, tiled=True)  16.6 us
    all_to_all x2, starting transfers between devices, body(): across = lambda array, axis: lax.all_to_all(array, axis, 0, 0, tiled=True)  12.2 us
    ppermute x1, starting transfers between devices, body(): ghost_low = lax.ppermute(upper, 'sy', up)  5.29 us
    unnamed x22, local copies, waits for them, and re-layouts  4.31 us
    all_to_all x2, waiting for transfers between devices, body(): across = lambda array, axis: lax.all_to_all(array, axis, 0, 0, tiled=True)  3.2 us
  transfers between devices with their start and end apart: 6, of which 3 were waited for; matrix products, arithmetic and copies ran while one was open for 1% of the time, Pallas kernels for 18%

profile of v7, /device:TPU:1, one launch (start us, length us, event | category | flops | bytes accessed | tf_op | source)
XLA Modules:
  0.0 147.1 jit_solution(4435472104334270789)
XLA Ops:
  0.6 0.0 copy-start
  0.6 0.9 copy-done
  1.6 0.0 copy-start.1
  1.6 0.7 copy-done.1
  2.2 0.0 copy-start.10
  2.2 1.6 %place.1 = (bf16[16,96,128]{2,1,0:T(8,128)(2,1)S(1)}, s32[1,1024]{1,0:T(1,128)S(1)}) custom-call(bf16[96,1024]{1,0:T(8,128)(2,1)S(1)} %bitcast.14, s32[1,1024]{1,0:T(1,128)S(1)} %bitcast.15), custom_call_target="tpu_custom_call" | custom-call | tf_op jit(solution)/shard_map/place/pallas_call | solution.py:112
  3.9 16.6 %all_to_all.20.owned_ref = bf16[16,96,128]{2,1,0:T(8,128)(2,1)S(1)} all-to-all(bf16[16,96,128]{2,1,0:T(8,128)(2,1)S(1)} %get-tuple-element.15), channel_id=1, replica_groups=mesh['sx'=16,'sy'=16] {'sx'}, dimensions={0} | all-to-all | bytes 786432 | tf_op jit(solution)/shard_map/all_to_all | solution.py:385
  20.4 0.0 copy-start.3
  20.5 0.7 copy-done.3
  21.1 0.5 faces.1
  21.7 5.3 %collective-permute-start = (bf16[96,256]{1,0:T(8,128)(2,1)S(1)}, bf16[96,256]{1,0:T(8,128)(2,1)S(1)}, u32[]{:S(2)}, u32[]{:S(2)}) collective-permute-start(bf16[96,256]{1,0:T(8,128)(2,1)S(1)} %get-tuple-element.16), channel_id=1, source_target_pairs={{0,1},{1,2},{2,3},{3,4},{4,5},{5,6},{6,7},{7,8},{8,9},{9,10},{10,1... | collective-permute-start | bytes 147464 | tf_op jit(solution)/shard_map/ppermute | solution.py:387
  27.0 1.9 %collective-permute-start.1 = (bf16[96,256]{1,0:T(8,128)(2,1)S(1)}, bf16[96,256]{1,0:T(8,128)(2,1)S(1)}, u32[]{:S(2)}, u32[]{:S(2)}) collective-permute-start(bf16[96,256]{1,0:T(8,128)(2,1)S(1)} %get-tuple-element.17), channel_id=1, source_target_pairs={{1,0},{2,1},{3,2},{4,3},{5,4},{6,5},{7,6},{8,7},{9,8},{10,9},{11,1... | collective-permute-start | bytes 147464 | tf_op jit(solution)/shard_map/ppermute | solution.py:388
  28.9 0.0 copy-done.10
  28.9 0.3 copy.11
  29.3 0.0 copy-start.5
  29.3 0.0 copy-start.6
  29.3 0.3 copy.12.weight_ref
  29.6 0.3 copy.13
  30.0 0.0 collective-permute-done.low_ref
  30.0 2.4 %collective-permute-done.1.high_ref = bf16[96,256]{1,0:T(8,128)(2,1)S(1)} collective-permute-done((bf16[96,256]{1,0:T(8,128)(2,1)S(1)}, bf16[96,256]{1,0:T(8,128)(2,1)S(1)}, u32[]{:S(2)}, u32[]{:S(2)}) %collective-permute-start.1) | collective-permute-done | bytes 49184 | tf_op jit(solution)/shard_map/ppermute | solution.py:388
  32.4 0.0 copy-done.5
  32.4 0.0 copy-done.6
  32.4 30.3 %gather_forward.1 = (bf16[96,2048]{1,0:T(8,128)(2,1)}, bf16[96,2048]{1,0:T(8,128)(2,1)S(1)}, bf16[16,128,128]{2,1,0:T(8,128)(2,1)}) custom-call(bf16[16,96,128]{2,1,0:T(8,128)(2,1)S(1)} %all_to_all.20.owned_ref, bf16[96,256]{1,0:T(8,128)(2,1)S(1)} %collective-permute-done.low_ref, bf16[96,256]{1,0:T(8,128)(2,1)S(1)} %collective-permute-done.1.high_ref, ...), custom_call_target="tpu_custom_call" | custom-call | flops 27179089920 | bytes 4194304 | tf_op jit(solution)/shard_map/gather_forward/pallas_call | solution.py:194
  62.7 0.0 copy-start.7
  62.7 3.8 %all-to-all-start.1 = ((bf16[16,128,128]{2,1,0:T(8,128)(2,1)}), bf16[16,128,128]{2,1,0:T(8,128)(2,1)S(1)}, u32[]{:S(2)}, u32[]{:S(2)}) async-start(bf16[16,128,128]{2,1,0:T(8,128)(2,1)} %get-tuple-element.20), calls=%async_computation.1 | async-start | bytes 1048576 | tf_op jit(solution)/shard_map/all_to_all | solution.py:395
  66.4 13.1 %scatter.3.after_ref.start_ref = f32[960,256]{1,0:T(8,128)S(1)} custom-call(bf16[96,2048]{1,0:T(8,128)(2,1)S(1)} %get-tuple-element.19.after_ref.start_ref.pre_ref, bf16[96,2048]{1,0:T(8,128)(2,1)S(1)} %get-tuple-element.19.after_ref.start_ref.pre_ref, s32[27,1,2048]{2,1,0:T(1,128)S(1)} %bitcast.21, bf16[2592,96]{1,0:T(8,128)(2,1)S(1)} %bitcast.11, ...), custom_call_target="tpu_custom_call" | custom-call | flops 10192158720 | bytes 2097152 | tf_op jit(solution)/shard_map/scatter/pallas_call | solution.py:282
  79.6 0.0 copy-done.7
  79.6 0.0 all-to-all-done.1.parts_ref
  79.6 0.9 sum_parts.1.after_ref
  80.5 8.4 %all-to-all-start.2 = ((bf16[16,128,128]{2,1,0:T(8,128)(2,1)}), bf16[16,128,128]{2,1,0:T(8,128)(2,1)S(1)}, u32[]{:S(2)}, u32[]{:S(2)}) async-start(bf16[16,128,128]{2,1,0:T(8,128)(2,1)} %sum_parts.1.after_ref), calls=%async_computation.2 | async-start | bytes 1048576 | tf_op jit(solution)/shard_map/all_to_all | solution.py:395
  88.9 0.0 copy-start.8
  88.9 1.0 copy-done.8
  89.9 13.1 %scatter.4.start_ref = f32[960,256]{1,0:T(8,128)S(1)} custom-call(bf16[16,128,128]{2,1,0:T(8,128)(2,1)} %sum_parts.1.after_ref, f32[960,256]{1,0:T(8,128)S(1)} %scatter.3.after_ref.start_ref, s32[27,1,2048]{2,1,0:T(1,128)S(1)} %bitcast.22, bf16[2592,96]{1,0:T(8,128)(2,1)S(1)} %bitcast.12, bf16[96,2048]{1,0:T(8,128)(2,1)S(1)} %copy-done.8), custom_call_target="tpu_custom_call" | custom-call | flops 10192158720 | bytes 2097152 | tf_op jit(solution)/shard_map/scatter/pallas_call | solution.py:282
  103.0 0.0 copy-start.4
  103.0 3.2 %all-to-all-done.2.after_ref.parts_ref = bf16[16,128,128]{2,1,0:T(8,128)(2,1)S(1)} async-done(((bf16[16,128,128]{2,1,0:T(8,128)(2,1)}), bf16[16,128,128]{2,1,0:T(8,128)(2,1)S(1)}, u32[]{:S(2)}, u32[]{:S(2)}) %all-to-all-start.2) | async-done | bytes 524320 | tf_op jit(solution)/shard_map/all_to_all | solution.py:395
  106.2 0.0 copy-start.9
  106.2 1.0 copy-done.9
  107.2 8.8 %scatter.5 = (f32[768,256]{1,0:T(8,128)S(1)}, bf16[96,256]{1,0:T(8,128)(2,1)S(1)}, bf16[96,256]{1,0:T(8,128)(2,1)S(1)}) custom-call(bf16[16,128,128]{2,1,0:T(8,128)(2,1)S(1)} %all-to-all-done.2.after_ref.parts_ref, f32[960,256]{1,0:T(8,128)S(1)} %scatter.4.start_ref, s32[27,1,2048]{2,1,0:T(1,128)S(1)} %bitcast.23, bf16[2592,96]{1,0:T(8,128)(2,1)S(1)} %bitcast.13, ...), custom_call_target="tpu_custom_call" | custom-call | flops 6794772480 | bytes 2097152 | tf_op jit(solution)/shard_map/scatter/pallas_call | solution.py:282
  116.1 1.9 %collective-permute-start.2 = (bf16[96,256]{1,0:T(8,128)(2,1)S(1)}, bf16[96,256]{1,0:T(8,128)(2,1)S(1)}, u32[]{:S(2)}, u32[]{:S(2)}) collective-permute-start(bf16[96,256]{1,0:T(8,128)(2,1)S(1)} %get-tuple-element.22), channel_id=1, source_target_pairs={{0,1},{1,2},{2,3},{3,4},{4,5},{5,6},{6,7},{7,8},{8,9},{9,10},{10,1... | collective-permute-start | bytes 147464 | tf_op jit(solution)/shard_map/ppermute | solution.py:402
  118.0 2.4 %collective-permute-start.3 = (bf16[96,256]{1,0:T(8,128)(2,1)S(1)}, bf16[96,256]{1,0:T(8,128)(2,1)S(1)}, u32[]{:S(2)}, u32[]{:S(2)}) collective-permute-start(bf16[96,256]{1,0:T(8,128)(2,1)S(1)} %get-tuple-element.23), channel_id=1, source_target_pairs={{1,0},{2,1},{3,2},{4,3},{5,4},{6,5},{7,6},{8,7},{9,8},{10,9},{11,1... | collective-permute-start | bytes 147464 | tf_op jit(solution)/shard_map/ppermute | solution.py:403
  120.4 0.0 collective-permute-done.2.from_low_ref
  120.4 3.0 %collective-permute-done.3.from_high_ref = bf16[96,256]{1,0:T(8,128)(2,1)S(1)} collective-permute-done((bf16[96,256]{1,0:T(8,128)(2,1)S(1)}, bf16[96,256]{1,0:T(8,128)(2,1)S(1)}, u32[]{:S(2)}, u32[]{:S(2)}) %collective-permute-start.3) | collective-permute-done | bytes 49184 | tf_op jit(solution)/shard_map/ppermute | solution.py:403
  123.4 0.0 copy-done.4
  123.4 0.4 fold.1
  123.8 0.0 copy-start.2
  123.8 21.2 %all_to_all.21.back_ref = bf16[16,224,128]{2,1,0:T(8,128)(2,1)S(1)} all-to-all(bf16[16,224,128]{2,1,0:T(8,128)(2,1)S(1)} %fold.1), channel_id=1, replica_groups=mesh['sx'=16,'sy'=16] {'sx'}, dimensions={0} | all-to-all | bytes 1835008 | tf_op jit(solution)/shard_map/all_to_all | solution.py:395
  145.0 0.0 copy-done.2
  145.0 2.1 %finish.1 = (bf16[96,1024]{1,0:T(8,128)(2,1)}, f32[27,96,96]{2,1,0:T(8,128)}) custom-call(bf16[16,224,128]{2,1,0:T(8,128)(2,1)S(1)} %all_to_all.21.back_ref, s32[1,1024]{1,0:T(1,128)S(1)} %bitcast.16, s32[1,1024]{1,0:T(1,128)S(1)} %get-tuple-element.24.slot_ref), custom_call_target="tpu_custom_call" | custom-call | tf_op jit(solution)/shard_map/finish/pallas_call | solution.py:368
Async XLA Ops:
  0.6 0.9 copy-start
  1.6 0.7 copy-start.1
  2.2 26.7 %copy-start.10 = (bf16[27,96,96]{2,1,0:T(8,128)(2,1)S(1)}, bf16[27,96,96]{2,1,0:T(8,128)(2,1)}, u32[]{:S(2)}) copy-start(bf16[27,96,96]{2,1,0:T(8,128)(2,1)} %param.10) | copy-start | bytes 1492996
  20.4 0.7 copy-start.3
  21.7 8.3 %collective-permute-start = (bf16[96,256]{1,0:T(8,128)(2,1)S(1)}, bf16[96,256]{1,0:T(8,128)(2,1)S(1)}, u32[]{:S(2)}, u32[]{:S(2)}) collective-permute-start(bf16[96,256]{1,0:T(8,128)(2,1)S(1)} %get-tuple-element.16), channel_id=1, source_target_pairs={{0,1},{1,2},{2,3},{3,4},{4,5},{5,6},{6,7},{7,8},{8,9},{9,10},{10,1... | collective-permute-start | bytes 147464 | tf_op jit(solution)/shard_map/ppermute | solution.py:387
  27.0 5.4 %collective-permute-start.1 = (bf16[96,256]{1,0:T(8,128)(2,1)S(1)}, bf16[96,256]{1,0:T(8,128)(2,1)S(1)}, u32[]{:S(2)}, u32[]{:S(2)}) collective-permute-start(bf16[96,256]{1,0:T(8,128)(2,1)S(1)} %get-tuple-element.17), channel_id=1, source_target_pairs={{1,0},{2,1},{3,2},{4,3},{5,4},{6,5},{7,6},{8,7},{9,8},{10,9},{11,1... | collective-permute-start | bytes 147464 | tf_op jit(solution)/shard_map/ppermute | solution.py:388
  29.3 3.1 %copy-start.5 = (bf16[1,1,96,2048]{3,2,1,0:T(8,128)(2,1)S(1)}, bf16[1,1,96,2048]{3,2,1,0:T(8,128)(2,1)}, u32[]{:S(2)}) copy-start(bf16[1,1,96,2048]{3,2,1,0:T(8,128)(2,1)} %param.11) | copy-start | bytes 1179652
  29.3 3.1 %copy-start.6 = (s32[1,1,27,2048]{3,1,2,0:T(1,128)S(1)}, s32[1,1,27,2048]{3,1,2,0:T(1,128)}, u32[]{:S(2)}) copy-start(s32[1,1,27,2048]{3,1,2,0:T(1,128)} %param.8) | copy-start | bytes 663556
  62.7 16.9 %copy-start.7 = (bf16[96,2048]{1,0:T(8,128)(2,1)}, bf16[96,2048]{1,0:T(8,128)(2,1)S(1)}, u32[]{:S(2)}) copy-start(bf16[96,2048]{1,0:T(8,128)(2,1)S(1)} %get-tuple-element.19.after_ref.start_ref.pre_ref) | copy-start | bytes 1179652
  62.7 16.9 %all-to-all-start.1 = ((bf16[16,128,128]{2,1,0:T(8,128)(2,1)}), bf16[16,128,128]{2,1,0:T(8,128)(2,1)S(1)}, u32[]{:S(2)}, u32[]{:S(2)}) async-start(bf16[16,128,128]{2,1,0:T(8,128)(2,1)} %get-tuple-element.20), calls=%async_computation.1 | async-start | bytes 1048576 | tf_op jit(solution)/shard_map/all_to_all | solution.py:395
  80.5 25.8 %all-to-all-start.2 = ((bf16[16,128,128]{2,1,0:T(8,128)(2,1)}), bf16[16,128,128]{2,1,0:T(8,128)(2,1)S(1)}, u32[]{:S(2)}, u32[]{:S(2)}) async-start(bf16[16,128,128]{2,1,0:T(8,128)(2,1)} %sum_parts.1.after_ref), calls=%async_computation.2 | async-start | bytes 1048576 | tf_op jit(solution)/shard_map/all_to_all | solution.py:395
  88.9 1.0 copy-start.8
  103.0 20.4 %copy-start.4 = (s32[1,1,2,256]{3,2,1,0:T(2,128)S(1)}, s32[1,1,2,256]{3,2,1,0:T(2,128)}, u32[]{:S(2)}) copy-start(s32[1,1,2,256]{3,2,1,0:T(2,128)} %param.9) | copy-start | bytes 6148
  106.2 1.0 copy-start.9
  116.1 4.3 %collective-permute-start.2 = (bf16[96,256]{1,0:T(8,128)(2,1)S(1)}, bf16[96,256]{1,0:T(8,128)(2,1)S(1)}, u32[]{:S(2)}, u32[]{:S(2)}) collective-permute-start(bf16[96,256]{1,0:T(8,128)(2,1)S(1)} %get-tuple-element.22), channel_id=1, source_target_pairs={{0,1},{1,2},{2,3},{3,4},{4,5},{5,6},{6,7},{7,8},{8,9},{9,10},{10,1... | collective-permute-start | bytes 147464 | tf_op jit(solution)/shard_map/ppermute | solution.py:402
  118.0 5.4 %collective-permute-start.3 = (bf16[96,256]{1,0:T(8,128)(2,1)S(1)}, bf16[96,256]{1,0:T(8,128)(2,1)S(1)}, u32[]{:S(2)}, u32[]{:S(2)}) collective-permute-start(bf16[96,256]{1,0:T(8,128)(2,1)S(1)} %get-tuple-element.23), channel_id=1, source_target_pairs={{1,0},{2,1},{3,2},{4,3},{5,4},{6,5},{7,6},{8,7},{9,8},{10,9},{11,1... | collective-permute-start | bytes 147464 | tf_op jit(solution)/shard_map/ppermute | solution.py:403
  123.8 21.2 %copy-start.2 = (s32[1,1,1024,1]{2,3,1,0:T(1,128)S(1)}, s32[1,1,1024,1]{2,3,1,0:T(1,128)}, u32[]{:S(2)}) copy-start(s32[1,1,1024,1]{2,3,1,0:T(1,128)} %param.7) | copy-start | bytes 12292

commit v8 on v7

--- a/solution.py
+++ b/solution.py
@@ -18,11 +18,11 @@
 LO = 256
 BANKS = V // LO
 ALL_BANKS = BANKS + 2
-WIDE = 512
+WIDE = 256
 WIDE_BANKS = ALL_BANKS * LO // WIDE
 VB = 256
 FORWARD_VB = 512
-MAIN = 80
+MAIN = 48
 PER_DOT = 3
 PARTS = (3, 3, 2)
 LANES = 128
@@ -64,14 +64,21 @@
 
 
 def gather_lanes(tiles_ref, index):
+    tiles, rows, _ = tiles_ref.shape
     lane, tile = rows16(index & (CAP - 1)), rows16(index >> 7)
-    kept = jnp.zeros((16, CAP), BF)
-    for t in range(tiles_ref.shape[0]):
-        read = lax.gather(
-            tiles_ref[t], lane[..., None], LANE_GATHER, (1, 1), mode=lax.GatherScatterMode.PROMISE_IN_BOUNDS
-        )
-        kept = jnp.where(tile == t, read, kept)
-    return kept
+    kept = [jnp.zeros((16, CAP), BF) for _ in range(rows // 16)]
+    for t in range(tiles):
+        mine = tile == t
+        for h in range(rows // 16):
+            read = lax.gather(
+                tiles_ref[t, h * 16 : (h + 1) * 16, :],
+                lane[..., None],
+                LANE_GATHER,
+                (1, 1),
+                mode=lax.GatherScatterMode.PROMISE_IN_BOUNDS,
+            )
+            kept[h] = jnp.where(mine, read, kept[h])
+    return jnp.concatenate(kept, axis=0)
 
 
 def masked_banks(values, bank, banks, out_ref, column):
@@ -139,8 +146,9 @@
 
 
 def forward_kernel(
-    owned_ref, low_ref, high_ref, map_ref, weight_ref, cot_ref, out_ref, pre_ref, wg_ref, table_ref, tail_ref, picked_ref, acc_ref
+    owned_ref, low_ref, high_ref, map_ref, weight_ref, cot_ref, out_ref, *refs
 ):
+    pre_refs, (wg_ref, table_ref, tail_ref, picked_ref, acc_ref) = refs[: len(PARTS)], refs[len(PARTS) :]
     step = pl.program_id(0)
 
     @pl.when(step == 0)
@@ -150,9 +158,9 @@
             rows = slice((g // per) * MAIN, (g // per + 1) * MAIN)
             table_ref[rows, (g % per) * CAP : (g % per + 1) * CAP] = owned_ref[g, :MAIN, :]
             tail_ref[g] = owned_ref[g, MAIN:, :]
-        table_ref[(WIDE_BANKS - 1) * MAIN :, :F] = low_ref[:MAIN, :]
-        table_ref[(WIDE_BANKS - 1) * MAIN :, F:] = high_ref[:MAIN, :]
         for j, ghost_ref in enumerate((low_ref, high_ref)):
+            bank, at = divmod(V + j * F, WIDE)
+            table_ref[bank * MAIN : (bank + 1) * MAIN, at : at + F] = ghost_ref[:MAIN, :]
             for i in range(F // CAP):
                 tail_ref[GROUPS + j * (F // CAP) + i] = ghost_ref[MAIN:, i * CAP : (i + 1) * CAP]
         acc_ref[...] = jnp.zeros_like(acc_ref)
@@ -161,7 +169,7 @@
     for k in range(K):
         index = map_ref[k]
         product = jnp.dot(table, onehot_rows(index & (WIDE - 1), WIDE), preferred_element_type=F32)
-        main = select_banks(product, index >> 9, WIDE_BANKS, MAIN)
+        main = select_banks(product, index >> (WIDE.bit_length() - 1), WIDE_BANKS, MAIN)
         picked_ref[k * C : k * C + MAIN, :] = main.astype(BF)
         for i in range(FORWARD_VB // CAP):
             cols = slice(i * CAP, (i + 1) * CAP)
@@ -171,7 +179,16 @@
     out_ref[...] = (preact * logistic).astype(BF)
     slope = logistic * (1.0 + preact * (1.0 - logistic))
     grad_pre = (cot_ref[...].astype(F32) * slope).astype(BF)
-    pre_ref[...] = grad_pre
+    for block in range(V // FORWARD_VB):
+
+        @pl.when(step == block)
+        def _(first=block * FORWARD_VB):
+            for part, pre_ref in enumerate(pre_refs):
+                at = sum(PARTS[:part]) * VB
+                low, high = max(first, at), min(first + FORWARD_VB, at + PARTS[part] * VB)
+                if low < high:
+                    pre_ref[:, low - at : high - at] = grad_pre[:, low - first : high - first]
+
     acc_ref[...] += lax.dot_general(picked_ref[...], grad_pre, NT, preferred_element_type=F32)
 
     @pl.when(step == pl.num_programs(0) - 1)
@@ -202,10 +219,10 @@
             whole(C, K * C),
             column(C),
         ],
-        out_specs=(column(C), column(C), whole(GROUPS, LANES, LANES)),
+        out_specs=(column(C), *(whole(C, n * VB) for n in PARTS), whole(GROUPS, LANES, LANES)),
         out_shape=(
             jax.ShapeDtypeStruct((C, V), BF),
-            jax.ShapeDtypeStruct((C, V), BF),
+            *(jax.ShapeDtypeStruct((C, n * VB), BF) for n in PARTS),
             jax.ShapeDtypeStruct((GROUPS, LANES, LANES), BF),
         ),
         scratch_shapes=[
@@ -222,82 +239,61 @@
     )(owned, low, high, kernel_map, weight, cotangent)
 
 
-def bank_rows(values, bank):
+def bank_rows(values, bank, banks):
     n = bank.shape[-1]
     bank16 = rows16(bank)
     values = values.reshape(C // 16, 16, n)
-    banks = [jnp.where((bank16 == a)[None], values, BF(0)).reshape(C, n) for a in range(ALL_BANKS)]
-    return jnp.concatenate(banks, axis=0)
-
-
-def scatter_step(map_ref, weight_ref, pre_ref, acc_ref, spread_ref):
+    return jnp.concatenate([jnp.where((bank16 == a)[None], values, BF(0)).reshape(C, n) for a in banks], axis=0)
+
+
+def scatter_kernel(banks, has_start, after_ref, start_ref, map_ref, weight_ref, pre_ref, *refs):
+    *out_refs, spread_ref, acc_ref = refs
+
+    @pl.when(pl.program_id(0) == 0)
+    def _():
+        acc_ref[...] = start_ref[...] if has_start else jnp.zeros_like(acc_ref)
+
     spread_ref[...] = jnp.dot(weight_ref[...], pre_ref[...], preferred_element_type=F32).astype(BF)
     for first in range(0, K, PER_DOT):
         spreads, hots = [], []
         for k in range(first, first + PER_DOT):
             index = map_ref[k]
-            spreads.append(bank_rows(spread_ref[k * C : (k + 1) * C, :], index >> 8))
+            spreads.append(bank_rows(spread_ref[k * C : (k + 1) * C, :], index >> 8, banks))
             hots.append(onehot_rows(index & (LO - 1), LO))
         acc_ref[...] += lax.dot_general(
             jnp.concatenate(spreads, axis=1), jnp.concatenate(hots, axis=1), NT, preferred_element_type=F32
         )
 
-
-def scatter_kernel(has_start, has_faces, after_ref, start_ref, map_ref, weight_ref, pre_ref, *refs):
-    if has_faces:
-        own_ref, low_ref, high_ref, spread_ref, acc_ref = refs
-    else:
-        acc_ref, spread_ref = refs
-
-    @pl.when(pl.program_id(0) == 0)
+    @pl.when(pl.program_id(0) == pl.num_programs(0) - 1)
     def _():
-        acc_ref[...] = start_ref[...] if has_start else jnp.zeros_like(acc_ref)
-
-    scatter_step(map_ref, weight_ref, pre_ref, acc_ref, spread_ref)
-
-    if has_faces:
-
-        @pl.when(pl.program_id(0) == pl.num_programs(0) - 1)
-        def _():
-            own_ref[...] = acc_ref[: BANKS * C, :]
-            low_ref[...] = acc_ref[BANKS * C : (BANKS + 1) * C, :].astype(BF)
-            high_ref[...] = acc_ref[(BANKS + 1) * C :, :].astype(BF)
-
-
-def scatter_part(part, after, start, kernel_map, weight, grad_pre):
+        rows = acc_ref.shape[0] // len(out_refs)
+        for i, out_ref in enumerate(out_refs):
+            out_ref[...] = acc_ref[i * rows : (i + 1) * rows, :].astype(out_ref.dtype)
+
+
+def scatter_part(part, banks, after, start, kernel_map, weight, grad_pre, split=1, dtype=F32):
     whole = lambda *shape: pl.BlockSpec(shape, lambda i: (0,) * len(shape))
-    sums = jax.ShapeDtypeStruct((ALL_BANKS * C, LO), F32)
-    scratch = [pltpu.VMEM((K * C, VB), BF)]
-    at, steps, last = sum(PARTS[:part]), PARTS[part], part == len(PARTS) - 1
-    if last:
-        out_specs = (whole(BANKS * C, LO), whole(C, F), whole(C, F))
-        out_shape = (
-            jax.ShapeDtypeStruct((BANKS * C, LO), F32),
-            jax.ShapeDtypeStruct((C, F), BF),
-            jax.ShapeDtypeStruct((C, F), BF),
-        )
-        scratch.append(pltpu.VMEM(sums.shape, F32))
-    else:
-        out_specs, out_shape = whole(*sums.shape), sums
-    return pl.pallas_call(
-        functools.partial(scatter_kernel, part > 0, last),
+    rows, at, steps = len(banks) * C, sum(PARTS[:part]), PARTS[part]
+    start_spec = pl.BlockSpec((rows, LO), lambda i: (banks[0] // len(banks), 0))
+    return pl.pallas_call(
+        functools.partial(scatter_kernel, banks, part > 0),
         grid=(steps,),
         in_specs=[
             pl.BlockSpec(memory_space=pl.ANY),
-            whole(*sums.shape) if part > 0 else pl.BlockSpec(memory_space=pl.ANY),
+            start_spec if part > 0 else pl.BlockSpec(memory_space=pl.ANY),
             pl.BlockSpec((K, 1, VB), lambda i: (0, 0, at + i)),
             whole(K * C, C),
-            pl.BlockSpec((C, VB), lambda i: (0, at + i)),
+            pl.BlockSpec((C, VB), lambda i: (0, i)),
         ],
-        out_specs=out_specs,
-        out_shape=out_shape,
-        scratch_shapes=scratch,
+        out_specs=(whole(rows // split, LO),) * split,
+        out_shape=(jax.ShapeDtypeStruct((rows // split, LO), dtype),) * split,
+        scratch_shapes=[pltpu.VMEM((K * C, VB), BF), pltpu.VMEM((rows, LO), F32)],
         compiler_params=pltpu.CompilerParams(vmem_limit_bytes=24 << 20),
         cost_estimate=pl.CostEstimate(
-            flops=2 * K * VB * steps * ALL_BANKS * C * LO, bytes_accessed=2 << 20, transcendentals=0
+            flops=2 * K * VB * steps * rows * LO, bytes_accessed=2 << 20, transcendentals=0
         ),
         name="scatter",
-    )(after, start, kernel_map, weight, grad_pre)
+    )(after, start, kernel_map, weight, grad_pre[part])
 
 
 def total_of(parts_ref):
@@ -387,18 +383,20 @@
     ghost_low = lax.ppermute(upper, "sy", up)
     ghost_high = lax.ppermute(lower, "sy", down)
     weight_rows = jnp.transpose(weight, (1, 0, 2)).reshape(C, K * C)
-    output, grad_pre, weight_part = forward_pass(
+    output, *grad_pre, weight_part = forward_pass(
         owned, ghost_low, ghost_high, kernel_map, weight_rows, incoming
     )
     weight_columns = jnp.transpose(weight, (0, 2, 1)).reshape(K * C, C)
     scatter = functools.partial(scatter_part, kernel_map=kernel_map, weight=weight_columns, grad_pre=grad_pre)
     across = lambda array, axis: lax.all_to_all(array, axis, 0, 0, tiled=True)
+    every = range(ALL_BANKS)
     parts = across(weight_part, "sx")
-    sums = scatter(0, grad_pre, grad_pre)
+    (sums,) = scatter(0, every, grad_pre[0], grad_pre[0])
     row_sums = sum_parts(sums, parts)
     parts = across(row_sums, "sy")
-    sums = scatter(1, row_sums, sums)
-    table_grad, to_low, to_high = scatter(2, parts, sums)
+    (sums,) = scatter(1, every, row_sums, sums)
+    to_low, to_high = scatter(2, every[BANKS:], parts, sums, split=2, dtype=BF)
+    (table_grad,) = scatter(2, every[:BANKS], to_low, sums)
     from_low = lax.ppermute(to_high, "sy", up)
     from_high = lax.ppermute(to_low, "sy", down)
     owned_grad = fold_faces(table_grad, from_low, from_high, face_list, parts)

time: 148 us -> 154 us (1.041)
  Pallas kernels: 70.9 us -> 78.7 us
  waiting for transfers between devices: 8.63 us -> 5.69 us
  blocking collectives: 37.7 us -> 39.3 us
    pallas_call x1, Pallas kernels: 30.3 us -> 35.7 us  [forward_pass(): pl.pallas_call(forward_kernel, grid=(V // FORWARD_VB,), in_specs=[whole(G...]
    ppermute x1, waiting for transfers between devices: 2.99 us -> 0.01 us  [body(): from_high = lax.ppermute(to_low, 'sy', down)]
    pallas_call x3 -> x4, Pallas kernels: 35 us -> 37.5 us  [scatter_part(): pl.pallas_call(functools.partial(scatter_kernel, banks, part > 0), grid=(...]
    all_to_all x1, blocking collectives: 21.2 us -> 22.7 us  [body(): across = lambda array, axis: lax.all_to_all(array, axis, 0, 0, tiled=True)]
    unnamed x22 -> x20, local copies, waits for them, and re-layouts: 4.31 us -> 3.88 us
  transfers between devices with their start and end apart: 6 -> 6, of which waited for: 3 -> 2; matrix products, arithmetic and copies ran while one was open for 1% -> 1% of each run, Pallas kernels for 18% -> 22%
where the time goes in v8:
time: 154 us; the launch traced here: 153 us
  Pallas kernels  78.7 us (51%)
  blocking collectives  39.3 us (26%)
  starting transfers between devices  24 us (16%)
  waiting for transfers between devices  5.69 us (4%)
  local copies, waits for them, and re-layouts  4.87 us (3%)
    pallas_call x4, Pallas kernels, scatter_part(): pl.pallas_call(functools.partial(scatter_kernel, banks, part > 0), grid=(...  37.5 us
    pallas_call x1, Pallas kernels, forward_pass(): pl.pallas_call(forward_kernel, grid=(V // FORWARD_VB,), in_specs=[whole(G...  35.7 us
    all_to_all x1, blocking collectives, body(): across = lambda array, axis: lax.all_to_all(array, axis, 0, 0, tiled=True)  22.7 us
    all_to_all x1, blocking collectives, body(): owned = lax.all_to_all(outgoing, 'sx', 0, 0, tiled=True)  16.6 us
    all_to_all x2, starting transfers between devices, body(): across = lambda array, axis: lax.all_to_all(array, axis, 0, 0, tiled=True)  12.2 us
    ppermute x1, starting transfers between devices, body(): ghost_low = lax.ppermute(upper, 'sy', up)  5.29 us
    unnamed x20, local copies, waits for them, and re-layouts  3.88 us
    all_to_all x2, waiting for transfers between devices, body(): across = lambda array, axis: lax.all_to_all(array, axis, 0, 0, tiled=True)  3.25 us
  transfers between devices with their start and end apart: 6, of which 2 were waited for; matrix products, arithmetic and copies ran while one was open for 1% of the time, Pallas kernels for 22%

profile of v8, /device:TPU:1, one launch (start us, length us, event | category | flops | bytes accessed | tf_op | source)
XLA Modules:
  0.0 153.3 jit_solution(10883611121167360239)
XLA Ops:
  0.6 0.0 copy-start
  0.6 0.9 copy-done
  1.6 0.0 copy-start.1
  1.6 0.7 copy-done.1
  2.2 0.0 copy-start.9
  2.2 1.6 %place.1 = (bf16[16,96,128]{2,1,0:T(8,128)(2,1)S(1)}, s32[1,1024]{1,0:T(1,128)S(1)}) custom-call(bf16[96,1024]{1,0:T(8,128)(2,1)S(1)} %bitcast.15, s32[1,1024]{1,0:T(1,128)S(1)} %bitcast.16), custom_call_target="tpu_custom_call" | custom-call | tf_op jit(solution)/shard_map/place/pallas_call | solution.py:119
  3.9 16.6 %all_to_all.20.owned_ref = bf16[16,96,128]{2,1,0:T(8,128)(2,1)S(1)} all-to-all(bf16[16,96,128]{2,1,0:T(8,128)(2,1)S(1)} %get-tuple-element.16), channel_id=1, replica_groups=mesh['sx'=16,'sy'=16] {'sx'}, dimensions={0} | all-to-all | bytes 786432 | tf_op jit(solution)/shard_map/all_to_all | solution.py:381
  20.4 0.0 copy-start.3
  20.5 0.7 copy-done.3
  21.1 0.5 faces.1
  21.7 5.3 %collective-permute-start = (bf16[96,256]{1,0:T(8,128)(2,1)S(1)}, bf16[96,256]{1,0:T(8,128)(2,1)S(1)}, u32[]{:S(2)}, u32[]{:S(2)}) collective-permute-start(bf16[96,256]{1,0:T(8,128)(2,1)S(1)} %get-tuple-element.17), channel_id=1, source_target_pairs={{0,1},{1,2},{2,3},{3,4},{4,5},{5,6},{6,7},{7,8},{8,9},{9,10},{10,1... | collective-permute-start | bytes 147464 | tf_op jit(solution)/shard_map/ppermute | solution.py:383
  27.0 1.9 %collective-permute-start.1 = (bf16[96,256]{1,0:T(8,128)(2,1)S(1)}, bf16[96,256]{1,0:T(8,128)(2,1)S(1)}, u32[]{:S(2)}, u32[]{:S(2)}) collective-permute-start(bf16[96,256]{1,0:T(8,128)(2,1)S(1)} %get-tuple-element.18), channel_id=1, source_target_pairs={{1,0},{2,1},{3,2},{4,3},{5,4},{6,5},{7,6},{8,7},{9,8},{10,9},{11,1... | collective-permute-start | bytes 147464 | tf_op jit(solution)/shard_map/ppermute | solution.py:384
  28.9 0.0 copy-done.9
  28.9 0.3 copy.11
  29.3 0.0 copy-start.5
  29.3 0.0 copy-start.6
  29.3 0.3 copy.12.weight_ref
  29.6 0.3 copy.13
  30.0 0.0 collective-permute-done.low_ref
  30.0 2.4 %collective-permute-done.1.high_ref = bf16[96,256]{1,0:T(8,128)(2,1)S(1)} collective-permute-done((bf16[96,256]{1,0:T(8,128)(2,1)S(1)}, bf16[96,256]{1,0:T(8,128)(2,1)S(1)}, u32[]{:S(2)}, u32[]{:S(2)}) %collective-permute-start.1) | collective-permute-done | bytes 49184 | tf_op jit(solution)/shard_map/ppermute | solution.py:384
  32.4 0.0 copy-done.5
  32.4 0.0 copy-done.6
  32.4 35.7 %gather_forward.1 = (bf16[96,2048]{1,0:T(8,128)(2,1)}, bf16[96,768]{1,0:T(8,128)(2,1)S(1)}, bf16[96,768]{1,0:T(8,128)(2,1)S(1)}, bf16[96,512]{1,0:T(8,128)(2,1)S(1)}, bf16[16,128,128]{2,1,0:T(8,128)(2,1)}) custom-call(bf16[16,96,128]{2,1,0:T(8,128)(2,1)S(1)} %all_to_all.20.owned_ref, bf16[96,256]{1,0:T(8,128)(2,1)S(1)} %collective-permute-done.low_ref, ...), custom_call_target="tpu_custom_call" | custom-call | flops 27179089920 | bytes 4194304 | tf_op jit(solution)/shard_map/gather_forward/pallas_call | solution.py:211
  68.1 0.0 copy-start.7
  68.1 0.7 copy-done.7
  68.7 3.8 %all-to-all-start.1 = ((bf16[16,128,128]{2,1,0:T(8,128)(2,1)}), bf16[16,128,128]{2,1,0:T(8,128)(2,1)S(1)}, u32[]{:S(2)}, u32[]{:S(2)}) async-start(bf16[16,128,128]{2,1,0:T(8,128)(2,1)} %get-tuple-element.21), calls=%async_computation.1 | async-start | bytes 1048576 | tf_op jit(solution)/shard_map/all_to_all | solution.py:391
  72.5 13.2 %scatter.4.after_ref.start_ref = f32[960,256]{1,0:T(8,128)S(1)} custom-call(bf16[96,768]{1,0:T(8,128)(2,1)S(1)} %get-tuple-element.20.after_ref.start_ref.pre_ref, bf16[96,768]{1,0:T(8,128)(2,1)S(1)} %get-tuple-element.20.after_ref.start_ref.pre_ref, s32[27,1,2048]{2,1,0:T(1,128)S(1)} %bitcast.22, bf16[2592,96]{1,0:T(8,128)(2,1)S(1)} %bitcast.11, ...), custom_call_target="tpu_custom_call" | custom-call | flops 10192158720 | bytes 2097152 | tf_op jit(solution)/shard_map/scatter/pallas_call | solution.py:278
  85.7 0.0 all-to-all-done.1.parts_ref
  85.7 0.9 sum_parts.1.after_ref
  86.6 8.5 %all-to-all-start.2 = ((bf16[16,128,128]{2,1,0:T(8,128)(2,1)}), bf16[16,128,128]{2,1,0:T(8,128)(2,1)S(1)}, u32[]{:S(2)}, u32[]{:S(2)}) async-start(bf16[16,128,128]{2,1,0:T(8,128)(2,1)} %sum_parts.1.after_ref), calls=%async_computation.2 | async-start | bytes 1048576 | tf_op jit(solution)/shard_map/all_to_all | solution.py:391
  95.0 0.0 copy-start.8
  95.0 0.9 copy-done.8
  95.9 13.2 %scatter.5.start_ref = f32[960,256]{1,0:T(8,128)S(1)} custom-call(bf16[16,128,128]{2,1,0:T(8,128)(2,1)} %sum_parts.1.after_ref, f32[960,256]{1,0:T(8,128)S(1)} %scatter.4.after_ref.start_ref, s32[27,1,2048]{2,1,0:T(1,128)S(1)} %bitcast.23, bf16[2592,96]{1,0:T(8,128)(2,1)S(1)} %bitcast.12, bf16[96,768]{1,0:T(8,128)(2,1)S(1)} %copy-done.8), custom_call_target="tpu_custom_call" | custom-call | flops 10192158720 | bytes 2097152 | tf_op jit(solution)/shard_map/scatter/pallas_call | solution.py:278
  109.1 3.2 %all-to-all-done.2.after_ref.parts_ref = bf16[16,128,128]{2,1,0:T(8,128)(2,1)S(1)} async-done(((bf16[16,128,128]{2,1,0:T(8,128)(2,1)}), bf16[16,128,128]{2,1,0:T(8,128)(2,1)S(1)}, u32[]{:S(2)}, u32[]{:S(2)}) %all-to-all-start.2) | async-done | bytes 524320 | tf_op jit(solution)/shard_map/all_to_all | solution.py:391
  112.3 3.8 %scatter.6 = (bf16[96,256]{1,0:T(8,128)(2,1)S(1)}, bf16[96,256]{1,0:T(8,128)(2,1)S(1)}) custom-call(bf16[16,128,128]{2,1,0:T(8,128)(2,1)S(1)} %all-to-all-done.2.after_ref.parts_ref, f32[960,256]{1,0:T(8,128)S(1)} %scatter.5.start_ref, s32[27,1,2048]{2,1,0:T(1,128)S(1)} %bitcast.24, bf16[2592,96]{1,0:T(8,128)(2,1)S(1)} %bitcast.13, ...), custom_call_target="tpu_custom_call" | custom-call | flops 1358954496 | bytes 2097152 | tf_op jit(solution)/shard_map/scatter/pallas_call | solution.py:278
  116.1 1.9 %collective-permute-start.2 = (bf16[96,256]{1,0:T(8,128)(2,1)S(1)}, bf16[96,256]{1,0:T(8,128)(2,1)S(1)}, u32[]{:S(2)}, u32[]{:S(2)}) collective-permute-start(bf16[96,256]{1,0:T(8,128)(2,1)S(1)} %get-tuple-element.25), channel_id=1, source_target_pairs={{0,1},{1,2},{2,3},{3,4},{4,5},{5,6},{6,7},{7,8},{8,9},{9,10},{10,1... | collective-permute-start | bytes 147464 | tf_op jit(solution)/shard_map/ppermute | solution.py:400
  118.1 0.0 copy-start.4
  118.1 2.6 %collective-permute-start.3 = (bf16[96,256]{1,0:T(8,128)(2,1)S(1)}, bf16[96,256]{1,0:T(8,128)(2,1)S(1)}, u32[]{:S(2)}, u32[]{:S(2)}) collective-permute-start(bf16[96,256]{1,0:T(8,128)(2,1)S(1)} %get-tuple-element.24.after_ref), channel_id=1, source_target_pairs={{1,0},{2,1},{3,2},{4,3},{5,4},{6,5},{7,6},{8,7},{9,8},{10,9},{11,1... | collective-permute-start | bytes 147464 | tf_op jit(solution)/shard_map/ppermute | solution.py:401
  120.7 7.4 %scatter.7.grad_ref = f32[768,256]{1,0:T(8,128)S(1)} custom-call(bf16[96,256]{1,0:T(8,128)(2,1)S(1)} %get-tuple-element.24.after_ref, f32[960,256]{1,0:T(8,128)S(1)} %scatter.5.start_ref, s32[27,1,2048]{2,1,0:T(1,128)S(1)} %bitcast.25, bf16[2592,96]{1,0:T(8,128)(2,1)S(1)} %bitcast.14, bf16[96,512]{1,0:T(8,128)(2,1)S(1)} %get-tuple-element.23.pre_ref), custom_call_target="tpu_custom_call" | custom-call | flops 5435817984 | bytes 2097152 | tf_op jit(solution)/shard_map/scatter/pallas_call | solution.py:278
  128.1 0.0 collective-permute-done.2.from_low_ref
  128.1 0.0 collective-permute-done.3.from_high_ref
  128.1 0.0 copy-done.4
  128.1 0.4 fold.1
  128.5 0.0 copy-start.2
  128.5 22.7 %all_to_all.21.back_ref = bf16[16,224,128]{2,1,0:T(8,128)(2,1)S(1)} all-to-all(bf16[16,224,128]{2,1,0:T(8,128)(2,1)S(1)} %fold.1), channel_id=1, replica_groups=mesh['sx'=16,'sy'=16] {'sx'}, dimensions={0} | all-to-all | bytes 1835008 | tf_op jit(solution)/shard_map/all_to_all | solution.py:391
  151.2 0.0 copy-done.2
  151.2 2.1 %finish.1 = (bf16[96,1024]{1,0:T(8,128)(2,1)}, f32[27,96,96]{2,1,0:T(8,128)}) custom-call(bf16[16,224,128]{2,1,0:T(8,128)(2,1)S(1)} %all_to_all.21.back_ref, s32[1,1024]{1,0:T(1,128)S(1)} %bitcast.17, s32[1,1024]{1,0:T(1,128)S(1)} %get-tuple-element.26.slot_ref), custom_call_target="tpu_custom_call" | custom-call | tf_op jit(solution)/shard_map/finish/pallas_call | solution.py:364
Async XLA Ops:
  0.6 0.9 copy-start
  1.6 0.7 copy-start.1
  2.2 26.7 %copy-start.9 = (bf16[27,96,96]{2,1,0:T(8,128)(2,1)S(1)}, bf16[27,96,96]{2,1,0:T(8,128)(2,1)}, u32[]{:S(2)}) copy-start(bf16[27,96,96]{2,1,0:T(8,128)(2,1)} %param.10) | copy-start | bytes 1492996
  20.4 0.7 copy-start.3
  21.7 8.3 %collective-permute-start = (bf16[96,256]{1,0:T(8,128)(2,1)S(1)}, bf16[96,256]{1,0:T(8,128)(2,1)S(1)}, u32[]{:S(2)}, u32[]{:S(2)}) collective-permute-start(bf16[96,256]{1,0:T(8,128)(2,1)S(1)} %get-tuple-element.17), channel_id=1, source_target_pairs={{0,1},{1,2},{2,3},{3,4},{4,5},{5,6},{6,7},{7,8},{8,9},{9,10},{10,1... | collective-permute-start | bytes 147464 | tf_op jit(solution)/shard_map/ppermute | solution.py:383
  27.0 5.4 %collective-permute-start.1 = (bf16[96,256]{1,0:T(8,128)(2,1)S(1)}, bf16[96,256]{1,0:T(8,128)(2,1)S(1)}, u32[]{:S(2)}, u32[]{:S(2)}) collective-permute-start(bf16[96,256]{1,0:T(8,128)(2,1)S(1)} %get-tuple-element.18), channel_id=1, source_target_pairs={{1,0},{2,1},{3,2},{4,3},{5,4},{6,5},{7,6},{8,7},{9,8},{10,9},{11,1... | collective-permute-start | bytes 147464 | tf_op jit(solution)/shard_map/ppermute | solution.py:384
  29.3 3.1 %copy-start.5 = (bf16[1,1,96,2048]{3,2,1,0:T(8,128)(2,1)S(1)}, bf16[1,1,96,2048]{3,2,1,0:T(8,128)(2,1)}, u32[]{:S(2)}) copy-start(bf16[1,1,96,2048]{3,2,1,0:T(8,128)(2,1)} %param.11) | copy-start | bytes 1179652
  29.3 3.1 %copy-start.6 = (s32[1,1,27,2048]{3,1,2,0:T(1,128)S(1)}, s32[1,1,27,2048]{3,1,2,0:T(1,128)}, u32[]{:S(2)}) copy-start(s32[1,1,27,2048]{3,1,2,0:T(1,128)} %param.8) | copy-start | bytes 663556
  68.1 0.7 copy-start.7
  68.7 16.9 %all-to-all-start.1 = ((bf16[16,128,128]{2,1,0:T(8,128)(2,1)}), bf16[16,128,128]{2,1,0:T(8,128)(2,1)S(1)}, u32[]{:S(2)}, u32[]{:S(2)}) async-start(bf16[16,128,128]{2,1,0:T(8,128)(2,1)} %get-tuple-element.21), calls=%async_computation.1 | async-start | bytes 1048576 | tf_op jit(solution)/shard_map/all_to_all | solution.py:391
  86.6 25.8 %all-to-all-start.2 = ((bf16[16,128,128]{2,1,0:T(8,128)(2,1)}), bf16[16,128,128]{2,1,0:T(8,128)(2,1)S(1)}, u32[]{:S(2)}, u32[]{:S(2)}) async-start(bf16[16,128,128]{2,1,0:T(8,128)(2,1)} %sum_parts.1.after_ref), calls=%async_computation.2 | async-start | bytes 1048576 | tf_op jit(solution)/shard_map/all_to_all | solution.py:391
  95.0 0.9 copy-start.8
  116.1 11.9 %collective-permute-start.2 = (bf16[96,256]{1,0:T(8,128)(2,1)S(1)}, bf16[96,256]{1,0:T(8,128)(2,1)S(1)}, u32[]{:S(2)}, u32[]{:S(2)}) collective-permute-start(bf16[96,256]{1,0:T(8,128)(2,1)S(1)} %get-tuple-element.25), channel_id=1, source_target_pairs={{0,1},{1,2},{2,3},{3,4},{4,5},{5,6},{6,7},{7,8},{8,9},{9,10},{10,1... | collective-permute-start | bytes 147464 | tf_op jit(solution)/shard_map/ppermute | solution.py:400
  118.1 10.0 %copy-start.4 = (s32[1,1,2,256]{3,2,1,0:T(2,128)S(1)}, s32[1,1,2,256]{3,2,1,0:T(2,128)}, u32[]{:S(2)}) copy-start(s32[1,1,2,256]{3,2,1,0:T(2,128)} %param.9) | copy-start | bytes 6148
  118.1 10.0 %collective-permute-start.3 = (bf16[96,256]{1,0:T(8,128)(2,1)S(1)}, bf16[96,256]{1,0:T(8,128)(2,1)S(1)}, u32[]{:S(2)}, u32[]{:S(2)}) collective-permute-start(bf16[96,256]{1,0:T(8,128)(2,1)S(1)} %get-tuple-element.24.after_ref), channel_id=1, source_target_pairs={{1,0},{2,1},{3,2},{4,3},{5,4},{6,5},{7,6},{8,7},{9,8},{10,9},{11,1... | collective-permute-start | bytes 147464 | tf_op jit(solution)/shard_map/ppermute | solution.py:401
  128.5 22.7 %copy-start.2 = (s32[1,1,1024,1]{2,3,1,0:T(1,128)S(1)}, s32[1,1,1024,1]{2,3,1,0:T(1,128)}, u32[]{:S(2)}) copy-start(s32[1,1,1024,1]{2,3,1,0:T(1,128)} %param.7) | copy-start | bytes 12292

commit v9 on v8

--- a/solution.py
+++ b/solution.py
@@ -18,11 +18,11 @@
 LO = 256
 BANKS = V // LO
 ALL_BANKS = BANKS + 2
-WIDE = 256
+WIDE = 512
 WIDE_BANKS = ALL_BANKS * LO // WIDE
 VB = 256
 FORWARD_VB = 512
-MAIN = 48
+MAIN = 64
 PER_DOT = 3
 PARTS = (3, 3, 2)
 LANES = 128
@@ -246,7 +246,7 @@
     return jnp.concatenate([jnp.where((bank16 == a)[None], values, BF(0)).reshape(C, n) for a in banks], axis=0)
 
 
-def scatter_kernel(banks, has_start, after_ref, start_ref, map_ref, weight_ref, pre_ref, *refs):
+def scatter_kernel(has_start, after_ref, start_ref, map_ref, weight_ref, pre_ref, *refs):
     *out_refs, spread_ref, acc_ref = refs
 
     @pl.when(pl.program_id(0) == 0)
@@ -258,7 +258,7 @@
         spreads, hots = [], []
         for k in range(first, first + PER_DOT):
             index = map_ref[k]
-            spreads.append(bank_rows(spread_ref[k * C : (k + 1) * C, :], index >> 8, banks))
+            spreads.append(bank_rows(spread_ref[k * C : (k + 1) * C, :], index >> 8, range(ALL_BANKS)))
             hots.append(onehot_rows(index & (LO - 1), LO))
         acc_ref[...] += lax.dot_general(
             jnp.concatenate(spreads, axis=1), jnp.concatenate(hots, axis=1), NT, preferred_element_type=F32
@@ -266,27 +266,29 @@
 
     @pl.when(pl.program_id(0) == pl.num_programs(0) - 1)
     def _():
-        rows = acc_ref.shape[0] // len(out_refs)
-        for i, out_ref in enumerate(out_refs):
-            out_ref[...] = acc_ref[i * rows : (i + 1) * rows, :].astype(out_ref.dtype)
-
-
-def scatter_part(part, banks, after, start, kernel_map, weight, grad_pre, split=1, dtype=F32):
+        at = 0
+        for out_ref in out_refs:
+            rows = out_ref.shape[0]
+            out_ref[...] = acc_ref[at : at + rows, :].astype(out_ref.dtype)
+            at += rows
+
+
+def scatter_part(part, after, start, kernel_map, weight, grad_pre):
     whole = lambda *shape: pl.BlockSpec(shape, lambda i: (0,) * len(shape))
-    rows, at, steps = len(banks) * C, sum(PARTS[:part]), PARTS[part]
-    start_spec = pl.BlockSpec((rows, LO), lambda i: (banks[0] // len(banks), 0))
-    return pl.pallas_call(
-        functools.partial(scatter_kernel, banks, part > 0),
+    rows, at, steps = ALL_BANKS * C, sum(PARTS[:part]), PARTS[part]
+    outs = [(rows, F32)] if part < len(PARTS) - 1 else [(BANKS * C, F32), (C, BF), (C, BF)]
+    return pl.pallas_call(
+        functools.partial(scatter_kernel, part > 0),
         grid=(steps,),
         in_specs=[
             pl.BlockSpec(memory_space=pl.ANY),
-            start_spec if part > 0 else pl.BlockSpec(memory_space=pl.ANY),
+            whole(rows, LO) if part > 0 else pl.BlockSpec(memory_space=pl.ANY),
             pl.BlockSpec((K, 1, VB), lambda i: (0, 0, at + i)),
             whole(K * C, C),
             pl.BlockSpec((C, VB), lambda i: (0, i)),
         ],
-        out_specs=(whole(rows // split, LO),) * split,
-        out_shape=(jax.ShapeDtypeStruct((rows // split, LO), dtype),) * split,
+        out_specs=tuple(whole(n, LO) for n, _ in outs),
+        out_shape=tuple(jax.ShapeDtypeStruct((n, LO), dtype) for n, dtype in outs),
         scratch_shapes=[pltpu.VMEM((K * C, VB), BF), pltpu.VMEM((rows, LO), F32)],
         compiler_params=pltpu.CompilerParams(vmem_limit_bytes=24 << 20),
         cost_estimate=pl.CostEstimate(
@@ -389,14 +391,12 @@
     weight_columns = jnp.transpose(weight, (0, 2, 1)).reshape(K * C, C)
     scatter = functools.partial(scatter_part, kernel_map=kernel_map, weight=weight_columns, grad_pre=grad_pre)
     across = lambda array, axis: lax.all_to_all(array, axis, 0, 0, tiled=True)
-    every = range(ALL_BANKS)
     parts = across(weight_part, "sx")
-    (sums,) = scatter(0, every, grad_pre[0], grad_pre[0])
+    (sums,) = scatter(0, grad_pre[0], grad_pre[0])
     row_sums = sum_parts(sums, parts)
     parts = across(row_sums, "sy")
-    (sums,) = scatter(1, every, row_sums, sums)
-    to_low, to_high = scatter(2, every[BANKS:], parts, sums, split=2, dtype=BF)
-    (table_grad,) = scatter(2, every[:BANKS], to_low, sums)
+    (sums,) = scatter(1, row_sums, sums)
+    table_grad, to_low, to_high = scatter(2, parts, sums)
     from_low = lax.ppermute(to_high, "sy", up)
     from_high = lax.ppermute(to_low, "sy", down)
     owned_grad = fold_faces(table_grad, from_low, from_high, face_list, parts)

time: 154 us -> 144 us (0.935)
  Pallas kernels: 78.7 us -> 67.3 us
  waiting for transfers between devices: 5.69 us -> 8.68 us
  blocking collectives: 39.3 us -> 37.7 us
    pallas_call x1, Pallas kernels: 35.7 us -> 26.6 us  [forward_pass(): pl.pallas_call(forward_kernel, grid=(V // FORWARD_VB,), in_specs=[whole(G...]
    ppermute x1, waiting for transfers between devices: 0.01 us -> 2.99 us  [body(): from_high = lax.ppermute(to_low, 'sy', down)]
    pallas_call x4 -> x3, Pallas kernels: 37.5 us -> 35.1 us  [scatter_part(): pl.pallas_call(functools.partial(scatter_kernel, part > 0), grid=(steps,)...]
    all_to_all x1, blocking collectives: 22.7 us -> 21.2 us  [body(): across = lambda array, axis: lax.all_to_all(array, axis, 0, 0, tiled=True)]
  transfers between devices with their start and end apart: 6 -> 6, of which waited for: 2 -> 3; matrix products, arithmetic and copies ran while one was open for 1% -> 1% of each run, Pallas kernels for 22% -> 18%
where the time goes in v9:
time: 144 us; the launch traced here: 143 us
  Pallas kernels  67.3 us (47%)
  blocking collectives  37.7 us (26%)
  starting transfers between devices  23.7 us (16%)
  waiting for transfers between devices  8.68 us (6%)
  local copies, waits for them, and re-layouts  4.87 us (3%)
    pallas_call x3, Pallas kernels, scatter_part(): pl.pallas_call(functools.partial(scatter_kernel, part > 0), grid=(steps,)...  35.1 us
    pallas_call x1, Pallas kernels, forward_pass(): pl.pallas_call(forward_kernel, grid=(V // FORWARD_VB,), in_specs=[whole(G...  26.6 us
    all_to_all x1, blocking collectives, body(): across = lambda array, axis: lax.all_to_all(array, axis, 0, 0, tiled=True)  21.2 us
    all_to_all x1, blocking collectives, body(): owned = lax.all_to_all(outgoing, 'sx', 0, 0, tiled=True)  16.6 us
    all_to_all x2, starting transfers between devices, body(): across = lambda array, axis: lax.all_to_all(array, axis, 0, 0, tiled=True)  12.2 us
    ppermute x1, starting transfers between devices, body(): ghost_low = lax.ppermute(upper, 'sy', up)  5.29 us
    unnamed x20, local copies, waits for them, and re-layouts  3.88 us
    all_to_all x2, waiting for transfers between devices, body(): across = lambda array, axis: lax.all_to_all(array, axis, 0, 0, tiled=True)  3.25 us
  transfers between devices with their start and end apart: 6, of which 3 were waited for; matrix products, arithmetic and copies ran while one was open for 1% of the time, Pallas kernels for 18%

profile of v9, /device:TPU:1, one launch (start us, length us, event | category | flops | bytes accessed | tf_op | source)
XLA Modules:
  0.0 143.1 jit_solution(7754953237579397700)
XLA Ops:
  0.6 0.0 copy-start
  0.6 0.9 copy-done
  1.6 0.0 copy-start.1
  1.6 0.7 copy-done.1
  2.2 0.0 copy-start.9
  2.2 1.6 %place.1 = (bf16[16,96,128]{2,1,0:T(8,128)(2,1)S(1)}, s32[1,1024]{1,0:T(1,128)S(1)}) custom-call(bf16[96,1024]{1,0:T(8,128)(2,1)S(1)} %bitcast.14, s32[1,1024]{1,0:T(1,128)S(1)} %bitcast.15), custom_call_target="tpu_custom_call" | custom-call | tf_op jit(solution)/shard_map/place/pallas_call | solution.py:119
  3.9 16.6 %all_to_all.20.owned_ref = bf16[16,96,128]{2,1,0:T(8,128)(2,1)S(1)} all-to-all(bf16[16,96,128]{2,1,0:T(8,128)(2,1)S(1)} %get-tuple-element.17), channel_id=1, replica_groups=mesh['sx'=16,'sy'=16] {'sx'}, dimensions={0} | all-to-all | bytes 786432 | tf_op jit(solution)/shard_map/all_to_all | solution.py:383
  20.4 0.0 copy-start.3
  20.5 0.7 copy-done.3
  21.1 0.5 faces.1
  21.7 5.3 %collective-permute-start = (bf16[96,256]{1,0:T(8,128)(2,1)S(1)}, bf16[96,256]{1,0:T(8,128)(2,1)S(1)}, u32[]{:S(2)}, u32[]{:S(2)}) collective-permute-start(bf16[96,256]{1,0:T(8,128)(2,1)S(1)} %get-tuple-element.18), channel_id=1, source_target_pairs={{0,1},{1,2},{2,3},{3,4},{4,5},{5,6},{6,7},{7,8},{8,9},{9,10},{10,1... | collective-permute-start | bytes 147464 | tf_op jit(solution)/shard_map/ppermute | solution.py:385
  27.0 1.9 %collective-permute-start.1 = (bf16[96,256]{1,0:T(8,128)(2,1)S(1)}, bf16[96,256]{1,0:T(8,128)(2,1)S(1)}, u32[]{:S(2)}, u32[]{:S(2)}) collective-permute-start(bf16[96,256]{1,0:T(8,128)(2,1)S(1)} %get-tuple-element.19), channel_id=1, source_target_pairs={{1,0},{2,1},{3,2},{4,3},{5,4},{6,5},{7,6},{8,7},{9,8},{10,9},{11,1... | collective-permute-start | bytes 147464 | tf_op jit(solution)/shard_map/ppermute | solution.py:386
  28.9 0.0 copy-done.9
  28.9 0.3 copy.11
  29.3 0.0 copy-start.5
  29.3 0.0 copy-start.6
  29.3 0.3 copy.12.weight_ref
  29.6 0.3 copy.13
  30.0 0.0 collective-permute-done.low_ref
  30.0 2.4 %collective-permute-done.1.high_ref = bf16[96,256]{1,0:T(8,128)(2,1)S(1)} collective-permute-done((bf16[96,256]{1,0:T(8,128)(2,1)S(1)}, bf16[96,256]{1,0:T(8,128)(2,1)S(1)}, u32[]{:S(2)}, u32[]{:S(2)}) %collective-permute-start.1) | collective-permute-done | bytes 49184 | tf_op jit(solution)/shard_map/ppermute | solution.py:386
  32.4 0.0 copy-done.5
  32.4 0.0 copy-done.6
  32.4 26.6 %gather_forward.1 = (bf16[96,2048]{1,0:T(8,128)(2,1)}, bf16[96,768]{1,0:T(8,128)(2,1)S(1)}, bf16[96,768]{1,0:T(8,128)(2,1)S(1)}, bf16[96,512]{1,0:T(8,128)(2,1)S(1)}, bf16[16,128,128]{2,1,0:T(8,128)(2,1)}) custom-call(bf16[16,96,128]{2,1,0:T(8,128)(2,1)S(1)} %all_to_all.20.owned_ref, bf16[96,256]{1,0:T(8,128)(2,1)S(1)} %collective-permute-done.low_ref, ...), custom_call_target="tpu_custom_call" | custom-call | flops 27179089920 | bytes 4194304 | tf_op jit(solution)/shard_map/gather_forward/pallas_call | solution.py:211
  59.0 0.0 copy-start.7
  59.0 0.7 copy-done.7
  59.7 3.8 %all-to-all-start.1 = ((bf16[16,128,128]{2,1,0:T(8,128)(2,1)}), bf16[16,128,128]{2,1,0:T(8,128)(2,1)S(1)}, u32[]{:S(2)}, u32[]{:S(2)}) async-start(bf16[16,128,128]{2,1,0:T(8,128)(2,1)} %get-tuple-element.22), calls=%async_computation.1 | async-start | bytes 1048576 | tf_op jit(solution)/shard_map/all_to_all | solution.py:393
  63.4 13.2 %scatter.3.after_ref.start_ref = f32[960,256]{1,0:T(8,128)S(1)} custom-call(bf16[96,768]{1,0:T(8,128)(2,1)S(1)} %get-tuple-element.21.after_ref.start_ref.pre_ref, bf16[96,768]{1,0:T(8,128)(2,1)S(1)} %get-tuple-element.21.after_ref.start_ref.pre_ref, s32[27,1,2048]{2,1,0:T(1,128)S(1)} %bitcast.21, bf16[2592,96]{1,0:T(8,128)(2,1)S(1)} %bitcast.11, ...), custom_call_target="tpu_custom_call" | custom-call | flops 10192158720 | bytes 2097152 | tf_op jit(solution)/shard_map/scatter/pallas_call | solution.py:280
  76.6 0.0 all-to-all-done.1.parts_ref
  76.6 0.9 sum_parts.1.after_ref
  77.5 8.4 %all-to-all-start.2 = ((bf16[16,128,128]{2,1,0:T(8,128)(2,1)}), bf16[16,128,128]{2,1,0:T(8,128)(2,1)S(1)}, u32[]{:S(2)}, u32[]{:S(2)}) async-start(bf16[16,128,128]{2,1,0:T(8,128)(2,1)} %sum_parts.1.after_ref), calls=%async_computation.2 | async-start | bytes 1048576 | tf_op jit(solution)/shard_map/all_to_all | solution.py:393
  85.9 0.0 copy-start.8
  85.9 0.9 copy-done.8
  86.8 13.2 %scatter.4.start_ref = f32[960,256]{1,0:T(8,128)S(1)} custom-call(bf16[16,128,128]{2,1,0:T(8,128)(2,1)} %sum_parts.1.after_ref, f32[960,256]{1,0:T(8,128)S(1)} %scatter.3.after_ref.start_ref, s32[27,1,2048]{2,1,0:T(1,128)S(1)} %bitcast.22, bf16[2592,96]{1,0:T(8,128)(2,1)S(1)} %bitcast.12, bf16[96,768]{1,0:T(8,128)(2,1)S(1)} %copy-done.8), custom_call_target="tpu_custom_call" | custom-call | flops 10192158720 | bytes 2097152 | tf_op jit(solution)/shard_map/scatter/pallas_call | solution.py:280
  100.0 3.2 %all-to-all-done.2.after_ref.parts_ref = bf16[16,128,128]{2,1,0:T(8,128)(2,1)S(1)} async-done(((bf16[16,128,128]{2,1,0:T(8,128)(2,1)}), bf16[16,128,128]{2,1,0:T(8,128)(2,1)S(1)}, u32[]{:S(2)}, u32[]{:S(2)}) %all-to-all-start.2) | async-done | bytes 524320 | tf_op jit(solution)/shard_map/all_to_all | solution.py:393
  103.2 0.0 copy-start.4
  103.2 8.8 %scatter.5 = (f32[768,256]{1,0:T(8,128)S(1)}, bf16[96,256]{1,0:T(8,128)(2,1)S(1)}, bf16[96,256]{1,0:T(8,128)(2,1)S(1)}) custom-call(bf16[16,128,128]{2,1,0:T(8,128)(2,1)S(1)} %all-to-all-done.2.after_ref.parts_ref, f32[960,256]{1,0:T(8,128)S(1)} %scatter.4.start_ref, s32[27,1,2048]{2,1,0:T(1,128)S(1)} %bitcast.23, bf16[2592,96]{1,0:T(8,128)(2,1)S(1)} %bitcast.13, ...), custom_call_target="tpu_custom_call" | custom-call | flops 6794772480 | bytes 2097152 | tf_op jit(solution)/shard_map/scatter/pallas_call | solution.py:280
  112.1 1.9 %collective-permute-start.2 = (bf16[96,256]{1,0:T(8,128)(2,1)S(1)}, bf16[96,256]{1,0:T(8,128)(2,1)S(1)}, u32[]{:S(2)}, u32[]{:S(2)}) collective-permute-start(bf16[96,256]{1,0:T(8,128)(2,1)S(1)} %get-tuple-element.26), channel_id=1, source_target_pairs={{0,1},{1,2},{2,3},{3,4},{4,5},{5,6},{6,7},{7,8},{8,9},{9,10},{10,1... | collective-permute-start | bytes 147464 | tf_op jit(solution)/shard_map/ppermute | solution.py:400
  114.0 2.4 %collective-permute-start.3 = (bf16[96,256]{1,0:T(8,128)(2,1)S(1)}, bf16[96,256]{1,0:T(8,128)(2,1)S(1)}, u32[]{:S(2)}, u32[]{:S(2)}) collective-permute-start(bf16[96,256]{1,0:T(8,128)(2,1)S(1)} %get-tuple-element.27), channel_id=1, source_target_pairs={{1,0},{2,1},{3,2},{4,3},{5,4},{6,5},{7,6},{8,7},{9,8},{10,9},{11,1... | collective-permute-start | bytes 147464 | tf_op jit(solution)/shard_map/ppermute | solution.py:401
  116.4 0.0 collective-permute-done.2.from_low_ref
  116.4 3.0 %collective-permute-done.3.from_high_ref = bf16[96,256]{1,0:T(8,128)(2,1)S(1)} collective-permute-done((bf16[96,256]{1,0:T(8,128)(2,1)S(1)}, bf16[96,256]{1,0:T(8,128)(2,1)S(1)}, u32[]{:S(2)}, u32[]{:S(2)}) %collective-permute-start.3) | collective-permute-done | bytes 49184 | tf_op jit(solution)/shard_map/ppermute | solution.py:401
  119.4 0.0 copy-done.4
  119.4 0.4 fold.1
  119.8 0.0 copy-start.2
  119.8 21.2 %all_to_all.21.back_ref = bf16[16,224,128]{2,1,0:T(8,128)(2,1)S(1)} all-to-all(bf16[16,224,128]{2,1,0:T(8,128)(2,1)S(1)} %fold.1), channel_id=1, replica_groups=mesh['sx'=16,'sy'=16] {'sx'}, dimensions={0} | all-to-all | bytes 1835008 | tf_op jit(solution)/shard_map/all_to_all | solution.py:393
  141.0 0.0 copy-done.2
  141.0 2.1 %finish.1 = (bf16[96,1024]{1,0:T(8,128)(2,1)}, f32[27,96,96]{2,1,0:T(8,128)}) custom-call(bf16[16,224,128]{2,1,0:T(8,128)(2,1)S(1)} %all_to_all.21.back_ref, s32[1,1024]{1,0:T(1,128)S(1)} %bitcast.16, s32[1,1024]{1,0:T(1,128)S(1)} %get-tuple-element.28.slot_ref), custom_call_target="tpu_custom_call" | custom-call | tf_op jit(solution)/shard_map/finish/pallas_call | solution.py:366
Async XLA Ops:
  0.6 0.9 copy-start
  1.6 0.7 copy-start.1
  2.2 26.7 %copy-start.9 = (bf16[27,96,96]{2,1,0:T(8,128)(2,1)S(1)}, bf16[27,96,96]{2,1,0:T(8,128)(2,1)}, u32[]{:S(2)}) copy-start(bf16[27,96,96]{2,1,0:T(8,128)(2,1)} %param.10) | copy-start | bytes 1492996
  20.4 0.7 copy-start.3
  21.7 8.3 %collective-permute-start = (bf16[96,256]{1,0:T(8,128)(2,1)S(1)}, bf16[96,256]{1,0:T(8,128)(2,1)S(1)}, u32[]{:S(2)}, u32[]{:S(2)}) collective-permute-start(bf16[96,256]{1,0:T(8,128)(2,1)S(1)} %get-tuple-element.18), channel_id=1, source_target_pairs={{0,1},{1,2},{2,3},{3,4},{4,5},{5,6},{6,7},{7,8},{8,9},{9,10},{10,1... | collective-permute-start | bytes 147464 | tf_op jit(solution)/shard_map/ppermute | solution.py:385
  27.0 5.4 %collective-permute-start.1 = (bf16[96,256]{1,0:T(8,128)(2,1)S(1)}, bf16[96,256]{1,0:T(8,128)(2,1)S(1)}, u32[]{:S(2)}, u32[]{:S(2)}) collective-permute-start(bf16[96,256]{1,0:T(8,128)(2,1)S(1)} %get-tuple-element.19), channel_id=1, source_target_pairs={{1,0},{2,1},{3,2},{4,3},{5,4},{6,5},{7,6},{8,7},{9,8},{10,9},{11,1... | collective-permute-start | bytes 147464 | tf_op jit(solution)/shard_map/ppermute | solution.py:386
  29.3 3.1 %copy-start.5 = (bf16[1,1,96,2048]{3,2,1,0:T(8,128)(2,1)S(1)}, bf16[1,1,96,2048]{3,2,1,0:T(8,128)(2,1)}, u32[]{:S(2)}) copy-start(bf16[1,1,96,2048]{3,2,1,0:T(8,128)(2,1)} %param.11) | copy-start | bytes 1179652
  29.3 3.1 %copy-start.6 = (s32[1,1,27,2048]{3,1,2,0:T(1,128)S(1)}, s32[1,1,27,2048]{3,1,2,0:T(1,128)}, u32[]{:S(2)}) copy-start(s32[1,1,27,2048]{3,1,2,0:T(1,128)} %param.8) | copy-start | bytes 663556
  59.0 0.7 copy-start.7
  59.7 16.9 %all-to-all-start.1 = ((bf16[16,128,128]{2,1,0:T(8,128)(2,1)}), bf16[16,128,128]{2,1,0:T(8,128)(2,1)S(1)}, u32[]{:S(2)}, u32[]{:S(2)}) async-start(bf16[16,128,128]{2,1,0:T(8,128)(2,1)} %get-tuple-element.22), calls=%async_computation.1 | async-start | bytes 1048576 | tf_op jit(solution)/shard_map/all_to_all | solution.py:393
  77.5 25.8 %all-to-all-start.2 = ((bf16[16,128,128]{2,1,0:T(8,128)(2,1)}), bf16[16,128,128]{2,1,0:T(8,128)(2,1)S(1)}, u32[]{:S(2)}, u32[]{:S(2)}) async-start(bf16[16,128,128]{2,1,0:T(8,128)(2,1)} %sum_parts.1.after_ref), calls=%async_computation.2 | async-start | bytes 1048576 | tf_op jit(solution)/shard_map/all_to_all | solution.py:393
  85.9 0.9 copy-start.8
  103.2 16.2 %copy-start.4 = (s32[1,1,2,256]{3,2,1,0:T(2,128)S(1)}, s32[1,1,2,256]{3,2,1,0:T(2,128)}, u32[]{:S(2)}) copy-start(s32[1,1,2,256]{3,2,1,0:T(2,128)} %param.9) | copy-start | bytes 6148
  112.1 4.3 %collective-permute-start.2 = (bf16[96,256]{1,0:T(8,128)(2,1)S(1)}, bf16[96,256]{1,0:T(8,128)(2,1)S(1)}, u32[]{:S(2)}, u32[]{:S(2)}) collective-permute-start(bf16[96,256]{1,0:T(8,128)(2,1)S(1)} %get-tuple-element.26), channel_id=1, source_target_pairs={{0,1},{1,2},{2,3},{3,4},{4,5},{5,6},{6,7},{7,8},{8,9},{9,10},{10,1... | collective-permute-start | bytes 147464 | tf_op jit(solution)/shard_map/ppermute | solution.py:400
  114.0 5.4 %collective-permute-start.3 = (bf16[96,256]{1,0:T(8,128)(2,1)S(1)}, bf16[96,256]{1,0:T(8,128)(2,1)S(1)}, u32[]{:S(2)}, u32[]{:S(2)}) collective-permute-start(bf16[96,256]{1,0:T(8,128)(2,1)S(1)} %get-tuple-element.27), channel_id=1, source_target_pairs={{1,0},{2,1},{3,2},{4,3},{5,4},{6,5},{7,6},{8,7},{9,8},{10,9},{11,1... | collective-permute-start | bytes 147464 | tf_op jit(solution)/shard_map/ppermute | solution.py:401
  119.8 21.2 %copy-start.2 = (s32[1,1,1024,1]{2,3,1,0:T(1,128)S(1)}, s32[1,1,1024,1]{2,3,1,0:T(1,128)}, u32[]{:S(2)}) copy-start(s32[1,1,1024,1]{2,3,1,0:T(1,128)} %param.7) | copy-start | bytes 12292

commit v10 on v9

--- a/solution.py
+++ b/solution.py
@@ -94,8 +94,8 @@
     return divmod(i * TILES + t if t < TILES else (C // 16) * TILES + i, SHARD_TILES)
 
 
-def place_kernel(points_ref, owner_ref, out_ref, slot_ref, masked_ref):
-    owner = owner_ref[...]
+def place_kernel(points_ref, lists_ref, out_ref, slot_ref, masked_ref):
+    owner = lists_ref[:, :R]
     row = lax.broadcasted_iota(jnp.int32, (CAP, CAP), 0)
     col = lax.broadcasted_iota(jnp.int32, (CAP, CAP), 1)
     earlier = jnp.where(row < col, 1.0, 0.0).astype(BF)
@@ -115,7 +115,7 @@
         ).astype(BF)
 
 
-def place_points(points, owner):
+def place_points(points, lists):
     return pl.pallas_call(
         place_kernel,
         out_shape=(
@@ -125,24 +125,24 @@
         scratch_shapes=[pltpu.VMEM((GROUPS * C, R), BF)],
         compiler_params=pltpu.CompilerParams(vmem_limit_bytes=16 << 20),
         name="place",
-    )(points, owner)
-
-
-def faces_kernel(owned_ref, rows_ref, lower_ref, upper_ref):
+    )(points, lists)
+
+
+def faces_kernel(owned_ref, lists_ref, lower_ref, upper_ref):
     table = owned_ref[...].reshape(GROUPS * C, CAP)
     for j, out_ref in enumerate((lower_ref, upper_ref)):
-        rows = rows_ref[j : j + 1, :]
+        rows = lists_ref[:, R + j * F : R + (j + 1) * F]
         product = jnp.dot(table, onehot_rows(rows & (CAP - 1), CAP), preferred_element_type=F32)
         out_ref[...] = select_banks(product, rows >> 7, GROUPS).astype(BF)
 
 
-def take_faces(owned, face_rows):
+def take_faces(owned, lists):
     return pl.pallas_call(
         faces_kernel,
         out_shape=(jax.ShapeDtypeStruct((C, F), BF),) * 2,
         compiler_params=pltpu.CompilerParams(vmem_limit_bytes=16 << 20),
         name="faces",
-    )(owned, face_rows)
+    )(owned, lists)
 
 
 def forward_kernel(
@@ -321,11 +321,11 @@
     )(after, parts)
 
 
-def fold_kernel(grad_ref, from_low_ref, from_high_ref, rows_ref, parts_ref, out_ref, masked_ref):
+def fold_kernel(grad_ref, from_low_ref, from_high_ref, lists_ref, parts_ref, out_ref, masked_ref):
     share = total_of(parts_ref)
     hots = []
     for j, part_ref in enumerate((from_low_ref, from_high_ref)):
-        rows = rows_ref[j : j + 1, :]
+        rows = lists_ref[:, R + j * F : R + (j + 1) * F]
         masked_banks(part_ref[...], rows >> 8, BANKS, masked_ref, j * F)
         hots.append(onehot_rows(rows & (LO - 1), LO))
     folded = lax.dot_general(
@@ -337,22 +337,22 @@
         out_ref[g, C:, :] = share
 
 
-def fold_faces(table_grad, from_low, from_high, face_rows, parts):
+def fold_faces(table_grad, from_low, from_high, lists, parts):
     return pl.pallas_call(
         fold_kernel,
         out_shape=jax.ShapeDtypeStruct((GROUPS, C + LANES, CAP), BF),
         scratch_shapes=[pltpu.VMEM((BANKS * C, 2 * F), BF)],
         compiler_params=pltpu.CompilerParams(vmem_limit_bytes=16 << 20),
         name="fold",
-    )(table_grad, from_low, from_high, face_rows, parts)
-
-
-def finish_kernel(scale, back_ref, owner_ref, slot_ref, out_ref, wg_ref, flat_ref):
+    )(table_grad, from_low, from_high, lists, parts)
+
+
+def finish_kernel(scale, back_ref, lists_ref, slot_ref, out_ref, wg_ref, flat_ref):
     table = back_ref[:, :C, :].reshape(GROUPS * C, CAP)
     for b in range(R // LO):
         cols = slice(b * LO, (b + 1) * LO)
         product = jnp.dot(table, onehot_rows(slot_ref[:, cols], CAP), preferred_element_type=F32)
-        out_ref[:, cols] = select_banks(product, owner_ref[:, cols], GROUPS).astype(BF)
+        out_ref[:, cols] = select_banks(product, lists_ref[:, cols], GROUPS).astype(BF)
     for t in range(TILES + 1):
         for i in range(C // 16):
             shard, slot = tile_place(i, t)
@@ -362,26 +362,26 @@
         wg_ref[k] = flat_ref[:, k * C : (k + 1) * C]
 
 
-def finish(returned, owner, slot, scale):
+def finish(returned, lists, slot, scale):
     return pl.pallas_call(
         functools.partial(finish_kernel, scale),
         out_shape=(jax.ShapeDtypeStruct((C, R), BF), jax.ShapeDtypeStruct((K, C, C), F32)),
         scratch_shapes=[pltpu.VMEM((C, (TILES + 1) * LANES), F32)],
         compiler_params=pltpu.CompilerParams(vmem_limit_bytes=24 << 20),
         name="finish",
-    )(returned, owner, slot)
+    )(returned, lists, slot)
 
 
 def body(points, owners, kernel_maps, face_rows, weight, cotangent):
-    points, owner = points[0, 0], owners.reshape(1, R)
-    kernel_map, face_list, incoming = kernel_maps.reshape(K, 1, V), face_rows[0, 0], cotangent[0, 0]
+    points, kernel_map, incoming = points[0, 0], kernel_maps.reshape(K, 1, V), cotangent[0, 0]
+    lists = jnp.concatenate([owners.reshape(1, R), face_rows.reshape(1, 2 * F)], axis=1)
     side = lax.axis_size("sy")
     up = [(i, i + 1) for i in range(side - 1)]
     down = [(i + 1, i) for i in range(side - 1)]
 
-    outgoing, slot = place_points(points, owner)
+    outgoing, slot = place_points(points, lists)
     owned = lax.all_to_all(outgoing, "sx", 0, 0, tiled=True)
-    lower, upper = take_faces(owned, face_list)
+    lower, upper = take_faces(owned, lists)
     ghost_low = lax.ppermute(upper, "sy", up)
     ghost_high = lax.ppermute(lower, "sy", down)
     weight_rows = jnp.transpose(weight, (1, 0, 2)).reshape(C, K * C)
@@ -399,10 +399,10 @@
     table_grad, to_low, to_high = scatter(2, parts, sums)
     from_low = lax.ppermute(to_high, "sy", up)
     from_high = lax.ppermute(to_low, "sy", down)
-    owned_grad = fold_faces(table_grad, from_low, from_high, face_list, parts)
+    owned_grad = fold_faces(table_grad, from_low, from_high, lists, parts)
     returned = across(owned_grad, "sx")
     scale = 1.0 / math.sqrt(GROUPS * side * V)
-    point_grad, weight_grad = finish(returned, owner, slot, scale)
+    point_grad, weight_grad = finish(returned, lists, slot, scale)
     return (output[None, None], point_grad[None, None], weight_grad)
 
 

time: 144 us -> 144 us (level)
    unnamed x20 -> x13, local copies, waits for them, and re-layouts: 3.88 us -> 3.19 us
where the time goes in v10:
time: 144 us; the launch traced here: 143 us
  Pallas kernels  67.3 us (47%)
  blocking collectives  37.7 us (26%)
  starting transfers between devices  23.8 us (17%)
  waiting for transfers between devices  8.68 us (6%)
  local copies, waits for them, and re-layouts  4.18 us (3%)
    pallas_call x3, Pallas kernels, scatter_part(): pl.pallas_call(functools.partial(scatter_kernel, part > 0), grid=(steps,)...  35.1 us
    pallas_call x1, Pallas kernels, forward_pass(): pl.pallas_call(forward_kernel, grid=(V // FORWARD_VB,), in_specs=[whole(G...  26.6 us
    all_to_all x1, blocking collectives, body(): across = lambda array, axis: lax.all_to_all(array, axis, 0, 0, tiled=True)  21.2 us
    all_to_all x1, blocking collectives, body(): owned = lax.all_to_all(outgoing, 'sx', 0, 0, tiled=True)  16.6 us
    all_to_all x2, starting transfers between devices, body(): across = lambda array, axis: lax.all_to_all(array, axis, 0, 0, tiled=True)  12.2 us
    ppermute x1, starting transfers between devices, body(): ghost_low = lax.ppermute(upper, 'sy', up)  5.3 us
    all_to_all x2, waiting for transfers between devices, body(): across = lambda array, axis: lax.all_to_all(array, axis, 0, 0, tiled=True)  3.25 us
    unnamed x13, local copies, waits for them, and re-layouts  3.19 us
  transfers between devices with their start and end apart: 6, of which 3 were waited for; matrix products, arithmetic and copies ran while one was open for 1% of the time, Pallas kernels for 18%

profile of v10, /device:TPU:1, one launch (start us, length us, event | category | flops | bytes accessed | tf_op | source)
XLA Modules:
  0.0 143.1 jit_solution(5986819661718646414)
XLA Ops:
  0.6 0.7 copy.14
  1.3 0.7 pad_add_fusion.lists_ref
  2.0 0.0 copy-start
  2.0 0.9 copy-done
  2.9 0.0 copy-start.5
  2.9 1.6 %place.1 = (bf16[16,96,128]{2,1,0:T(8,128)(2,1)S(1)}, s32[1,1024]{1,0:T(1,128)S(1)}) custom-call(bf16[96,1024]{1,0:T(8,128)(2,1)S(1)} %bitcast.16, s32[1,1536]{1,0:T(1,128)S(1)} %pad_add_fusion.lists_ref), custom_call_target="tpu_custom_call" | custom-call | tf_op jit(solution)/shard_map/place/pallas_call | solution.py:119
  4.6 16.6 %all_to_all.20.owned_ref = bf16[16,96,128]{2,1,0:T(8,128)(2,1)S(1)} all-to-all(bf16[16,96,128]{2,1,0:T(8,128)(2,1)S(1)} %get-tuple-element.17), channel_id=1, replica_groups=mesh['sx'=16,'sy'=16] {'sx'}, dimensions={0} | all-to-all | bytes 786432 | tf_op jit(solution)/shard_map/all_to_all | solution.py:383
  21.1 0.5 faces.1
  21.7 5.3 %collective-permute-start = (bf16[96,256]{1,0:T(8,128)(2,1)S(1)}, bf16[96,256]{1,0:T(8,128)(2,1)S(1)}, u32[]{:S(2)}, u32[]{:S(2)}) collective-permute-start(bf16[96,256]{1,0:T(8,128)(2,1)S(1)} %get-tuple-element.18), channel_id=1, source_target_pairs={{0,1},{1,2},{2,3},{3,4},{4,5},{5,6},{6,7},{7,8},{8,9},{9,10},{10,1... | collective-permute-start | bytes 147464 | tf_op jit(solution)/shard_map/ppermute | solution.py:385
  27.0 1.9 %collective-permute-start.1 = (bf16[96,256]{1,0:T(8,128)(2,1)S(1)}, bf16[96,256]{1,0:T(8,128)(2,1)S(1)}, u32[]{:S(2)}, u32[]{:S(2)}) collective-permute-start(bf16[96,256]{1,0:T(8,128)(2,1)S(1)} %get-tuple-element.19), channel_id=1, source_target_pairs={{1,0},{2,1},{3,2},{4,3},{5,4},{6,5},{7,6},{8,7},{9,8},{10,9},{11,1... | collective-permute-start | bytes 147464 | tf_op jit(solution)/shard_map/ppermute | solution.py:386
  28.9 0.0 copy-done.5
  28.9 0.3 copy.11
  29.3 0.0 copy-start.1
  29.3 0.0 copy-start.2
  29.3 0.3 copy.12.weight_ref
  29.6 0.3 copy.13
  30.0 0.0 collective-permute-done.low_ref
  30.0 2.4 %collective-permute-done.1.high_ref = bf16[96,256]{1,0:T(8,128)(2,1)S(1)} collective-permute-done((bf16[96,256]{1,0:T(8,128)(2,1)S(1)}, bf16[96,256]{1,0:T(8,128)(2,1)S(1)}, u32[]{:S(2)}, u32[]{:S(2)}) %collective-permute-start.1) | collective-permute-done | bytes 49184 | tf_op jit(solution)/shard_map/ppermute | solution.py:386
  32.4 0.0 copy-done.1
  32.4 0.0 copy-done.2
  32.4 26.6 %gather_forward.1 = (bf16[96,2048]{1,0:T(8,128)(2,1)}, bf16[96,768]{1,0:T(8,128)(2,1)S(1)}, bf16[96,768]{1,0:T(8,128)(2,1)S(1)}, bf16[96,512]{1,0:T(8,128)(2,1)S(1)}, bf16[16,128,128]{2,1,0:T(8,128)(2,1)}) custom-call(bf16[16,96,128]{2,1,0:T(8,128)(2,1)S(1)} %all_to_all.20.owned_ref, bf16[96,256]{1,0:T(8,128)(2,1)S(1)} %collective-permute-done.low_ref, ...), custom_call_target="tpu_custom_call" | custom-call | flops 27179089920 | bytes 4194304 | tf_op jit(solution)/shard_map/gather_forward/pallas_call | solution.py:211
  59.0 0.0 copy-start.3
  59.0 0.7 copy-done.3
  59.7 3.8 %all-to-all-start.1 = ((bf16[16,128,128]{2,1,0:T(8,128)(2,1)}), bf16[16,128,128]{2,1,0:T(8,128)(2,1)S(1)}, u32[]{:S(2)}, u32[]{:S(2)}) async-start(bf16[16,128,128]{2,1,0:T(8,128)(2,1)} %get-tuple-element.22), calls=%async_computation.1 | async-start | bytes 1048576 | tf_op jit(solution)/shard_map/all_to_all | solution.py:393
  63.4 13.2 %scatter.3.after_ref.start_ref = f32[960,256]{1,0:T(8,128)S(1)} custom-call(bf16[96,768]{1,0:T(8,128)(2,1)S(1)} %get-tuple-element.21.after_ref.start_ref.pre_ref, bf16[96,768]{1,0:T(8,128)(2,1)S(1)} %get-tuple-element.21.after_ref.start_ref.pre_ref, s32[27,1,2048]{2,1,0:T(1,128)S(1)} %bitcast.19, bf16[2592,96]{1,0:T(8,128)(2,1)S(1)} %bitcast.13, ...), custom_call_target="tpu_custom_call" | custom-call | flops 10192158720 | bytes 2097152 | tf_op jit(solution)/shard_map/scatter/pallas_call | solution.py:280
  76.6 0.0 all-to-all-done.1.parts_ref
  76.6 0.9 sum_parts.1.after_ref
  77.5 8.5 %all-to-all-start.2 = ((bf16[16,128,128]{2,1,0:T(8,128)(2,1)}), bf16[16,128,128]{2,1,0:T(8,128)(2,1)S(1)}, u32[]{:S(2)}, u32[]{:S(2)}) async-start(bf16[16,128,128]{2,1,0:T(8,128)(2,1)} %sum_parts.1.after_ref), calls=%async_computation.2 | async-start | bytes 1048576 | tf_op jit(solution)/shard_map/all_to_all | solution.py:393
  85.9 0.0 copy-start.4
  85.9 0.9 copy-done.4
  86.8 13.2 %scatter.4.start_ref = f32[960,256]{1,0:T(8,128)S(1)} custom-call(bf16[16,128,128]{2,1,0:T(8,128)(2,1)} %sum_parts.1.after_ref, f32[960,256]{1,0:T(8,128)S(1)} %scatter.3.after_ref.start_ref, s32[27,1,2048]{2,1,0:T(1,128)S(1)} %bitcast.20, bf16[2592,96]{1,0:T(8,128)(2,1)S(1)} %bitcast.14, bf16[96,768]{1,0:T(8,128)(2,1)S(1)} %copy-done.4), custom_call_target="tpu_custom_call" | custom-call | flops 10192158720 | bytes 2097152 | tf_op jit(solution)/shard_map/scatter/pallas_call | solution.py:280
  100.0 3.2 %all-to-all-done.2.after_ref.parts_ref = bf16[16,128,128]{2,1,0:T(8,128)(2,1)S(1)} async-done(((bf16[16,128,128]{2,1,0:T(8,128)(2,1)}), bf16[16,128,128]{2,1,0:T(8,128)(2,1)S(1)}, u32[]{:S(2)}, u32[]{:S(2)}) %all-to-all-start.2) | async-done | bytes 524320 | tf_op jit(solution)/shard_map/all_to_all | solution.py:393
  103.3 8.8 %scatter.5 = (f32[768,256]{1,0:T(8,128)S(1)}, bf16[96,256]{1,0:T(8,128)(2,1)S(1)}, bf16[96,256]{1,0:T(8,128)(2,1)S(1)}) custom-call(bf16[16,128,128]{2,1,0:T(8,128)(2,1)S(1)} %all-to-all-done.2.after_ref.parts_ref, f32[960,256]{1,0:T(8,128)S(1)} %scatter.4.start_ref, s32[27,1,2048]{2,1,0:T(1,128)S(1)} %bitcast.21, bf16[2592,96]{1,0:T(8,128)(2,1)S(1)} %bitcast.15, ...), custom_call_target="tpu_custom_call" | custom-call | flops 6794772480 | bytes 2097152 | tf_op jit(solution)/shard_map/scatter/pallas_call | solution.py:280
  112.1 1.9 %collective-permute-start.2 = (bf16[96,256]{1,0:T(8,128)(2,1)S(1)}, bf16[96,256]{1,0:T(8,128)(2,1)S(1)}, u32[]{:S(2)}, u32[]{:S(2)}) collective-permute-start(bf16[96,256]{1,0:T(8,128)(2,1)S(1)} %get-tuple-element.26), channel_id=1, source_target_pairs={{0,1},{1,2},{2,3},{3,4},{4,5},{5,6},{6,7},{7,8},{8,9},{9,10},{10,1... | collective-permute-start | bytes 147464 | tf_op jit(solution)/shard_map/ppermute | solution.py:400
  114.0 2.4 %collective-permute-start.3 = (bf16[96,256]{1,0:T(8,128)(2,1)S(1)}, bf16[96,256]{1,0:T(8,128)(2,1)S(1)}, u32[]{:S(2)}, u32[]{:S(2)}) collective-permute-start(bf16[96,256]{1,0:T(8,128)(2,1)S(1)} %get-tuple-element.27), channel_id=1, source_target_pairs={{1,0},{2,1},{3,2},{4,3},{5,4},{6,5},{7,6},{8,7},{9,8},{10,9},{11,1... | collective-permute-start | bytes 147464 | tf_op jit(solution)/shard_map/ppermute | solution.py:401
  116.4 0.0 collective-permute-done.2.from_low_ref
  116.4 3.0 %collective-permute-done.3.from_high_ref = bf16[96,256]{1,0:T(8,128)(2,1)S(1)} collective-permute-done((bf16[96,256]{1,0:T(8,128)(2,1)S(1)}, bf16[96,256]{1,0:T(8,128)(2,1)S(1)}, u32[]{:S(2)}, u32[]{:S(2)}) %collective-permute-start.3) | collective-permute-done | bytes 49184 | tf_op jit(solution)/shard_map/ppermute | solution.py:401
  119.4 0.4 fold.1
  119.8 21.2 %all_to_all.21.back_ref = bf16[16,224,128]{2,1,0:T(8,128)(2,1)S(1)} all-to-all(bf16[16,224,128]{2,1,0:T(8,128)(2,1)S(1)} %fold.1), channel_id=1, replica_groups=mesh['sx'=16,'sy'=16] {'sx'}, dimensions={0} | all-to-all | bytes 1835008 | tf_op jit(solution)/shard_map/all_to_all | solution.py:393
  141.0 2.1 %finish.1 = (bf16[96,1024]{1,0:T(8,128)(2,1)}, f32[27,96,96]{2,1,0:T(8,128)}) custom-call(bf16[16,224,128]{2,1,0:T(8,128)(2,1)S(1)} %all_to_all.21.back_ref, s32[1,1536]{1,0:T(1,128)S(1)} %pad_add_fusion.lists_ref, s32[1,1024]{1,0:T(1,128)S(1)} %get-tuple-element.28.slot_ref), custom_call_target="tpu_custom_call" | custom-call | tf_op jit(solution)/shard_map/finish/pallas_call | solution.py:366
Async XLA Ops:
  2.0 0.9 copy-start
  2.9 26.0 %copy-start.5 = (bf16[27,96,96]{2,1,0:T(8,128)(2,1)S(1)}, bf16[27,96,96]{2,1,0:T(8,128)(2,1)}, u32[]{:S(2)}) copy-start(bf16[27,96,96]{2,1,0:T(8,128)(2,1)} %param.10) | copy-start | bytes 1492996
  21.7 8.3 %collective-permute-start = (bf16[96,256]{1,0:T(8,128)(2,1)S(1)}, bf16[96,256]{1,0:T(8,128)(2,1)S(1)}, u32[]{:S(2)}, u32[]{:S(2)}) collective-permute-start(bf16[96,256]{1,0:T(8,128)(2,1)S(1)} %get-tuple-element.18), channel_id=1, source_target_pairs={{0,1},{1,2},{2,3},{3,4},{4,5},{5,6},{6,7},{7,8},{8,9},{9,10},{10,1... | collective-permute-start | bytes 147464 | tf_op jit(solution)/shard_map/ppermute | solution.py:385
  27.0 5.4 %collective-permute-start.1 = (bf16[96,256]{1,0:T(8,128)(2,1)S(1)}, bf16[96,256]{1,0:T(8,128)(2,1)S(1)}, u32[]{:S(2)}, u32[]{:S(2)}) collective-permute-start(bf16[96,256]{1,0:T(8,128)(2,1)S(1)} %get-tuple-element.19), channel_id=1, source_target_pairs={{1,0},{2,1},{3,2},{4,3},{5,4},{6,5},{7,6},{8,7},{9,8},{10,9},{11,1... | collective-permute-start | bytes 147464 | tf_op jit(solution)/shard_map/ppermute | solution.py:386
  29.3 3.1 %copy-start.1 = (bf16[1,1,96,2048]{3,2,1,0:T(8,128)(2,1)S(1)}, bf16[1,1,96,2048]{3,2,1,0:T(8,128)(2,1)}, u32[]{:S(2)}) copy-start(bf16[1,1,96,2048]{3,2,1,0:T(8,128)(2,1)} %param.11) | copy-start | bytes 1179652
  29.3 3.1 %copy-start.2 = (s32[1,1,27,2048]{3,1,2,0:T(1,128)S(1)}, s32[1,1,27,2048]{3,1,2,0:T(1,128)}, u32[]{:S(2)}) copy-start(s32[1,1,27,2048]{3,1,2,0:T(1,128)} %param.8) | copy-start | bytes 663556
  59.0 0.7 copy-start.3
  59.7 16.9 %all-to-all-start.1 = ((bf16[16,128,128]{2,1,0:T(8,128)(2,1)}), bf16[16,128,128]{2,1,0:T(8,128)(2,1)S(1)}, u32[]{:S(2)}, u32[]{:S(2)}) async-start(bf16[16,128,128]{2,1,0:T(8,128)(2,1)} %get-tuple-element.22), calls=%async_computation.1 | async-start | bytes 1048576 | tf_op jit(solution)/shard_map/all_to_all | solution.py:393
  77.5 25.8 %all-to-all-start.2 = ((bf16[16,128,128]{2,1,0:T(8,128)(2,1)}), bf16[16,128,128]{2,1,0:T(8,128)(2,1)S(1)}, u32[]{:S(2)}, u32[]{:S(2)}) async-start(bf16[16,128,128]{2,1,0:T(8,128)(2,1)} %sum_parts.1.after_ref), calls=%async_computation.2 | async-start | bytes 1048576 | tf_op jit(solution)/shard_map/all_to_all | solution.py:393
  85.9 0.9 copy-start.4
  112.1 4.3 %collective-permute-start.2 = (bf16[96,256]{1,0:T(8,128)(2,1)S(1)}, bf16[96,256]{1,0:T(8,128)(2,1)S(1)}, u32[]{:S(2)}, u32[]{:S(2)}) collective-permute-start(bf16[96,256]{1,0:T(8,128)(2,1)S(1)} %get-tuple-element.26), channel_id=1, source_target_pairs={{0,1},{1,2},{2,3},{3,4},{4,5},{5,6},{6,7},{7,8},{8,9},{9,10},{10,1... | collective-permute-start | bytes 147464 | tf_op jit(solution)/shard_map/ppermute | solution.py:400
  114.0 5.4 %collective-permute-start.3 = (bf16[96,256]{1,0:T(8,128)(2,1)S(1)}, bf16[96,256]{1,0:T(8,128)(2,1)S(1)}, u32[]{:S(2)}, u32[]{:S(2)}) collective-permute-start(bf16[96,256]{1,0:T(8,128)(2,1)S(1)} %get-tuple-element.27), channel_id=1, source_target_pairs={{1,0},{2,1},{3,2},{4,3},{5,4},{6,5},{7,6},{8,7},{9,8},{10,9},{11,1... | collective-permute-start | bytes 147464 | tf_op jit(solution)/shard_map/ppermute | solution.py:401
